TPU v7x, 128 devices: a whole 4x4x4 slice. The times are simulated.
128 devices in a mesh: row: 8 (over z, y_lo), col: 16 (over x, y_hi, core).
Axes of the slice: x: 4, y: 4 (y_hi: 2, y_lo: 2; y = y_hi * 2 + y_lo), z: 4, core: 2. Of those that a mesh axis runs over, the one named last changes fastest.
Arguments:
- tile_values: bfloat16 [8, 16, 128, 128, 128], P('row', 'col'), may hold values from -0.125 to 0.125
- tile_rows: int32 [8, 16, 128], P('row', 'col'), may hold values from 0 to 63
- tile_cols: int32 [8, 16, 128], P('row', 'col'), may hold values from 0 to 31
- tile_counts: int32 [8, 16], P('row', 'col'), may hold values from 16 to 128, as said below
- features: bfloat16 [65536, 256], P(('col', 'row')), may hold values from -6 to 6
- weight: bfloat16 [256, 256], replicated, may hold values from -0.375 to 0.375
- cotangent: bfloat16 [65536, 256], P(('row', 'col')), may hold values from -6 to 6
Outputs:
- output: bfloat16 [65536, 256], P(('row', 'col'))
- grad_features: bfloat16 [65536, 256], P(('col', 'row'))
- weight_grad: float32 [256, 256], replicated
Inputs may be any that keep to these rules, and one draw needn't show every extreme that they name: `tile_counts`: every grid cell lists at least 16 tiles, and at least one cell in every draw lists 128; slots past a cell's count hold entries that are no part of the adjacency.
All inputs are finite; a program needn't handle non-finite values.
Results may differ from a plain program's by a relative error of at most 0.024.
Values may be sent and summed in bfloat16 or wider, within the bound.
No kernel may reach another device: no remote copies, remote signals or barrier semaphores. Data moves between devices by JAX's collectives and lax.ppermute only.
A program may use at most 128 MiB of HBM per device.

v0:
```python
import math

import jax
import jax.numpy as jnp
from jax import lax
from jax.sharding import PartitionSpec as P

BLK = 128


def shards(tile_values, tile_rows, tile_cols, tile_counts, features, weight, cotangent):
    node_rows = features.shape[0]
    feat_width = features.shape[1]
    row_size = lax.axis_size("row")
    col_size = lax.axis_size("col")
    row_blocks = node_rows * col_size // BLK
    col_blocks = node_rows * row_size // BLK
    blocks = tile_values[0, 0]
    tile_row = tile_rows[0, 0]
    tile_col = tile_cols[0, 0]
    tile_total = tile_counts[0, 0]
    live_slots = (jnp.arange(blocks.shape[0]) < tile_total).astype(jnp.float32)[:, None, None]
    column_feats = lax.all_gather(features, "row", axis=0, tiled=True)
    feature_blocks = column_feats.reshape(col_blocks, BLK, feat_width)
    picked = feature_blocks[tile_col]
    products = (
        jnp.einsum("kab,kbw->kaw", blocks, picked, preferred_element_type=jnp.float32) * live_slots
    )
    partial_value = jax.ops.segment_sum(products, tile_row, num_segments=row_blocks)
    partial_value = partial_value.reshape(row_blocks * BLK, feat_width)
    agg_sum = lax.psum_scatter(
        partial_value.astype(jnp.bfloat16), "col", scatter_dimension=0, tiled=True
    )
    pre_act = jnp.dot(agg_sum, weight, preferred_element_type=jnp.float32)
    sigmoid_pre = jax.nn.sigmoid(pre_act)
    output = (pre_act * sigmoid_pre).astype(jnp.bfloat16)
    grad_pre = (
        cotangent.astype(jnp.float32) * sigmoid_pre * (1.0 + pre_act * (1.0 - sigmoid_pre))
    ).astype(jnp.bfloat16)
    local_grad = lax.dot_general(
        agg_sum, grad_pre, (((0,), (0,)), ((), ())), preferred_element_type=jnp.float32
    )
    scale = 1.0 / math.sqrt(node_rows * row_size * col_size)
    weight_grad = lax.psum(local_grad, ("row", "col")) * scale
    grad_agg = lax.dot_general(
        grad_pre, weight, (((1,), (1,)), ((), ())), preferred_element_type=jnp.float32
    ).astype(jnp.bfloat16)
    row_grads = lax.all_gather(grad_agg, "col", axis=0, tiled=True)
    grad_blocks = row_grads.reshape(row_blocks, BLK, feat_width)
    picked_grads = grad_blocks[tile_row]
    back_products = (
        jnp.einsum("kab,kaw->kbw", blocks, picked_grads, preferred_element_type=jnp.float32)
        * live_slots
    )
    back_partial = jax.ops.segment_sum(back_products, tile_col, num_segments=col_blocks)
    back_partial = back_partial.reshape(col_blocks * BLK, feat_width)
    grad_features = lax.psum_scatter(
        back_partial.astype(jnp.bfloat16), "row", scatter_dimension=0, tiled=True
    )
    return (output, grad_features, weight_grad)


def solution(mesh):
    in_specs = (
        P("row", "col", None, None, None),
        P("row", "col", None),
        P("row", "col", None),
        P("row", "col"),
        P(("col", "row"), None),
        P(),
        P(("row", "col"), None),
    )
    out_specs = (P(("row", "col"), None), P(("col", "row"), None), P())
    return jax.shard_map(shards, mesh=mesh, in_specs=in_specs, out_specs=out_specs, check_vma=False)
```

profile of v0, /device:TPU:0, one launch (start us, length us, event | category | flops | bytes accessed | tf_op | source)
XLA Modules:
  0.0 495.4 jit_solution(4808306989984746044)
XLA Ops:
  7.2 0.7 all-gather.3.cloned.1.call-update
  8.6 0.7 fusion.2
  9.3 55.2 %all-gather.3.cloned.1.call-done = bf16[4096,256]{1,0:T(8,128)(2,1)} async-done(((bf16[512,256]{1,0:T(8,128)(2,1)}), bf16[4096,256]{1,0:T(8,128)(2,1)}) %all-gather.3.cloned.1.call-update) | async-done | bytes 2097168 | tf_op jit(solution)/shard_map/all_gather | solution.py:23
  64.5 8.2 %gather_fusion = bf16[128,128,256]{2,1,0:T(8,128)(2,1)} fusion(bf16[32,128,256]{2,1,0:T(8,128)(2,1)} %bitcast.33, s32[1024]{0:T(1024)S(1)} %pad_clamp_fusion.1), kind=kCustom, calls=%fused_computation | custom fusion | bytes 16777728 | tf_op jit(solution)/shard_map/gather | solution.py:25
  72.6 13.0 %multiply_bitcast_fusion.1 = f32[128,128,256]{1,2,0:T(8,128)} fusion(bf16[128,128,256]{2,1,0:T(8,128)(2,1)} %gather_fusion, f32[128]{0:T(128)S(1)} %compare_convert_fusion, bf16[1,1,128,128,128]{4,3,2,1,0:T(8,128)(2,1)} %param.7), kind=kOutput, calls=%fused_computation.5 | convolution fusion | flops 1077936128 | bytes 29360640 | tf_op jit(solution)/shard_map/kab,kbw->kaw/dot_general | solution.py:27
  85.6 17.4 %copy.13 = f32[128,128,256]{2,1,0:T(8,128)} copy(f32[128,128,256]{1,2,0:T(8,128)} %multiply_bitcast_fusion.1) | data formatting | bytes 33554432 | tf_op jit(solution)/shard_map/mul | solution.py:27
  103.1 4.3 broadcast_in_dim.4
  107.3 38.5 %scatter_fusion = f32[64,128,256]{2,1,0:T(8,128)} fusion(f32[64,128,256]{2,1,0:T(8,128)} %broadcast_in_dim.4, s32[128]{0:T(128)S(1)} %bitcast.37, f32[128,128,256]{2,1,0:T(8,128)} %copy.13), kind=kCustom, calls=%fused_computation.2 | custom fusion | flops 4194304 | bytes 50332160 | tf_op jit(solution)/shard_map/scatter-add | solution.py:29
  145.8 6.0 %convert_element_type.32 = bf16[64,128,256]{2,1,0:T(8,128)(2,1)} convert(f32[64,128,256]{2,1,0:T(8,128)} %scatter_fusion) | non-fusion elementwise | flops 2097152 | bytes 12582912 | tf_op jit(solution)/shard_map/convert_element_type | solution.py:32
  151.8 79.6 %reduce-scatter.3.cloned.1.call-done = bf16[512,256]{1,0:T(8,128)(2,1)} async-done(((bf16[8192,256]{1,0:T(8,128)(2,1)}), bf16[512,256]{1,0:T(8,128)(2,1)}) %reduce-scatter.3.cloned.1.call-update) | async-done | bytes 262160 | tf_op jit(solution)/shard_map/reduce_scatter | solution.py:31
  231.4 2.1 multiply_convert_fusion
  233.5 1.0 convolution_convert_fusion
  234.5 1.9 fusion.4
  236.5 0.2 reduce-scatter.5.cloned.1.call-start
  236.7 52.8 %all-gather.5.cloned.1.call-done = bf16[8192,256]{1,0:T(8,128)(2,1)} async-done(((bf16[512,256]{1,0:T(8,128)(2,1)}), bf16[8192,256]{1,0:T(8,128)(2,1)}) %all-gather.5.cloned.1.call-update) | async-done | bytes 4194320 | tf_op jit(solution)/shard_map/all_gather | solution.py:48
  289.5 8.8 %gather_fusion.1 = bf16[128,128,256]{2,1,0:T(8,128)(2,1)} fusion(bf16[64,128,256]{2,1,0:T(8,128)(2,1)} %bitcast.34, s32[1024]{0:T(1024)S(1)} %pad_clamp_fusion), kind=kCustom, calls=%fused_computation.1 | custom fusion | bytes 16777728 | tf_op jit(solution)/shard_map/gather | solution.py:50
  298.2 13.7 %multiply_bitcast_fusion = f32[128,128,256]{1,2,0:T(8,128)} fusion(bf16[128,128,256]{2,1,0:T(8,128)(2,1)} %gather_fusion.1, f32[128]{0:T(128)S(1)} %compare_convert_fusion, bf16[1,1,128,128,128]{4,3,2,1,0:T(8,128)(2,1)} %param.7), kind=kOutput, calls=%fused_computation.4 | convolution fusion | flops 1077936128 | bytes 29360640 | tf_op jit(solution)/shard_map/kab,kaw->kbw/dot_general | solution.py:52
  312.0 17.5 %copy.15 = f32[128,128,256]{2,1,0:T(8,128)} copy(f32[128,128,256]{1,2,0:T(8,128)} %multiply_bitcast_fusion) | data formatting | bytes 33554432 | tf_op jit(solution)/shard_map/mul | solution.py:52
  329.4 2.4 broadcast_in_dim.10
  331.9 37.8 %scatter_fusion.1 = f32[32,128,256]{2,1,0:T(8,128)} fusion(f32[32,128,256]{2,1,0:T(8,128)} %broadcast_in_dim.10, s32[128]{0:T(128)S(1)} %bitcast.38, f32[128,128,256]{2,1,0:T(8,128)} %copy.15), kind=kCustom, calls=%fused_computation.3 | custom fusion | flops 4194304 | bytes 50332160 | tf_op jit(solution)/shard_map/scatter-add | solution.py:55
  369.7 3.9 convert_element_type.38
  373.5 62.6 %all-reduce.2.cloned.1.call-done = f32[256,256]{1,0:T(8,128)} async-done(((f32[256,256]{1,0:T(8,128)}), f32[256,256]{1,0:T(8,128)}) %all-reduce.2.cloned.1.call-update) | async-done | bytes 262160 | tf_op jit(solution)/shard_map/psum | solution.py:44
  436.2 1.7 broadcast_multiply_fusion
  437.9 51.0 %reduce-scatter.5.cloned.1.call-done = bf16[512,256]{1,0:T(8,128)(2,1)} async-done(((bf16[4096,256]{1,0:T(8,128)(2,1)}), bf16[512,256]{1,0:T(8,128)(2,1)}) %reduce-scatter.5.cloned.1.call-update) | async-done | bytes 262160 | tf_op jit(solution)/shard_map/reduce_scatter | solution.py:57
  (22 shorter events, 0.3 us)
Async XLA Ops:
  7.2 224.3 %copy-start = (bf16[256,256]{1,0:T(8,128)(2,1)S(1)}, bf16[256,256]{1,0:T(8,128)(2,1)}, u32[]{:S(2)}) copy-start(bf16[256,256]{1,0:T(8,128)(2,1)} %param.12) | copy-start | bytes 393220
  7.2 57.3 %all-gather.3.cloned.1.call-start = ((), (), s32[]{:S(2)}) async-start(), calls=%async_computation.2 | async-start | bytes 2359296 | tf_op jit(solution)/shard_map/all_gather | solution.py:23
  7.9 223.5 %reduce-scatter.3.cloned.1.call-start = ((), (), s32[]{:S(2)}) async-start(), calls=%async_computation.3 | async-start | bytes 4456448 | tf_op jit(solution)/shard_map/reduce_scatter | solution.py:31
  103.1 4.3 copy-start.2
  145.8 85.6 %copy-start.4 = (bf16[512,256]{1,0:T(8,128)(2,1)S(1)}, bf16[512,256]{1,0:T(8,128)(2,1)}, u32[]{:S(2)}) copy-start(bf16[512,256]{1,0:T(8,128)(2,1)} %param.13) | copy-start | bytes 786436
  151.8 137.7 %all-gather.5.cloned.1.call-start = ((), (), s32[]{:S(2)}) async-start(), calls=%async_computation.4 | async-start | bytes 4456448 | tf_op jit(solution)/shard_map/all_gather | solution.py:48
  234.5 201.7 %all-reduce.2.cloned.1.call-start = ((), (), s32[]{:S(2)}) async-start(), calls=%async_computation.6 | async-start | bytes 524288 | tf_op jit(solution)/shard_map/psum | solution.py:44
  236.5 252.4 %reduce-scatter.5.cloned.1.call-start = ((), (), s32[]{:S(2)}) async-start(), calls=%async_computation.5 | async-start | bytes 2359296 | tf_op jit(solution)/shard_map/reduce_scatter | solution.py:57
  312.0 19.9 %copy-start.3 = (s32[1,1,128]{2,1,0:T(1,128)S(1)}, s32[1,1,128]{2,1,0:T(1,128)}, u32[]{:S(2)}) copy-start(s32[1,1,128]{2,1,0:T(1,128)} %param.9) | copy-start | bytes 1540
  331.9 157.0 %copy-start.1 = (bf16[256,256]{1,0:T(8,128)(2,1)S(1)}, bf16[256,256]{1,0:T(8,128)(2,1)}, u32[]{:S(2)}) copy-start(bf16[256,256]{1,0:T(8,128)(2,1)} %param.12) | copy-start | bytes 393220
Sparse Core Ops, SparseCore 0:
  9.7 54.7 all-gather.2
  151.9 79.4 reduce-scatter.2
  234.7 54.7 all-gather.4
  295.4 140.7 all-reduce.1
  439.1 49.6 reduce-scatter.4
where the time goes:
time: 497 us; the launch traced here: 495 us
  waiting for transfers between devices  302 us (61%)
  other arithmetic  88.5 us (18%)
  local copies, waits for them, and re-layouts  58.5 us (12%)
  matrix products  31.6 us (6%)
  between operations  14.5 us (3%)
    reduce_scatter x1, waiting for transfers between devices, shards(): lax.psum_scatter(partial_value.astype(jnp.bfloat16), 'col', scatter_dimen...  79.6 us
    psum x1, waiting for transfers between devices, shards(): weight_grad = lax.psum(local_grad, ('row', 'col')) * scale  62.6 us
    all_gather x1, waiting for transfers between devices, shards(): column_feats = lax.all_gather(features, 'row', axis=0, tiled=True)  55.2 us
    all_gather x1, waiting for transfers between devices, shards(): row_grads = lax.all_gather(grad_agg, 'col', axis=0, tiled=True)  52.8 us
    reduce_scatter x1, waiting for transfers between devices, shards(): lax.psum_scatter(back_partial.astype(jnp.bfloat16), 'row', scatter_dimens...  51 us
    scatter-add x1, other arithmetic, shards(): jax.ops.segment_sum(products, tile_row, num_segments=row_blocks)  38.5 us
    scatter-add x1, other arithmetic, shards(): jax.ops.segment_sum(back_products, tile_col, num_segments=col_blocks)  37.8 us
    mul x1, local copies, waits for them, and re-layouts, shards(): jnp.einsum('kab,kaw->kbw', blocks, picked_grads, preferred_element_type=j...  17.5 us
  transfers between devices with their start and end apart: 5, of which 5 were waited for; matrix products, arithmetic and copies ran while one was open for 18% of the time, Pallas kernels for 0%

commit v1 on v0

v1 whole, which is shorter than its diff:
```python
import functools
import math

import jax
import jax.numpy as jnp
from jax import lax
from jax.experimental import pallas as pl
from jax.experimental.pallas import tpu as pltpu
from jax.sharding import PartitionSpec as P

BLK = 128
WIDTH = 256
CAP = 128
UNROLL = 4
CHUNKS = 4
BF16 = jnp.bfloat16
F32 = jnp.float32

NZ, NX = 4, 4


def z_perm(step):
    return [(z * 2 + yl, (z + step) % NZ * 2 + yl) for z in range(NZ) for yl in range(2)]


def yl_perm():
    return [(r, r ^ 1) for r in range(2 * NZ)]


def x_perm(step):
    return [(x * 4 + q, (x + step) % NX * 4 + q) for x in range(NX) for q in range(4)]


def yh_perm():
    return [(c, c ^ 2) for c in range(4 * NX)]


def core_perm():
    return [(c, c ^ 1) for c in range(4 * NX)]


def z_send(v, step):
    return lax.ppermute(v, "row", z_perm(step))


def yl_swap(v):
    return lax.ppermute(v, "row", yl_perm())


def x_send(v, step):
    return lax.ppermute(v, "col", x_perm(step))


def yh_swap(v):
    return lax.ppermute(v, "col", yh_perm())


def core_swap(v):
    return lax.ppermute(v, "col", core_perm())


def add(*terms):
    total = terms[0].astype(F32)
    for term in terms[1:]:
        total = total + term.astype(F32)
    return total.astype(BF16)


def tile_loop(count, tiles_hbm, tiles, tile_sems, step, acc, product):
    size = CAP // CHUNKS
    for chunk in range(CHUNKS):
        pltpu.make_async_copy(
            tiles_hbm.at[pl.ds(chunk * size, size)],
            tiles.at[pl.ds(chunk * size, size)],
            tile_sems.at[chunk],
        ).wait()
        live = jnp.clip(count - chunk * size, 0, size)
        groups = live // UNROLL

        def group(i, carry):
            first = chunk * size + i * UNROLL
            parts = [product(first + u) for u in range(UNROLL)]
            for u in range(UNROLL):
                slot = step[first + u]
                acc[slot] += parts[u]
            return carry

        lax.fori_loop(0, groups, group, 0)

        def single(i, carry):
            k = chunk * size + i
            acc[step[k]] += product(k)
            return carry

        lax.fori_loop(groups * UNROLL, live, single, 0)


def start_tiles(tiles_hbm, tiles, tile_sems):
    size = CAP // CHUNKS
    for chunk in range(CHUNKS):
        pltpu.make_async_copy(
            tiles_hbm.at[pl.ds(chunk * size, size)],
            tiles.at[pl.ds(chunk * size, size)],
            tile_sems.at[chunk],
        ).start()


def clear(acc):
    def body(i, carry):
        acc[i] = jnp.zeros(acc.shape[1:], acc.dtype)
        return carry

    lax.fori_loop(0, acc.shape[0], body, 0)


def cell_kernel(transposed, places, n_out, out_ref, in_ref, cnt_ref, tiles_hbm, *rest):
    n_in = len(places)
    pieces = rest[:n_in]
    outs = rest[n_in : n_in + n_out]
    tiles, blocks, acc, tile_sems, piece_sems = rest[n_in + n_out :]
    copies = []
    for i, (piece, (first, size)) in enumerate(zip(pieces, places)):
        copy = pltpu.make_async_copy(piece, blocks.at[pl.ds(first, size)], piece_sems.at[i])
        copy.start()
        copies.append(copy)
    start_tiles(tiles_hbm, tiles, tile_sems)
    clear(acc)
    for copy in copies:
        copy.wait()
    count = cnt_ref[0]
    dims = (((0,), (0,)), ((), ())) if transposed else (((1,), (0,)), ((), ()))

    def product(k):
        return lax.dot_general(
            tiles[k], blocks[in_ref[k]], dims, preferred_element_type=F32
        )

    tile_loop(count, tiles_hbm, tiles, tile_sems, out_ref, acc, product)
    first = 0
    for out in outs:
        def store(i, carry, out=out, first=first):
            out[i] = acc[first + i].astype(BF16)
            return carry

        lax.fori_loop(0, out.shape[0], store, 0)
        first += out.shape[0]


def cell_product(name, transposed, out_slot, in_slot, count, tiles, pieces, places, out_sizes, in_blocks):
    out_blocks = sum(out_sizes)
    kernel = functools.partial(cell_kernel, transposed, places, len(out_sizes))
    any_spec = pl.BlockSpec(memory_space=pl.ANY)
    vmem_spec = pl.BlockSpec(memory_space=pltpu.VMEM)
    return pl.pallas_call(
        kernel,
        grid_spec=pltpu.PrefetchScalarGridSpec(
            num_scalar_prefetch=3,
            grid=(),
            in_specs=[any_spec] * (1 + len(pieces)),
            out_specs=[vmem_spec] * len(out_sizes),
            scratch_shapes=[
                pltpu.VMEM((CAP, BLK, BLK), BF16),
                pltpu.VMEM((in_blocks, BLK, WIDTH), BF16),
                pltpu.VMEM((out_blocks, BLK, WIDTH), F32),
                pltpu.SemaphoreType.DMA((CHUNKS,)),
                pltpu.SemaphoreType.DMA((len(pieces),)),
            ],
        ),
        out_shape=[jax.ShapeDtypeStruct((n, BLK, WIDTH), BF16) for n in out_sizes],
        compiler_params=pltpu.CompilerParams(vmem_limit_bytes=48 * 1024 * 1024),
        cost_estimate=pl.CostEstimate(
            flops=2 * CAP * BLK * BLK * WIDTH,
            bytes_accessed=2 * CAP * BLK * BLK + 2 * (in_blocks + out_blocks) * BLK * WIDTH,
            transcendentals=0,
        ),
        name=name,
    )(out_slot, in_slot, count, tiles, *pieces)


def dense_kernel(scale, a0, a1, b0, b1, b2, b3, w_ref, cot_ref, out_ref, ga_ref, gb_ref, wg_ref):
    rows = 2 * BLK
    w = w_ref[...]
    terms = ((a0, a1), (b0, b1, b2, b3))
    weight_grad = None
    for half in range(2):
        total = terms[half][0][...].astype(F32)
        for term in terms[half][1:]:
            total = total + term[...].astype(F32)
        agg = total.astype(BF16).reshape(rows, WIDTH)
        pre = jnp.dot(agg, w, preferred_element_type=F32)
        sig = jax.nn.sigmoid(pre)
        span = pl.ds(half * rows, rows)
        out_ref[span, :] = (pre * sig).astype(BF16)
        grad_pre = (cot_ref[span, :].astype(F32) * sig * (1.0 + pre * (1.0 - sig))).astype(BF16)
        grad_agg = lax.dot_general(
            grad_pre, w, (((1,), (1,)), ((), ())), preferred_element_type=F32
        ).astype(BF16)
        (ga_ref, gb_ref)[half][...] = grad_agg.reshape(2, BLK, WIDTH)
        term = lax.dot_general(
            agg, grad_pre, (((0,), (0,)), ((), ())), preferred_element_type=F32
        )
        weight_grad = term if weight_grad is None else weight_grad + term
    wg_ref[...] = weight_grad * scale


def dense(scale, parts, weight, cotangent):
    vmem_spec = pl.BlockSpec(memory_space=pltpu.VMEM)
    nodes = cotangent.shape[0]
    return pl.pallas_call(
        functools.partial(dense_kernel, scale),
        in_specs=[vmem_spec] * 8,
        out_specs=[vmem_spec] * 4,
        out_shape=[
            jax.ShapeDtypeStruct((nodes, WIDTH), BF16),
            jax.ShapeDtypeStruct((2, BLK, WIDTH), BF16),
            jax.ShapeDtypeStruct((2, BLK, WIDTH), BF16),
            jax.ShapeDtypeStruct((WIDTH, WIDTH), F32),
        ],
        compiler_params=pltpu.CompilerParams(vmem_limit_bytes=32 * 1024 * 1024),
        cost_estimate=pl.CostEstimate(
            flops=6 * nodes * WIDTH * WIDTH,
            bytes_accessed=8 * nodes * WIDTH,
            transcendentals=nodes * WIDTH,
        ),
        name="dense",
    )(*parts, weight, cotangent)


def gather_row(features):
    own = features.reshape(4, BLK, WIDTH)
    a, b = own[:2], own[2:]
    a_y = yl_swap(a)
    b_z = [z_send(b, -d) for d in (1, 3, 2)]
    a_z = [z_send(a, -d) for d in (1, 3, 2)]
    a_yz = [z_send(a_y, -d) for d in (1, 3, 2)]
    b_y = [yl_swap(v) for v in [b] + b_z]
    pieces, places = [a, a_y, b, b_y[0]], [(0, 2), (2, 2), (16, 2), (18, 2)]
    for i, d in enumerate((1, 3, 2)):
        pieces += [a_z[i], a_yz[i], b_z[i], b_y[i + 1]]
        places += [(d * 4, 2), (d * 4 + 2, 2), (16 + d * 4, 2), (16 + d * 4 + 2, 2)]
    return pieces, places


def gather_col(ga, gb):
    b_y = yh_swap(gb)
    a_x = [x_send(ga, -d) for d in (1, 3, 2)]
    b_x = [x_send(gb, -d) for d in (1, 3, 2)]
    b_yx = [x_send(b_y, -d) for d in (1, 3, 2)]
    a_y = [yh_swap(v) for v in [ga] + a_x]
    a_all = jnp.concatenate(
        [ga, a_y[0], a_x[0], a_y[1], a_x[2], a_y[3], a_x[1], a_y[2]], axis=0
    )
    b_all = jnp.concatenate(
        [gb, b_y, b_x[0], b_yx[0], b_x[2], b_yx[2], b_x[1], b_yx[1]], axis=0
    )
    pieces = [a_all, b_all, core_swap(a_all), core_swap(b_all)]
    return pieces, [(0, 16), (16, 16), (32, 16), (48, 16)]


def scatter_col(mine, other):
    recv = core_swap(other)
    total = add(mine, recv)
    a = [total[4 * d : 4 * d + 4] for d in range(4)]
    b0, b1 = total[16:24], total[24:32]
    r = [x_send(a[d], d) for d in (1, 3, 2)]
    q = yh_swap(b1)
    s = add(a[0], *r)
    u = add(b0, q)
    c = yh_swap(s[2:4])
    e = [x_send(u[2 * d : 2 * d + 2], d) for d in (1, 3, 2)]
    return s[:2], c, u[:2], *e


def scatter_row(a0, a1, a2, a3, b0, b1):
    r = [z_send(v, d) for v, d in ((a1, 1), (a3, 3), (a2, 2))]
    q = yl_swap(b1)
    s = add(a0, *r)
    u = add(b0, q)
    c = yl_swap(s[2:4])
    e = [z_send(u[2 * d : 2 * d + 2], d) for d in (1, 3, 2)]
    first = add(s[:2], c)
    second = add(u[:2], *e)
    return jnp.concatenate([first, second], axis=0).reshape(4 * BLK, WIDTH)


def ring_sum(own, send):
    opposite, left, right = send(own, 2), send(own, 1), send(own, -1)
    return (own + opposite) + (left + right)


def y_send(v, step):
    pairs = []
    for r in range(2 * NZ):
        for c in range(4 * NX):
            y = ((c // 2 % 2) * 2 + r % 2 + step) % 4
            to = (r - r % 2 + y % 2) * (4 * NX) + c - (c & 2) + (y // 2) * 2
            pairs.append((r * 4 * NX + c, to))
    return lax.ppermute(v, ("row", "col"), pairs)


def sum_everywhere(term, core):
    half = WIDTH // 2
    mine = lax.dynamic_slice_in_dim(term, core * half, half, 0)
    other = lax.dynamic_slice_in_dim(term, (1 - core) * half, half, 0)
    total = mine + core_swap(other)
    total = ring_sum(total, x_send)
    total = ring_sum(total, z_send)
    total = ring_sum(total, y_send)
    far = core_swap(total)
    first = jnp.where(core == 0, total, far)
    second = jnp.where(core == 0, far, total)
    return jnp.concatenate([first, second], axis=0)


def shards(tile_values, tile_rows, tile_cols, tile_counts, features, weight, cotangent):
    row, col = lax.axis_index("row"), lax.axis_index("col")
    z, yl = row // 2, row % 2
    x, yh, core = col // 4, col // 2 % 2, col % 2
    tiles = tile_values[0, 0]
    t_row, t_col = tile_rows[0, 0], tile_cols[0, 0]
    count = tile_counts[0]

    own, j = t_row // 4, t_row % 4
    dx, dyh, dk = (own // 4 - x) % 4, (own // 2 % 2) ^ yh, (own % 2) ^ core
    h, jj = j // 2, j % 2
    row_out = dk * 32 + h * 16 + jj + jnp.where(h == 0, dx * 4 + dyh * 2, dyh * 8 + dx * 2)
    row_in = dk * 32 + h * 16 + dx * 4 + dyh * 2 + jj

    own, j = t_col // 4, t_col % 4
    dz, dyl = (own // 2 - z) % 4, (own % 2) ^ yl
    h, jj = j // 2, j % 2
    col_out = h * 16 + jj + jnp.where(h == 0, dz * 4 + dyl * 2, dyl * 8 + dz * 2)
    col_in = h * 16 + dz * 4 + dyl * 2 + jj

    pieces, places = gather_row(features)
    mine, other = cell_product(
        "forward_cell", False, row_out, col_in, count, tiles, pieces, places, [32, 32], 32
    )
    parts = scatter_col(mine, other)
    scale = 1.0 / math.sqrt(features.shape[0] * lax.axis_size("row") * lax.axis_size("col"))
    output, ga, gb, local_grad = dense(scale, parts, weight, cotangent)
    weight_grad = sum_everywhere(local_grad, core)
    pieces, places = gather_col(ga, gb)
    back = cell_product(
        "backward_cell", True, col_out, row_in, count, tiles, pieces, places, [4, 4, 4, 4, 8, 8], 64
    )
    grad_features = scatter_row(*back)
    return (output, grad_features, weight_grad)


def solution(mesh):
    in_specs = (
        P("row", "col", None, None, None),
        P("row", "col", None),
        P("row", "col", None),
        P("row", "col"),
        P(("col", "row"), None),
        P(),
        P(("row", "col"), None),
    )
    out_specs = (P(("row", "col"), None), P(("col", "row"), None), P())
    return jax.shard_map(shards, mesh=mesh, in_specs=in_specs, out_specs=out_specs, check_vma=False)
```

time: 497 us -> 189 us (0.38)
  waiting for transfers between devices: 302 us -> 68.4 us
  starting transfers between devices: 0.38 us -> 94.2 us
  other arithmetic: 88.5 us -> 3.82 us
  local copies, waits for them, and re-layouts: 58.5 us -> 1.35 us
  matrix products: 31.6 us -> 0 us
  Pallas kernels: 0 us -> 19.7 us
  between operations: 14.5 us -> 1.74 us
    reduce_scatter x2 -> x0, waiting for transfers between devices: 131 us -> none  [the longest x1 79.6 us: shards(): lax.psum_scatter(partial_value.astype(jnp.bfloat16), 'col', scatter_dimen...]
    all_gather x2 -> x0, waiting for transfers between devices: 108 us -> none  [the longest x1 55.2 us: shards(): column_feats = lax.all_gather(features, 'row', axis=0, tiled=True)]
    ppermute x0 -> x58, starting transfers between devices: none -> 94.2 us  [the longest x18 37 us: z_send(): return lax.ppermute(v, 'row', z_perm(step))]
    scatter-add x2 -> x0, other arithmetic: 76.3 us -> none  [the longest x1 38.5 us: shards(): jax.ops.segment_sum(products, tile_row, num_segments=row_blocks)]
    ppermute x0 -> x58, waiting for transfers between devices: none -> 68.4 us  [the longest x18 22 us: z_send(): return lax.ppermute(v, 'row', z_perm(step))]
    psum x1 -> x0, waiting for transfers between devices: 62.6 us -> none  [shards(): weight_grad = lax.psum(local_grad, ('row', 'col')) * scale]
    mul x2 -> x0, local copies, waits for them, and re-layouts: 34.9 us -> none  [the longest x1 17.5 us: shards(): jnp.einsum('kab,kaw->kbw', blocks, picked_grads, preferred_element_type=j...]
    dot_general x5 -> x0, matrix products: 31.6 us -> none  [the longest x1 13.7 us: shards(): jnp.einsum('kab,kaw->kbw', blocks, picked_grads, preferred_element_type=j...]
  transfers between devices with their start and end apart: 5 -> 58, of which waited for: 5 -> 28; matrix products, arithmetic and copies ran while one was open for 18% -> 1% of each run, Pallas kernels for 0% -> 4%
where the time goes in v1:
time: 189 us
  starting transfers between devices  94.2 us (50%)
  waiting for transfers between devices  68.4 us (36%)
  Pallas kernels  19.7 us (10%)
  other arithmetic  3.82 us (2%)
    ppermute x18, starting transfers between devices, z_send(): return lax.ppermute(v, 'row', z_perm(step))  37 us
    ppermute x18, starting transfers between devices, x_send(): return lax.ppermute(v, 'col', x_perm(step))  25.3 us
    ppermute x7, starting transfers between devices, yh_swap(): return lax.ppermute(v, 'col', yh_perm())  22.8 us
    ppermute x18, waiting for transfers between devices, z_send(): return lax.ppermute(v, 'row', z_perm(step))  22 us
    pallas_call x2, Pallas kernels, cell_product(): pl.pallas_call(kernel, grid_spec=pltpu.PrefetchScalarGridSpec(num_scalar_...  18.7 us
    ppermute x18, waiting for transfers between devices, x_send(): return lax.ppermute(v, 'col', x_perm(step))  18 us
    ppermute x7, waiting for transfers between devices, yh_swap(): return lax.ppermute(v, 'col', yh_perm())  9.09 us
    ppermute x7, waiting for transfers between devices, yl_swap(): return lax.ppermute(v, 'row', yl_perm())  7.24 us
  transfers between devices with their start and end apart: 58, of which 28 were waited for; matrix products, arithmetic and copies ran while one was open for 1% of the time, Pallas kernels for 4%

profile of v1, /device:TPU:0, one launch (start us, length us, event | category | flops | bytes accessed | tf_op | source)
XLA Modules:
  0.0 189.2 jit_solution(5732561205736032805)
XLA Ops:
  1.6 4.0 %collective-permute-start.10 = (bf16[2,128,256]{2,1,0:T(8,128)(2,1)S(1)}, bf16[2,128,256]{2,1,0:T(8,128)(2,1)S(1)}, u32[]{:S(2)}, u32[]{:S(2)}) collective-permute-start(bf16[2,128,256]{2,1,0:T(8,128)(2,1)S(1)} %bitcast.36), channel_id=1, source_target_pairs={{0,64},{16,80},{32,96},{48,112},{64,0},{80,16},{96,32},{112,48},{1... | collective-permute-start | bytes 393224 | tf_op jit(solution)/shard_map/ppermute | solution.py:43
  15.7 2.8 %collective-permute-start.11 = (bf16[2,128,256]{2,1,0:T(8,128)(2,1)S(1)}, bf16[2,128,256]{2,1,0:T(8,128)(2,1)S(1)}, u32[]{:S(2)}, u32[]{:S(2)}) collective-permute-start(bf16[2,128,256]{2,1,0:T(8,128)(2,1)S(1)} %collective-permute-done.rest_1_), channel_id=1, source_target_pairs={{0,64},{16,80},{32,96},{48,112},{64,0},{80,16},{96,32},{112,48},{1... | collective-permute-start | bytes 393224 | tf_op jit(solution)/shard_map/ppermute | solution.py:43
  29.6 10.7 %forward_cell.1 = (bf16[32,128,256]{2,1,0:T(8,128)(2,1)S(1)}, bf16[32,128,256]{2,1,0:T(8,128)(2,1)}) custom-call(s32[128]{0:T(128)S(1)} %fusion.3.out_ref, s32[128]{0:T(128)S(1)} %add_add_fusion.4.in_ref, s32[1]{0:T(128)} %bitcast.29.cnt_ref, bf16[128,128,128]{2,1,0:T(8,128)(2,1)} %bitcast.41, bf16[2,128,256]{2,1,0:T(8,128)(2,1)S(1)} %bitcast.40, ...), custom_call_target="tpu_custom_call" | custom-call | flops 1073741824 | bytes 10485760 | tf_op jit(solution)/shard_map/forward_cell/pallas_call | solution.py:154
  40.5 4.4 %collective-permute-done.14 = bf16[32,128,256]{2,1,0:T(8,128)(2,1)S(1)} collective-permute-done((bf16[32,128,256]{2,1,0:T(8,128)(2,1)}, bf16[32,128,256]{2,1,0:T(8,128)(2,1)S(1)}, u32[]{:S(2)}, u32[]{:S(2)}) %collective-permute-start.14) | collective-permute-done | bytes 2097184 | tf_op jit(solution)/shard_map/ppermute | solution.py:59
  49.1 5.0 %collective-permute-start.19 = (bf16[8,128,256]{2,1,0:T(8,128)(2,1)S(1)}, bf16[8,128,256]{2,1,0:T(8,128)(2,1)S(1)}, u32[]{:S(2)}, u32[]{:S(2)}) collective-permute-start(bf16[8,128,256]{2,1,0:T(8,128)(2,1)S(1)} %slice.95), channel_id=1, source_target_pairs={{0,2},{1,3},{2,0},{3,1},{4,6},{5,7},{6,4},{7,5},{8,10},{9,11},{10,... | collective-permute-start | bytes 1572872 | tf_op jit(solution)/shard_map/ppermute | solution.py:55
  54.1 6.9 %collective-permute-done.15 = bf16[4,128,256]{2,1,0:T(8,128)(2,1)S(1)} collective-permute-done((bf16[4,128,256]{2,1,0:T(8,128)(2,1)S(1)}, bf16[4,128,256]{2,1,0:T(8,128)(2,1)S(1)}, u32[]{:S(2)}, u32[]{:S(2)}) %collective-permute-start.15) | collective-permute-done | bytes 262176 | tf_op jit(solution)/shard_map/ppermute | solution.py:51
  61.7 3.0 %collective-permute-start.18 = (bf16[2,128,256]{2,1,0:T(8,128)(2,1)S(1)}, bf16[2,128,256]{2,1,0:T(8,128)(2,1)S(1)}, u32[]{:S(2)}, u32[]{:S(2)}) collective-permute-start(bf16[2,128,256]{2,1,0:T(8,128)(2,1)S(1)} %get-tuple-element.54), channel_id=1, source_target_pairs={{0,2},{1,3},{2,0},{3,1},{4,6},{5,7},{6,4},{7,5},{8,10},{9,11},{10,... | collective-permute-start | bytes 393224 | tf_op jit(solution)/shard_map/ppermute | solution.py:55
  69.7 3.6 %collective-permute-done.22.b3 = bf16[2,128,256]{2,1,0:T(8,128)(2,1)S(1)} collective-permute-done((bf16[2,128,256]{2,1,0:T(8,128)(2,1)S(1)}, bf16[2,128,256]{2,1,0:T(8,128)(2,1)S(1)}, u32[]{:S(2)}, u32[]{:S(2)}) %collective-permute-start.22) | collective-permute-done | bytes 131104 | tf_op jit(solution)/shard_map/ppermute | solution.py:51
  90.2 2.8 %collective-permute-done.30 = bf16[2,128,256]{2,1,0:T(8,128)(2,1)S(1)} collective-permute-done((bf16[2,128,256]{2,1,0:T(8,128)(2,1)S(1)}, bf16[2,128,256]{2,1,0:T(8,128)(2,1)S(1)}, u32[]{:S(2)}, u32[]{:S(2)}) %collective-permute-start.30) | collective-permute-done | bytes 131104 | tf_op jit(solution)/shard_map/ppermute | solution.py:55
  95.7 4.0 %collective-permute-start.33 = (bf16[2,128,256]{2,1,0:T(8,128)(2,1)S(1)}, bf16[2,128,256]{2,1,0:T(8,128)(2,1)S(1)}, u32[]{:S(2)}, u32[]{:S(2)}) collective-permute-start(bf16[2,128,256]{2,1,0:T(8,128)(2,1)S(1)} %get-tuple-element.19), channel_id=1, source_target_pairs={{0,8},{1,9},{2,10},{3,11},{4,12},{5,13},{6,14},{7,15},{8,0},{9,1},... | collective-permute-start | bytes 393224 | tf_op jit(solution)/shard_map/ppermute | solution.py:51
  104.8 3.2 %collective-permute-start.34 = (bf16[2,128,256]{2,1,0:T(8,128)(2,1)S(1)}, bf16[2,128,256]{2,1,0:T(8,128)(2,1)S(1)}, u32[]{:S(2)}, u32[]{:S(2)}) collective-permute-start(bf16[2,128,256]{2,1,0:T(8,128)(2,1)S(1)} %collective-permute-done.30), channel_id=1, source_target_pairs={{0,8},{1,9},{2,10},{3,11},{4,12},{5,13},{6,14},{7,15},{8,0},{9,1},... | collective-permute-start | bytes 393224 | tf_op jit(solution)/shard_map/ppermute | solution.py:51
  108.8 2.9 %collective-permute-done.34 = bf16[2,128,256]{2,1,0:T(8,128)(2,1)S(1)} collective-permute-done((bf16[2,128,256]{2,1,0:T(8,128)(2,1)S(1)}, bf16[2,128,256]{2,1,0:T(8,128)(2,1)S(1)}, u32[]{:S(2)}, u32[]{:S(2)}) %collective-permute-start.34) | collective-permute-done | bytes 131104 | tf_op jit(solution)/shard_map/ppermute | solution.py:51
  112.6 4.1 %collective-permute-start.27 = (bf16[2,128,256]{2,1,0:T(8,128)(2,1)S(1)}, bf16[2,128,256]{2,1,0:T(8,128)(2,1)S(1)}, u32[]{:S(2)}, u32[]{:S(2)}) collective-permute-start(bf16[2,128,256]{2,1,0:T(8,128)(2,1)S(1)} %collective-permute-done.26), channel_id=1, source_target_pairs={{0,2},{1,3},{2,0},{3,1},{4,6},{5,7},{6,4},{7,5},{8,10},{9,11},{10,... | collective-permute-start | bytes 393224 | tf_op jit(solution)/shard_map/ppermute | solution.py:55
  120.4 3.9 %collective-permute-done.29 = bf16[2,128,256]{2,1,0:T(8,128)(2,1)S(1)} collective-permute-done((bf16[2,128,256]{2,1,0:T(8,128)(2,1)S(1)}, bf16[2,128,256]{2,1,0:T(8,128)(2,1)S(1)}, u32[]{:S(2)}, u32[]{:S(2)}) %collective-permute-start.29) | collective-permute-done | bytes 131104 | tf_op jit(solution)/shard_map/ppermute | solution.py:55
  124.5 8.9 %collective-permute-start.53 = (f32[128,256]{1,0:T(8,128)S(1)}, f32[128,256]{1,0:T(8,128)S(1)}, u32[]{:S(2)}, u32[]{:S(2)}) collective-permute-start(f32[128,256]{1,0:T(8,128)S(1)} %add_add_fusion.2), channel_id=1, source_target_pairs={{0,96},{16,112},{32,0},{48,16},{64,32},{80,48},{96,64},{112,80},{1... | collective-permute-start | bytes 393224 | tf_op jit(solution)/shard_map/ppermute | solution.py:43
  136.8 6.2 %collective-permute-done.52 = f32[128,256]{1,0:T(8,128)S(1)} collective-permute-done((f32[128,256]{1,0:T(8,128)S(1)}, f32[128,256]{1,0:T(8,128)S(1)}, u32[]{:S(2)}, u32[]{:S(2)}) %collective-permute-start.52) | collective-permute-done | bytes 131104 | tf_op jit(solution)/shard_map/ppermute | solution.py:43
  148.7 3.9 %collective-permute-done.55 = f32[128,256]{1,0:T(8,128)S(1)} collective-permute-done((f32[128,256]{1,0:T(8,128)S(1)}, f32[128,256]{1,0:T(8,128)S(1)}, u32[]{:S(2)}, u32[]{:S(2)}) %collective-permute-start.55) | collective-permute-done | bytes 131104 | tf_op jit(solution)/shard_map/ppermute | solution.py:298
  152.8 7.9 %backward_cell.1 = (bf16[4,128,256]{2,1,0:T(8,128)(2,1)S(1)}, bf16[4,128,256]{2,1,0:T(8,128)(2,1)S(1)}, bf16[4,128,256]{2,1,0:T(8,128)(2,1)S(1)}, bf16[4,128,256...) custom-call(s32[128]{0:T(128)S(1)} %get-tuple-element.33.out_ref, ...), custom_call_target="tpu_custom_call" | custom-call | flops 1073741824 | bytes 10485760 | tf_op jit(solution)/shard_map/backward_cell/pallas_call | solution.py:154
  160.8 3.2 %collective-permute-start.40 = (bf16[4,128,256]{2,1,0:T(8,128)(2,1)S(1)}, bf16[4,128,256]{2,1,0:T(8,128)(2,1)S(1)}, u32[]{:S(2)}, u32[]{:S(2)}) collective-permute-start(bf16[4,128,256]{2,1,0:T(8,128)(2,1)S(1)} %get-tuple-element.22), channel_id=1, source_target_pairs={{0,96},{16,112},{32,0},{48,16},{64,32},{80,48},{96,64},{112,80},{1... | collective-permute-start | bytes 786440 | tf_op jit(solution)/shard_map/ppermute | solution.py:43
  164.9 4.2 %collective-permute-done.39 = bf16[4,128,256]{2,1,0:T(8,128)(2,1)S(1)} collective-permute-done((bf16[4,128,256]{2,1,0:T(8,128)(2,1)S(1)}, bf16[4,128,256]{2,1,0:T(8,128)(2,1)S(1)}, u32[]{:S(2)}, u32[]{:S(2)}) %collective-permute-start.39) | collective-permute-done | bytes 262176 | tf_op jit(solution)/shard_map/ppermute | solution.py:43
  169.1 4.0 %collective-permute-done.40 = bf16[4,128,256]{2,1,0:T(8,128)(2,1)S(1)} collective-permute-done((bf16[4,128,256]{2,1,0:T(8,128)(2,1)S(1)}, bf16[4,128,256]{2,1,0:T(8,128)(2,1)S(1)}, u32[]{:S(2)}, u32[]{:S(2)}) %collective-permute-start.40) | collective-permute-done | bytes 262176 | tf_op jit(solution)/shard_map/ppermute | solution.py:43
  174.2 3.3 %collective-permute-done.43 = bf16[8,128,256]{2,1,0:T(8,128)(2,1)S(1)} collective-permute-done((bf16[8,128,256]{2,1,0:T(8,128)(2,1)S(1)}, bf16[8,128,256]{2,1,0:T(8,128)(2,1)S(1)}, u32[]{:S(2)}, u32[]{:S(2)}) %collective-permute-start.43) | collective-permute-done | bytes 524320 | tf_op jit(solution)/shard_map/ppermute | solution.py:47
  178.7 3.1 %collective-permute-start.46 = (bf16[2,128,256]{2,1,0:T(8,128)(2,1)S(1)}, bf16[2,128,256]{2,1,0:T(8,128)(2,1)S(1)}, u32[]{:S(2)}, u32[]{:S(2)}) collective-permute-start(bf16[2,128,256]{2,1,0:T(8,128)(2,1)S(1)} %get-tuple-element.46), channel_id=1, source_target_pairs={{0,64},{16,80},{32,96},{48,112},{64,0},{80,16},{96,32},{112,48},{1... | collective-permute-start | bytes 393224 | tf_op jit(solution)/shard_map/ppermute | solution.py:43
  184.4 3.2 %collective-permute-done.46 = bf16[2,128,256]{2,1,0:T(8,128)(2,1)S(1)} collective-permute-done((bf16[2,128,256]{2,1,0:T(8,128)(2,1)S(1)}, bf16[2,128,256]{2,1,0:T(8,128)(2,1)S(1)}, u32[]{:S(2)}, u32[]{:S(2)}) %collective-permute-start.46) | collective-permute-done | bytes 131104 | tf_op jit(solution)/shard_map/ppermute | solution.py:43
  (142 shorter events, 78.3 us)
Async XLA Ops:
  1.6 10.3 %collective-permute-start.10 = (bf16[2,128,256]{2,1,0:T(8,128)(2,1)S(1)}, bf16[2,128,256]{2,1,0:T(8,128)(2,1)S(1)}, u32[]{:S(2)}, u32[]{:S(2)}) collective-permute-start(bf16[2,128,256]{2,1,0:T(8,128)(2,1)S(1)} %bitcast.36), channel_id=1, source_target_pairs={{0,64},{16,80},{32,96},{48,112},{64,0},{80,16},{96,32},{112,48},{1... | collective-permute-start | bytes 393224 | tf_op jit(solution)/shard_map/ppermute | solution.py:43
  12.8 9.0 %collective-permute-start.4 = (bf16[2,128,256]{2,1,0:T(8,128)(2,1)S(1)}, bf16[2,128,256]{2,1,0:T(8,128)(2,1)S(1)}, u32[]{:S(2)}, u32[]{:S(2)}) collective-permute-start(bf16[2,128,256]{2,1,0:T(8,128)(2,1)S(1)} %bitcast.33), channel_id=1, source_target_pairs={{0,96},{16,112},{32,0},{48,16},{64,32},{80,48},{96,64},{112,80},{1... | collective-permute-start | bytes 393224 | tf_op jit(solution)/shard_map/ppermute | solution.py:43
  45.7 15.2 %collective-permute-start.15 = (bf16[4,128,256]{2,1,0:T(8,128)(2,1)S(1)}, bf16[4,128,256]{2,1,0:T(8,128)(2,1)S(1)}, u32[]{:S(2)}, u32[]{:S(2)}) collective-permute-start(bf16[4,128,256]{2,1,0:T(8,128)(2,1)S(1)} %get-tuple-element.42), channel_id=1, source_target_pairs={{0,4},{1,5},{2,6},{3,7},{4,8},{5,9},{6,10},{7,11},{8,12},{9,13},{1... | collective-permute-start | bytes 786440 | tf_op jit(solution)/shard_map/ppermute | solution.py:51
  45.8 15.2 %collective-permute-start.17 = (bf16[4,128,256]{2,1,0:T(8,128)(2,1)S(1)}, bf16[4,128,256]{2,1,0:T(8,128)(2,1)S(1)}, u32[]{:S(2)}, u32[]{:S(2)}) collective-permute-start(bf16[4,128,256]{2,1,0:T(8,128)(2,1)S(1)} %get-tuple-element.43), channel_id=1, source_target_pairs={{0,8},{1,9},{2,10},{3,11},{4,12},{5,13},{6,14},{7,15},{8,0},{9,1},... | collective-permute-start | bytes 786440 | tf_op jit(solution)/shard_map/ppermute | solution.py:51
  48.3 13.3 %collective-permute-start.16 = (bf16[4,128,256]{2,1,0:T(8,128)(2,1)S(1)}, bf16[4,128,256]{2,1,0:T(8,128)(2,1)S(1)}, u32[]{:S(2)}, u32[]{:S(2)}) collective-permute-start(bf16[4,128,256]{2,1,0:T(8,128)(2,1)S(1)} %get-tuple-element.44), channel_id=1, source_target_pairs={{0,12},{1,13},{2,14},{3,15},{4,0},{5,1},{6,2},{7,3},{8,4},{9,5},{1... | collective-permute-start | bytes 786440 | tf_op jit(solution)/shard_map/ppermute | solution.py:51
  49.1 16.8 %collective-permute-start.19 = (bf16[8,128,256]{2,1,0:T(8,128)(2,1)S(1)}, bf16[8,128,256]{2,1,0:T(8,128)(2,1)S(1)}, u32[]{:S(2)}, u32[]{:S(2)}) collective-permute-start(bf16[8,128,256]{2,1,0:T(8,128)(2,1)S(1)} %slice.95), channel_id=1, source_target_pairs={{0,2},{1,3},{2,0},{3,1},{4,6},{5,7},{6,4},{7,5},{8,10},{9,11},{10,... | collective-permute-start | bytes 1572872 | tf_op jit(solution)/shard_map/ppermute | solution.py:55
  76.7 40.0 %collective-permute-start.28 = (bf16[2,128,256]{2,1,0:T(8,128)(2,1)S(1)}, bf16[2,128,256]{2,1,0:T(8,128)(2,1)S(1)}, u32[]{:S(2)}, u32[]{:S(2)}) collective-permute-start(bf16[2,128,256]{2,1,0:T(8,128)(2,1)S(1)} %get-tuple-element.18), channel_id=1, source_target_pairs={{0,4},{1,5},{2,6},{3,7},{4,8},{5,9},{6,10},{7,11},{8,12},{9,13},{1... | collective-permute-start | bytes 393224 | tf_op jit(solution)/shard_map/ppermute | solution.py:51
  76.7 24.3 %collective-permute-start.26 = (bf16[2,128,256]{2,1,0:T(8,128)(2,1)S(1)}, bf16[2,128,256]{2,1,0:T(8,128)(2,1)S(1)}, u32[]{:S(2)}, u32[]{:S(2)}) collective-permute-start(bf16[2,128,256]{2,1,0:T(8,128)(2,1)S(1)} %get-tuple-element.18), channel_id=1, source_target_pairs={{0,8},{1,9},{2,10},{3,11},{4,12},{5,13},{6,14},{7,15},{8,0},{9,1},... | collective-permute-start | bytes 393224 | tf_op jit(solution)/shard_map/ppermute | solution.py:51
  79.4 9.9 %collective-permute-start.24 = (bf16[2,128,256]{2,1,0:T(8,128)(2,1)S(1)}, bf16[2,128,256]{2,1,0:T(8,128)(2,1)S(1)}, u32[]{:S(2)}, u32[]{:S(2)}) collective-permute-start(bf16[2,128,256]{2,1,0:T(8,128)(2,1)S(1)} %get-tuple-element.18), channel_id=1, source_target_pairs={{0,12},{1,13},{2,14},{3,15},{4,0},{5,1},{6,2},{7,3},{8,4},{9,5},{1... | collective-permute-start | bytes 393224 | tf_op jit(solution)/shard_map/ppermute | solution.py:51
  84.4 28.2 %collective-permute-start.35 = (bf16[2,128,256]{2,1,0:T(8,128)(2,1)S(1)}, bf16[2,128,256]{2,1,0:T(8,128)(2,1)S(1)}, u32[]{:S(2)}, u32[]{:S(2)}) collective-permute-start(bf16[2,128,256]{2,1,0:T(8,128)(2,1)S(1)} %get-tuple-element.19), channel_id=1, source_target_pairs={{0,4},{1,5},{2,6},{3,7},{4,8},{5,9},{6,10},{7,11},{8,12},{9,13},{1... | collective-permute-start | bytes 393224 | tf_op jit(solution)/shard_map/ppermute | solution.py:51
  95.7 12.3 %collective-permute-start.33 = (bf16[2,128,256]{2,1,0:T(8,128)(2,1)S(1)}, bf16[2,128,256]{2,1,0:T(8,128)(2,1)S(1)}, u32[]{:S(2)}, u32[]{:S(2)}) collective-permute-start(bf16[2,128,256]{2,1,0:T(8,128)(2,1)S(1)} %get-tuple-element.19), channel_id=1, source_target_pairs={{0,8},{1,9},{2,10},{3,11},{4,12},{5,13},{6,14},{7,15},{8,0},{9,1},... | collective-permute-start | bytes 393224 | tf_op jit(solution)/shard_map/ppermute | solution.py:51
  101.0 23.5 %collective-permute-start.50 = (f32[128,256]{1,0:T(8,128)S(1)}, f32[128,256]{1,0:T(8,128)S(1)}, u32[]{:S(2)}, u32[]{:S(2)}) collective-permute-start(f32[128,256]{1,0:T(8,128)S(1)} %dynamic-slice_add_fusion), channel_id=1, source_target_pairs={{0,12},{1,13},{2,14},{3,15},{4,0},{5,1},{6,2},{7,3},{8,4},{9,5},{1... | collective-permute-start | bytes 393224 | tf_op jit(solution)/shard_map/ppermute | solution.py:51
  108.0 16.5 %collective-permute-start.49 = (f32[128,256]{1,0:T(8,128)S(1)}, f32[128,256]{1,0:T(8,128)S(1)}, u32[]{:S(2)}, u32[]{:S(2)}) collective-permute-start(f32[128,256]{1,0:T(8,128)S(1)} %dynamic-slice_add_fusion), channel_id=1, source_target_pairs={{0,4},{1,5},{2,6},{3,7},{4,8},{5,9},{6,10},{7,11},{8,12},{9,13},{1... | collective-permute-start | bytes 393224 | tf_op jit(solution)/shard_map/ppermute | solution.py:51
  120.3 32.5 %collective-permute-start.38 = (bf16[16,128,256]{2,1,0:T(8,128)(2,1)S(1)}, bf16[16,128,256]{2,1,0:T(8,128)(2,1)}, u32[]{:S(2)}, u32[]{:S(2)}) collective-permute-start(bf16[16,128,256]{2,1,0:T(8,128)(2,1)S(1)} %constant_dynamic-update-slice_fusion.8.rest_1_), channel_id=1, source_target_pairs={{0,1},{1,0},{2,3},{3,2},{4,5},{5,4},{6,7},{7,6},{8,9},{9,8},{10,11... | collective-permute-start | bytes 3145736 | tf_op jit(solution)/shard_map/ppermute | solution.py:59
  124.3 28.4 %collective-permute-start.37 = (bf16[16,128,256]{2,1,0:T(8,128)(2,1)S(1)}, bf16[16,128,256]{2,1,0:T(8,128)(2,1)S(1)}, u32[]{:S(2)}, u32[]{:S(2)}) collective-permute-start(bf16[16,128,256]{2,1,0:T(8,128)(2,1)S(1)} %constant_dynamic-update-slice_fusion.rest_0_), channel_id=1, source_target_pairs={{0,1},{1,0},{2,3},{3,2},{4,5},{5,4},{6,7},{7,6},{8,9},{9,8},{10,11... | collective-permute-start | bytes 3145736 | tf_op jit(solution)/shard_map/ppermute | solution.py:59
  124.5 12.3 %collective-permute-start.53 = (f32[128,256]{1,0:T(8,128)S(1)}, f32[128,256]{1,0:T(8,128)S(1)}, u32[]{:S(2)}, u32[]{:S(2)}) collective-permute-start(f32[128,256]{1,0:T(8,128)S(1)} %add_add_fusion.2), channel_id=1, source_target_pairs={{0,96},{16,112},{32,0},{48,16},{64,32},{80,48},{96,64},{112,80},{1... | collective-permute-start | bytes 393224 | tf_op jit(solution)/shard_map/ppermute | solution.py:43
  133.4 9.6 %collective-permute-start.52 = (f32[128,256]{1,0:T(8,128)S(1)}, f32[128,256]{1,0:T(8,128)S(1)}, u32[]{:S(2)}, u32[]{:S(2)}) collective-permute-start(f32[128,256]{1,0:T(8,128)S(1)} %add_add_fusion.2), channel_id=1, source_target_pairs={{0,32},{16,48},{32,64},{48,80},{64,96},{80,112},{96,0},{112,16},{1... | collective-permute-start | bytes 393224 | tf_op jit(solution)/shard_map/ppermute | solution.py:43
  133.4 9.6 %collective-permute-start.51 = (f32[128,256]{1,0:T(8,128)S(1)}, f32[128,256]{1,0:T(8,128)S(1)}, u32[]{:S(2)}, u32[]{:S(2)}) collective-permute-start(f32[128,256]{1,0:T(8,128)S(1)} %add_add_fusion.2), channel_id=1, source_target_pairs={{0,64},{16,80},{32,96},{48,112},{64,0},{80,16},{96,32},{112,48},{1... | collective-permute-start | bytes 393224 | tf_op jit(solution)/shard_map/ppermute | solution.py:43
  152.7 11.5 %collective-permute-start.57 = (f32[128,256]{1,0:T(8,128)S(1)}, f32[128,256]{1,0:T(8,128)S(1)}, u32[]{:S(2)}, u32[]{:S(2)}) collective-permute-start(f32[128,256]{1,0:T(8,128)S(1)} %add_add_fusion), channel_id=1, source_target_pairs={{0,1},{1,0},{2,3},{3,2},{4,5},{5,4},{6,7},{7,6},{8,9},{9,8},{10,11... | collective-permute-start | bytes 393224 | tf_op jit(solution)/shard_map/ppermute | solution.py:59
  160.8 12.2 %collective-permute-start.40 = (bf16[4,128,256]{2,1,0:T(8,128)(2,1)S(1)}, bf16[4,128,256]{2,1,0:T(8,128)(2,1)S(1)}, u32[]{:S(2)}, u32[]{:S(2)}) collective-permute-start(bf16[4,128,256]{2,1,0:T(8,128)(2,1)S(1)} %get-tuple-element.22), channel_id=1, source_target_pairs={{0,96},{16,112},{32,0},{48,16},{64,32},{80,48},{96,64},{112,80},{1... | collective-permute-start | bytes 786440 | tf_op jit(solution)/shard_map/ppermute | solution.py:43
  164.0 10.0 %collective-permute-start.41 = (bf16[4,128,256]{2,1,0:T(8,128)(2,1)S(1)}, bf16[4,128,256]{2,1,0:T(8,128)(2,1)S(1)}, u32[]{:S(2)}, u32[]{:S(2)}) collective-permute-start(bf16[4,128,256]{2,1,0:T(8,128)(2,1)S(1)} %get-tuple-element.23), channel_id=1, source_target_pairs={{0,64},{16,80},{32,96},{48,112},{64,0},{80,16},{96,32},{112,48},{1... | collective-permute-start | bytes 786440 | tf_op jit(solution)/shard_map/ppermute | solution.py:43
  164.0 13.6 %collective-permute-start.43 = (bf16[8,128,256]{2,1,0:T(8,128)(2,1)S(1)}, bf16[8,128,256]{2,1,0:T(8,128)(2,1)S(1)}, u32[]{:S(2)}, u32[]{:S(2)}) collective-permute-start(bf16[8,128,256]{2,1,0:T(8,128)(2,1)S(1)} %get-tuple-element.25), channel_id=1, source_target_pairs={{0,16},{16,0},{32,48},{48,32},{64,80},{80,64},{96,112},{112,96},{1... | collective-permute-start | bytes 1572872 | tf_op jit(solution)/shard_map/ppermute | solution.py:47
  174.2 10.2 %collective-permute-start.42 = (bf16[2,128,256]{2,1,0:T(8,128)(2,1)S(1)}, bf16[2,128,256]{2,1,0:T(8,128)(2,1)S(1)}, u32[]{:S(2)}, u32[]{:S(2)}) collective-permute-start(bf16[2,128,256]{2,1,0:T(8,128)(2,1)S(1)} %slice.101), channel_id=1, source_target_pairs={{0,16},{16,0},{32,48},{48,32},{64,80},{80,64},{96,112},{112,96},{1... | collective-permute-start | bytes 393224 | tf_op jit(solution)/shard_map/ppermute | solution.py:47
  178.7 8.8 %collective-permute-start.46 = (bf16[2,128,256]{2,1,0:T(8,128)(2,1)S(1)}, bf16[2,128,256]{2,1,0:T(8,128)(2,1)S(1)}, u32[]{:S(2)}, u32[]{:S(2)}) collective-permute-start(bf16[2,128,256]{2,1,0:T(8,128)(2,1)S(1)} %get-tuple-element.46), channel_id=1, source_target_pairs={{0,64},{16,80},{32,96},{48,112},{64,0},{80,16},{96,32},{112,48},{1... | collective-permute-start | bytes 393224 | tf_op jit(solution)/shard_map/ppermute | solution.py:43
  (36 other events, 279.4 us)

commit v2 on v0

v2 whole, which is shorter than its diff:
```python
import functools
import math

import jax
import jax.numpy as jnp
from jax import lax
from jax.experimental import pallas as pl
from jax.experimental.pallas import tpu as pltpu
from jax.sharding import PartitionSpec as P

BLK = 128
WIDTH = 256
CAP = 128
UNROLL = 16
BF16 = jnp.bfloat16
F32 = jnp.float32

NZ, NX = 4, 4


def z_perm(step):
    return [(z * 2 + yl, (z + step) % NZ * 2 + yl) for z in range(NZ) for yl in range(2)]


def yl_perm():
    return [(r, r ^ 1) for r in range(2 * NZ)]


def x_perm(step):
    return [(x * 4 + q, (x + step) % NX * 4 + q) for x in range(NX) for q in range(4)]


def yh_perm():
    return [(c, c ^ 2) for c in range(4 * NX)]


def core_perm():
    return [(c, c ^ 1) for c in range(4 * NX)]


def z_send(v, step):
    return lax.ppermute(v, "row", z_perm(step))


def yl_swap(v):
    return lax.ppermute(v, "row", yl_perm())


def x_send(v, step):
    return lax.ppermute(v, "col", x_perm(step))


def yh_swap(v):
    return lax.ppermute(v, "col", yh_perm())


def core_swap(v):
    return lax.ppermute(v, "col", core_perm())


def add(*terms):
    total = terms[0].astype(F32)
    for term in terms[1:]:
        total = total + term.astype(F32)
    return total.astype(BF16)


def cell_kernel(transposed, places, n_out, out_ref, in_ref, cnt_ref, tiles, *rest):
    n_in = len(places)
    pieces = rest[:n_in]
    outs = rest[n_in : n_in + n_out]
    blocks, acc, piece_sems = rest[n_in + n_out :]
    copies = []
    for i, (piece, (first, size)) in enumerate(zip(pieces, places)):
        copy = pltpu.make_async_copy(piece, blocks.at[pl.ds(first, size)], piece_sems.at[i])
        copy.start()
        copies.append(copy)

    def clear(i, carry):
        acc[i] = jnp.zeros(acc.shape[1:], acc.dtype)
        return carry

    lax.fori_loop(0, acc.shape[0] - 1, clear, 0)
    for copy in copies:
        copy.wait()
    dims = (((0,), (0,)), ((), ())) if transposed else (((1,), (0,)), ((), ()))

    def group(i, carry):
        first = i * UNROLL
        products = [
            lax.dot_general(
                tiles[first + u], blocks[in_ref[first + u]], dims, preferred_element_type=F32
            )
            for u in range(UNROLL)
        ]
        for u in range(UNROLL):
            slot = out_ref[first + u]
            acc[slot] += products[u]
        return carry

    lax.fori_loop(0, (cnt_ref[0] + UNROLL - 1) // UNROLL, group, 0)
    first = 0
    for out in outs:
        def store(i, carry, out=out, first=first):
            out[i] = acc[first + i].astype(BF16)
            return carry

        lax.fori_loop(0, out.shape[0], store, 0)
        first += out.shape[0]


def cell_product(name, transposed, out_slot, in_slot, count, tiles, pieces, places, out_sizes, in_blocks):
    out_blocks = sum(out_sizes)
    live = jnp.arange(CAP, dtype=jnp.int32) < count[0]
    out_slot = jnp.where(live, out_slot, out_blocks)
    in_slot = jnp.where(live, in_slot, 0)
    kernel = functools.partial(cell_kernel, transposed, places, len(out_sizes))
    any_spec = pl.BlockSpec(memory_space=pl.ANY)
    vmem_spec = pl.BlockSpec(memory_space=pltpu.VMEM)
    return pl.pallas_call(
        kernel,
        grid_spec=pltpu.PrefetchScalarGridSpec(
            num_scalar_prefetch=3,
            grid=(),
            in_specs=[vmem_spec] + [any_spec] * len(pieces),
            out_specs=[vmem_spec] * len(out_sizes),
            scratch_shapes=[
                pltpu.VMEM((in_blocks, BLK, WIDTH), BF16),
                pltpu.VMEM((out_blocks + 1, BLK, WIDTH), F32),
                pltpu.SemaphoreType.DMA((len(pieces),)),
            ],
        ),
        out_shape=[jax.ShapeDtypeStruct((n, BLK, WIDTH), BF16) for n in out_sizes],
        compiler_params=pltpu.CompilerParams(vmem_limit_bytes=24 * 1024 * 1024),
        cost_estimate=pl.CostEstimate(
            flops=2 * CAP * BLK * BLK * WIDTH,
            bytes_accessed=2 * CAP * BLK * BLK + 2 * (in_blocks + out_blocks) * BLK * WIDTH,
            transcendentals=0,
        ),
        name=name,
    )(out_slot, in_slot, count, tiles, *pieces)


def dense_kernel(scale, n_terms, *refs):
    terms, (w_ref, cot_ref, out_ref, grad_ref, wg_ref) = refs[:n_terms], refs[n_terms:]
    total = terms[0][...].astype(F32)
    for term in terms[1:]:
        total = total + term[...].astype(F32)
    w = w_ref[...]
    agg = total.astype(BF16).reshape(cot_ref.shape)
    pre = jnp.dot(agg, w, preferred_element_type=F32)
    sig = jax.nn.sigmoid(pre)
    out_ref[...] = (pre * sig).astype(BF16)
    grad_pre = (cot_ref[...].astype(F32) * sig * (1.0 + pre * (1.0 - sig))).astype(BF16)
    grad_agg = lax.dot_general(
        grad_pre, w, (((1,), (1,)), ((), ())), preferred_element_type=F32
    ).astype(BF16)
    grad_ref[...] = grad_agg.reshape(grad_ref.shape)
    weight_grad = lax.dot_general(
        agg, grad_pre, (((0,), (0,)), ((), ())), preferred_element_type=F32
    )
    wg_ref[...] = weight_grad * scale


def dense(scale, terms, weight, cotangent):
    vmem_spec = pl.BlockSpec(memory_space=pltpu.VMEM)
    nodes = cotangent.shape[0]
    return pl.pallas_call(
        functools.partial(dense_kernel, scale, len(terms)),
        in_specs=[vmem_spec] * (len(terms) + 2),
        out_specs=[vmem_spec] * 3,
        out_shape=[
            jax.ShapeDtypeStruct((nodes, WIDTH), BF16),
            jax.ShapeDtypeStruct((nodes // BLK, BLK, WIDTH), BF16),
            jax.ShapeDtypeStruct((WIDTH, WIDTH), F32),
        ],
        compiler_params=pltpu.CompilerParams(vmem_limit_bytes=24 * 1024 * 1024),
        cost_estimate=pl.CostEstimate(
            flops=6 * nodes * WIDTH * WIDTH,
            bytes_accessed=8 * nodes * WIDTH,
            transcendentals=nodes * WIDTH,
        ),
        name="dense",
    )(*terms, weight, cotangent)


def gather(own, ring, swap, first_ties=(), second_ties=()):
    far = swap(own)
    up, down, across = ring(own, -1), ring(own, 1), ring(own, 2)
    far_up, far_down = ring(far, -1), ring(far, 1)
    far_across = swap(across)
    return [own, far, up, far_up, across, far_across, down, far_down]


def scatter_terms(chunks, ring, swap):
    two = swap(add(*chunks[2][1]))
    up, down = ring(add(*chunks[1][1]), 1), ring(add(*chunks[3][1]), -1)
    own_up, own_down = ring(add(*chunks[1][0]), 1), ring(add(*chunks[3][0]), -1)
    across = ring(add(*chunks[2][0], two), 2)
    far = swap(add(*chunks[0][1], up, down))
    return [*chunks[0][0], own_up, own_down, across, far]


def y_send(v, step):
    pairs = []
    for r in range(2 * NZ):
        for c in range(4 * NX):
            y = ((c // 2 % 2) * 2 + r % 2 + step) % 4
            to = (r - r % 2 + y % 2) * (4 * NX) + c - (c & 2) + (y // 2) * 2
            pairs.append((r * 4 * NX + c, to))
    return lax.ppermute(v, ("row", "col"), pairs)


def pair_perm(extent, stride, bit):
    return [(i, i ^ (stride * bit)) for i in range(extent)]


def tie(*arrays):
    return lax.optimization_barrier(arrays)


def pair_sum(v, axis, flip):
    return v + lax.ppermute(v, axis, [(i, i ^ flip) for i in range(lax.axis_size(axis))])


def shards(tile_values, tile_rows, tile_cols, tile_counts, features, weight, cotangent):
    row, col = lax.axis_index("row"), lax.axis_index("col")
    z, yl = row // 2, row % 2
    x, yh, core = col // 4, col // 2 % 2, col % 2
    tiles = tile_values[0, 0]
    t_row, t_col = tile_rows[0, 0], tile_cols[0, 0]
    count = tile_counts[0]

    own, j = t_row // 4, t_row % 4
    dx, dyh, dk = (own // 4 - x) % 4, (own // 2 % 2) ^ yh, (own % 2) ^ core
    row_slot = dk * 32 + dx * 8 + dyh * 4 + j
    own, j = t_col // 4, t_col % 4
    dz, dyl = (own // 2 - z) % 4, (own % 2) ^ yl
    col_slot = dz * 8 + dyl * 4 + j
    places = [(4 * i, 4) for i in range(16)]

    pieces = gather(features.reshape(4, BLK, WIDTH), z_send, yl_swap)
    parts = cell_product(
        "forward_cell", False, row_slot, col_slot, count, tiles, pieces, places[:8], [4] * 16, 32
    )
    mine, other = parts[:8], [core_swap(v) for v in parts[8:]]
    chunks = [[(mine[2 * d + s], other[2 * d + s]) for s in range(2)] for d in range(4)]
    terms = scatter_terms(chunks, x_send, yh_swap)
    scale = 1.0 / math.sqrt(features.shape[0] * lax.axis_size("row") * lax.axis_size("col"))
    output, grad_agg, local_grad = dense(scale, terms, weight, cotangent)

    half = WIDTH // 2
    term = lax.dynamic_slice_in_dim(local_grad, core * half, half, 0)
    term = term + core_swap(lax.dynamic_slice_in_dim(local_grad, (1 - core) * half, half, 0))
    term = pair_sum(term, "row", 2)
    pieces = gather(grad_agg, x_send, yh_swap)
    term = pair_sum(term, "row", 4)
    pieces = pieces + [core_swap(v) for v in pieces]
    term = pair_sum(term, "row", 1)
    term, *pieces = tie(term, *pieces)
    back = cell_product(
        "backward_cell", True, col_slot, row_slot, count, tiles, pieces, places, [4] * 8, 64
    )
    term = pair_sum(term, "col", 2)
    term, *back = tie(term, *back)
    term = pair_sum(term, "col", 4)
    term = pair_sum(term, "col", 8)
    far_term = core_swap(term)
    weight_grad = jnp.concatenate(
        [jnp.where(core == 0, term, far_term), jnp.where(core == 0, far_term, term)], axis=0
    )
    chunks = [[(back[2 * d + s],) for s in range(2)] for d in range(4)]
    grad_features = add(*scatter_terms(chunks, z_send, yl_swap))
    return (output, grad_features.reshape(4 * BLK, WIDTH), weight_grad)


def solution(mesh):
    in_specs = (
        P("row", "col", None, None, None),
        P("row", "col", None),
        P("row", "col", None),
        P("row", "col"),
        P(("col", "row"), None),
        P(),
        P(("row", "col"), None),
    )
    out_specs = (P(("row", "col"), None), P(("col", "row"), None), P())
    return jax.shard_map(shards, mesh=mesh, in_specs=in_specs, out_specs=out_specs, check_vma=False)
```

time: 497 us -> 138 us (0.28)
  waiting for transfers between devices: 302 us -> 56.1 us
  other arithmetic: 88.5 us -> 3.18 us
  starting transfers between devices: 0.38 us -> 64 us
  local copies, waits for them, and re-layouts: 58.5 us -> 5.35 us
  matrix products: 31.6 us -> 0 us
  between operations: 14.5 us -> 1.57 us
  Pallas kernels: 0 us -> 6.57 us
    reduce_scatter x2 -> x0, waiting for transfers between devices: 131 us -> none  [the longest x1 79.6 us: shards(): lax.psum_scatter(partial_value.astype(jnp.bfloat16), 'col', scatter_dimen...]
    all_gather x2 -> x0, waiting for transfers between devices: 108 us -> none  [the longest x1 55.2 us: shards(): column_feats = lax.all_gather(features, 'row', axis=0, tiled=True)]
    scatter-add x2 -> x0, other arithmetic: 76.3 us -> none  [the longest x1 38.5 us: shards(): jax.ops.segment_sum(products, tile_row, num_segments=row_blocks)]
    ppermute x0 -> x52, starting transfers between devices: none -> 64 us  [the longest x10 18.3 us: z_send(): return lax.ppermute(v, 'row', z_perm(step))]
    psum x1 -> x0, waiting for transfers between devices: 62.6 us -> none  [shards(): weight_grad = lax.psum(local_grad, ('row', 'col')) * scale]
    ppermute x0 -> x52, waiting for transfers between devices: none -> 56.1 us  [the longest x10 17.8 us: x_send(): return lax.ppermute(v, 'col', x_perm(step))]
    mul x2 -> x0, local copies, waits for them, and re-layouts: 34.9 us -> none  [the longest x1 17.5 us: shards(): jnp.einsum('kab,kaw->kbw', blocks, picked_grads, preferred_element_type=j...]
    dot_general x5 -> x0, matrix products: 31.6 us -> none  [the longest x1 13.7 us: shards(): jnp.einsum('kab,kaw->kbw', blocks, picked_grads, preferred_element_type=j...]
  transfers between devices with their start and end apart: 5 -> 52, of which waited for: 5 -> 27; matrix products, arithmetic and copies ran while one was open for 18% -> 2% of each run, Pallas kernels for 0% -> 2%
where the time goes in v2:
time: 138 us; the launch traced here: 137 us
  starting transfers between devices  64 us (46%)
  waiting for transfers between devices  56.1 us (41%)
  Pallas kernels  6.57 us (5%)
  local copies, waits for them, and re-layouts  5.35 us (4%)
  other arithmetic  3.18 us (2%)
  between operations  1.57 us (1%)
    ppermute x10, starting transfers between devices, z_send(): return lax.ppermute(v, 'row', z_perm(step))  18.3 us
    ppermute x10, waiting for transfers between devices, x_send(): return lax.ppermute(v, 'col', x_perm(step))  17.8 us
    ppermute x10, starting transfers between devices, x_send(): return lax.ppermute(v, 'col', x_perm(step))  15.7 us
    ppermute x10, waiting for transfers between devices, z_send(): return lax.ppermute(v, 'row', z_perm(step))  13 us
    ppermute x4, starting transfers between devices, yh_swap(): return lax.ppermute(v, 'col', yh_perm())  12.7 us
    ppermute x6, starting transfers between devices, pair_sum(): lax.ppermute(v, axis, [(i, i ^ flip) for i in range(lax.axis_size(axis))])  11.3 us
    ppermute x6, waiting for transfers between devices, pair_sum(): lax.ppermute(v, axis, [(i, i ^ flip) for i in range(lax.axis_size(axis))])  9.47 us
    ppermute x4, waiting for transfers between devices, yh_swap(): return lax.ppermute(v, 'col', yh_perm())  6.43 us
  transfers between devices with their start and end apart: 52, of which 27 were waited for; matrix products, arithmetic and copies ran while one was open for 2% of the time, Pallas kernels for 2%

profile of v2, /device:TPU:0, one launch (start us, length us, event | category | flops | bytes accessed | tf_op | source)
XLA Modules:
  0.0 136.8 jit_solution(16257820689298855476)
XLA Ops:
  2.4 3.9 %collective-permute-start.3 = (bf16[4,128,256]{2,1,0:T(8,128)(2,1)}, bf16[4,128,256]{2,1,0:T(8,128)(2,1)S(1)}, u32[]{:S(2)}, u32[]{:S(2)}) collective-permute-start(bf16[4,128,256]{2,1,0:T(8,128)(2,1)} %bitcast.41), channel_id=1, source_target_pairs={{0,64},{16,80},{32,96},{48,112},{64,0},{80,16},{96,32},{112,48},{1... | collective-permute-start | bytes 786440 | tf_op jit(solution)/shard_map/ppermute | solution.py:42
  11.0 3.2 %collective-permute-start.2 = (bf16[4,128,256]{2,1,0:T(8,128)(2,1)S(1)}, bf16[4,128,256]{2,1,0:T(8,128)(2,1)S(1)}, u32[]{:S(2)}, u32[]{:S(2)}) collective-permute-start(bf16[4,128,256]{2,1,0:T(8,128)(2,1)S(1)} %collective-permute-done.rest_1_), channel_id=1, source_target_pairs={{0,96},{16,112},{32,0},{48,16},{64,32},{80,48},{96,64},{112,80},{1... | collective-permute-start | bytes 786440 | tf_op jit(solution)/shard_map/ppermute | solution.py:42
  14.7 4.3 %collective-permute-done.5.rest_6_ = bf16[4,128,256]{2,1,0:T(8,128)(2,1)S(1)} collective-permute-done((bf16[4,128,256]{2,1,0:T(8,128)(2,1)}, bf16[4,128,256]{2,1,0:T(8,128)(2,1)S(1)}, u32[]{:S(2)}, u32[]{:S(2)}) %collective-permute-start.5) | collective-permute-done | bytes 262176 | tf_op jit(solution)/shard_map/ppermute | solution.py:42
  20.6 3.2 %collective-permute-done.6.rest_7_ = bf16[4,128,256]{2,1,0:T(8,128)(2,1)S(1)} collective-permute-done((bf16[4,128,256]{2,1,0:T(8,128)(2,1)S(1)}, bf16[4,128,256]{2,1,0:T(8,128)(2,1)S(1)}, u32[]{:S(2)}, u32[]{:S(2)}) %collective-permute-start.6) | collective-permute-done | bytes 262176 | tf_op jit(solution)/shard_map/ppermute | solution.py:42
  27.6 2.9 %forward_cell.1 = (bf16[4,128,256]{2,1,0:T(8,128)(2,1)S(1)}, bf16[4,128,256]{2,1,0:T(8,128)(2,1)S(1)}, bf16[4,128,256]{2,1,0:T(8,128)(2,1)S(1)}, bf16[4,128,256]...) custom-call(s32[128]{0:T(128)S(1)} %fusion.19.out_ref, ...), custom_call_target="tpu_custom_call" | custom-call | flops 1073741824 | bytes 10485760 | tf_op jit(solution)/shard_map/forward_cell/pallas_call | solution.py:120
  34.1 3.8 %collective-permute-start.14 = (bf16[4,128,256]{2,1,0:T(8,128)(2,1)S(1)}, bf16[4,128,256]{2,1,0:T(8,128)(2,1)S(1)}, u32[]{:S(2)}, u32[]{:S(2)}) collective-permute-start(bf16[4,128,256]{2,1,0:T(8,128)(2,1)S(1)} %add_convert_fusion.7), channel_id=1, source_target_pairs={{0,2},{1,3},{2,0},{3,1},{4,6},{5,7},{6,4},{7,5},{8,10},{9,11},{10,... | collective-permute-start | bytes 786440 | tf_op jit(solution)/shard_map/ppermute | solution.py:54
  41.6 2.9 %collective-permute-done.14 = bf16[4,128,256]{2,1,0:T(8,128)(2,1)S(1)} collective-permute-done((bf16[4,128,256]{2,1,0:T(8,128)(2,1)S(1)}, bf16[4,128,256]{2,1,0:T(8,128)(2,1)S(1)}, u32[]{:S(2)}, u32[]{:S(2)}) %collective-permute-start.14) | collective-permute-done | bytes 262176 | tf_op jit(solution)/shard_map/ppermute | solution.py:54
  49.7 3.0 %collective-permute-start.21 = (bf16[4,128,256]{2,1,0:T(8,128)(2,1)S(1)}, bf16[4,128,256]{2,1,0:T(8,128)(2,1)S(1)}, u32[]{:S(2)}, u32[]{:S(2)}) collective-permute-start(bf16[4,128,256]{2,1,0:T(8,128)(2,1)S(1)} %add_convert_fusion.3), channel_id=1, source_target_pairs={{0,2},{1,3},{2,0},{3,1},{4,6},{5,7},{6,4},{7,5},{8,10},{9,11},{10,... | collective-permute-start | bytes 786440 | tf_op jit(solution)/shard_map/ppermute | solution.py:54
  54.7 3.9 %collective-permute-done.11.refs_3_ = bf16[4,128,256]{2,1,0:T(8,128)(2,1)S(1)} collective-permute-done((bf16[4,128,256]{2,1,0:T(8,128)(2,1)S(1)}, bf16[4,128,256]{2,1,0:T(8,128)(2,1)S(1)}, u32[]{:S(2)}, u32[]{:S(2)}) %collective-permute-start.11) | collective-permute-done | bytes 262176 | tf_op jit(solution)/shard_map/ppermute | solution.py:50
  62.3 2.4 %collective-permute-start.23 = (f32[128,256]{1,0:T(8,128)S(1)}, f32[128,256]{1,0:T(8,128)S(1)}, u32[]{:S(2)}, u32[]{:S(2)}) collective-permute-start(f32[128,256]{1,0:T(8,128)S(1)} %dynamic-slice_add_fusion), channel_id=1, source_target_pairs={{0,32},{16,48},{32,0},{48,16},{64,96},{80,112},{96,64},{112,80},{1... | collective-permute-start | bytes 393224 | tf_op jit(solution)/shard_map/ppermute | solution.py:223
  64.7 3.8 %collective-permute-done.23 = f32[128,256]{1,0:T(8,128)S(1)} collective-permute-done((f32[128,256]{1,0:T(8,128)S(1)}, f32[128,256]{1,0:T(8,128)S(1)}, u32[]{:S(2)}, u32[]{:S(2)}) %collective-permute-start.23) | collective-permute-done | bytes 131104 | tf_op jit(solution)/shard_map/ppermute | solution.py:223
  68.5 3.4 %collective-permute-start.24 = (f32[128,256]{1,0:T(8,128)S(1)}, f32[128,256]{1,0:T(8,128)S(1)}, u32[]{:S(2)}, u32[]{:S(2)}) collective-permute-start(f32[128,256]{1,0:T(8,128)S(1)} %add.169), channel_id=1, source_target_pairs={{0,64},{16,80},{32,96},{48,112},{64,0},{80,16},{96,32},{112,48},{1... | collective-permute-start | bytes 393224 | tf_op jit(solution)/shard_map/ppermute | solution.py:223
  73.2 2.7 %collective-permute-start.29 = (bf16[4,128,256]{2,1,0:T(8,128)(2,1)S(1)}, bf16[4,128,256]{2,1,0:T(8,128)(2,1)S(1)}, u32[]{:S(2)}, u32[]{:S(2)}) collective-permute-start(bf16[4,128,256]{2,1,0:T(8,128)(2,1)S(1)} %get-tuple-element.76.rest_0_), channel_id=1, source_target_pairs={{0,8},{1,9},{2,10},{3,11},{4,12},{5,13},{6,14},{7,15},{8,0},{9,1},... | collective-permute-start | bytes 786440 | tf_op jit(solution)/shard_map/ppermute | solution.py:50
  75.9 3.0 %collective-permute-start.26 = (bf16[4,128,256]{2,1,0:T(8,128)(2,1)S(1)}, bf16[4,128,256]{2,1,0:T(8,128)(2,1)S(1)}, u32[]{:S(2)}, u32[]{:S(2)}) collective-permute-start(bf16[4,128,256]{2,1,0:T(8,128)(2,1)S(1)} %get-tuple-element.76.rest_0_), channel_id=1, source_target_pairs={{0,2},{1,3},{2,0},{3,1},{4,6},{5,7},{6,4},{7,5},{8,10},{9,11},{10,... | collective-permute-start | bytes 786440 | tf_op jit(solution)/shard_map/ppermute | solution.py:54
  81.8 6.4 %collective-permute-done.29.rest_4_ = bf16[4,128,256]{2,1,0:T(8,128)(2,1)S(1)} collective-permute-done((bf16[4,128,256]{2,1,0:T(8,128)(2,1)S(1)}, bf16[4,128,256]{2,1,0:T(8,128)(2,1)S(1)}, u32[]{:S(2)}, u32[]{:S(2)}) %collective-permute-start.29) | collective-permute-done | bytes 262176 | tf_op jit(solution)/shard_map/ppermute | solution.py:50
  88.2 2.9 %collective-permute-start.30 = (bf16[4,128,256]{2,1,0:T(8,128)(2,1)S(1)}, bf16[4,128,256]{2,1,0:T(8,128)(2,1)S(1)}, u32[]{:S(2)}, u32[]{:S(2)}) collective-permute-start(bf16[4,128,256]{2,1,0:T(8,128)(2,1)S(1)} %collective-permute-done.29.rest_4_), channel_id=1, source_target_pairs={{0,2},{1,3},{2,0},{3,1},{4,6},{5,7},{6,4},{7,5},{8,10},{9,11},{10,... | collective-permute-start | bytes 786440 | tf_op jit(solution)/shard_map/ppermute | solution.py:54
  94.9 3.5 %collective-permute-done.30.rest_5_ = bf16[4,128,256]{2,1,0:T(8,128)(2,1)S(1)} collective-permute-done((bf16[4,128,256]{2,1,0:T(8,128)(2,1)S(1)}, bf16[4,128,256]{2,1,0:T(8,128)(2,1)S(1)}, u32[]{:S(2)}, u32[]{:S(2)}) %collective-permute-start.30) | collective-permute-done | bytes 262176 | tf_op jit(solution)/shard_map/ppermute | solution.py:54
  98.5 2.4 %collective-permute-done.32.rest_7_ = bf16[4,128,256]{2,1,0:T(8,128)(2,1)S(1)} collective-permute-done((bf16[4,128,256]{2,1,0:T(8,128)(2,1)S(1)}, bf16[4,128,256]{2,1,0:T(8,128)(2,1)S(1)}, u32[]{:S(2)}, u32[]{:S(2)}) %collective-permute-start.32) | collective-permute-done | bytes 262176 | tf_op jit(solution)/shard_map/ppermute | solution.py:50
  105.9 2.6 %backward_cell.1 = (bf16[4,128,256]{2,1,0:T(8,128)(2,1)S(1)}, bf16[4,128,256]{2,1,0:T(8,128)(2,1)S(1)}, bf16[4,128,256]{2,1,0:T(8,128)(2,1)S(1)}, bf16[4,128,256...) custom-call(s32[128]{0:T(128)S(1)} %get-tuple-element.115.out_ref, ...), custom_call_target="tpu_custom_call" | custom-call | flops 1073741824 | bytes 10485760 | tf_op jit(solution)/shard_map/backward_cell/pallas_call | solution.py:120
  117.4 3.7 %collective-permute-start.50 = (f32[128,256]{1,0:T(8,128)S(1)}, f32[128,256]{1,0:T(8,128)S(1)}, u32[]{:S(2)}, u32[]{:S(2)}) collective-permute-start(f32[128,256]{1,0:T(8,128)S(1)} %add.180), channel_id=1, source_target_pairs={{0,8},{1,9},{2,10},{3,11},{4,12},{5,13},{6,14},{7,15},{8,0},{9,1},... | collective-permute-start | bytes 393224 | tf_op jit(solution)/shard_map/ppermute | solution.py:223
  121.2 2.9 %collective-permute-done.50 = f32[128,256]{1,0:T(8,128)S(1)} collective-permute-done((f32[128,256]{1,0:T(8,128)S(1)}, f32[128,256]{1,0:T(8,128)S(1)}, u32[]{:S(2)}, u32[]{:S(2)}) %collective-permute-start.50) | collective-permute-done | bytes 131104 | tf_op jit(solution)/shard_map/ppermute | solution.py:223
  124.0 2.8 %collective-permute-start.45 = (bf16[4,128,256]{2,1,0:T(8,128)(2,1)S(1)}, bf16[4,128,256]{2,1,0:T(8,128)(2,1)S(1)}, u32[]{:S(2)}, u32[]{:S(2)}) collective-permute-start(bf16[4,128,256]{2,1,0:T(8,128)(2,1)S(1)} %add_convert_fusion.2), channel_id=1, source_target_pairs={{0,64},{16,80},{32,96},{48,112},{64,0},{80,16},{96,32},{112,48},{1... | collective-permute-start | bytes 786440 | tf_op jit(solution)/shard_map/ppermute | solution.py:42
  129.1 3.4 %collective-permute-done.45 = bf16[4,128,256]{2,1,0:T(8,128)(2,1)S(1)} collective-permute-done((bf16[4,128,256]{2,1,0:T(8,128)(2,1)S(1)}, bf16[4,128,256]{2,1,0:T(8,128)(2,1)S(1)}, u32[]{:S(2)}, u32[]{:S(2)}) %collective-permute-start.45) | collective-permute-done | bytes 262176 | tf_op jit(solution)/shard_map/ppermute | solution.py:42
  132.4 3.4 %collective-permute-done.48 = bf16[4,128,256]{2,1,0:T(8,128)(2,1)S(1)} collective-permute-done((bf16[4,128,256]{2,1,0:T(8,128)(2,1)S(1)}, bf16[4,128,256]{2,1,0:T(8,128)(2,1)S(1)}, u32[]{:S(2)}, u32[]{:S(2)}) %collective-permute-start.48) | collective-permute-done | bytes 262176 | tf_op jit(solution)/shard_map/ppermute | solution.py:46
  (116 shorter events, 54.9 us)
Async XLA Ops:
  0.6 10.2 %collective-permute-start = (bf16[4,128,256]{2,1,0:T(8,128)(2,1)}, bf16[4,128,256]{2,1,0:T(8,128)(2,1)S(1)}, u32[]{:S(2)}, u32[]{:S(2)}) collective-permute-start(bf16[4,128,256]{2,1,0:T(8,128)(2,1)} %bitcast.40), channel_id=1, source_target_pairs={{0,16},{16,0},{32,48},{48,32},{64,80},{80,64},{96,112},{112,96},{1... | collective-permute-start | bytes 786440 | tf_op jit(solution)/shard_map/ppermute | solution.py:46
  2.4 11.8 %collective-permute-start.3 = (bf16[4,128,256]{2,1,0:T(8,128)(2,1)}, bf16[4,128,256]{2,1,0:T(8,128)(2,1)S(1)}, u32[]{:S(2)}, u32[]{:S(2)}) collective-permute-start(bf16[4,128,256]{2,1,0:T(8,128)(2,1)} %bitcast.41), channel_id=1, source_target_pairs={{0,64},{16,80},{32,96},{48,112},{64,0},{80,16},{96,32},{112,48},{1... | collective-permute-start | bytes 786440 | tf_op jit(solution)/shard_map/ppermute | solution.py:42
  6.2 12.7 %collective-permute-start.5 = (bf16[4,128,256]{2,1,0:T(8,128)(2,1)}, bf16[4,128,256]{2,1,0:T(8,128)(2,1)S(1)}, u32[]{:S(2)}, u32[]{:S(2)}) collective-permute-start(bf16[4,128,256]{2,1,0:T(8,128)(2,1)} %bitcast.42), channel_id=1, source_target_pairs={{0,32},{16,48},{32,64},{48,80},{64,96},{80,112},{96,0},{112,16},{1... | collective-permute-start | bytes 786440 | tf_op jit(solution)/shard_map/ppermute | solution.py:42
  7.3 13.1 %collective-permute-start.1 = (bf16[4,128,256]{2,1,0:T(8,128)(2,1)}, bf16[4,128,256]{2,1,0:T(8,128)(2,1)S(1)}, u32[]{:S(2)}, u32[]{:S(2)}) collective-permute-start(bf16[4,128,256]{2,1,0:T(8,128)(2,1)} %bitcast.43), channel_id=1, source_target_pairs={{0,96},{16,112},{32,0},{48,16},{64,32},{80,48},{96,64},{112,80},{1... | collective-permute-start | bytes 786440 | tf_op jit(solution)/shard_map/ppermute | solution.py:42
  10.9 12.9 %collective-permute-start.6 = (bf16[4,128,256]{2,1,0:T(8,128)(2,1)S(1)}, bf16[4,128,256]{2,1,0:T(8,128)(2,1)S(1)}, u32[]{:S(2)}, u32[]{:S(2)}) collective-permute-start(bf16[4,128,256]{2,1,0:T(8,128)(2,1)S(1)} %collective-permute-done.rest_1_), channel_id=1, source_target_pairs={{0,32},{16,48},{32,64},{48,80},{64,96},{80,112},{96,0},{112,16},{1... | collective-permute-start | bytes 786440 | tf_op jit(solution)/shard_map/ppermute | solution.py:42
  11.0 13.5 %collective-permute-start.2 = (bf16[4,128,256]{2,1,0:T(8,128)(2,1)S(1)}, bf16[4,128,256]{2,1,0:T(8,128)(2,1)S(1)}, u32[]{:S(2)}, u32[]{:S(2)}) collective-permute-start(bf16[4,128,256]{2,1,0:T(8,128)(2,1)S(1)} %collective-permute-done.rest_1_), channel_id=1, source_target_pairs={{0,96},{16,112},{32,0},{48,16},{64,32},{80,48},{96,64},{112,80},{1... | collective-permute-start | bytes 786440 | tf_op jit(solution)/shard_map/ppermute | solution.py:42
  31.3 10.2 %collective-permute-start.12 = (bf16[4,128,256]{2,1,0:T(8,128)(2,1)S(1)}, bf16[4,128,256]{2,1,0:T(8,128)(2,1)S(1)}, u32[]{:S(2)}, u32[]{:S(2)}) collective-permute-start(bf16[4,128,256]{2,1,0:T(8,128)(2,1)S(1)} %get-tuple-element.63), channel_id=1, source_target_pairs={{0,1},{1,0},{2,3},{3,2},{4,5},{5,4},{6,7},{7,6},{8,9},{9,8},{10,11... | collective-permute-start | bytes 786440 | tf_op jit(solution)/shard_map/ppermute | solution.py:58
  31.7 14.4 %collective-permute-start.16 = (bf16[4,128,256]{2,1,0:T(8,128)(2,1)S(1)}, bf16[4,128,256]{2,1,0:T(8,128)(2,1)S(1)}, u32[]{:S(2)}, u32[]{:S(2)}) collective-permute-start(bf16[4,128,256]{2,1,0:T(8,128)(2,1)S(1)} %get-tuple-element.67), channel_id=1, source_target_pairs={{0,1},{1,0},{2,3},{3,2},{4,5},{5,4},{6,7},{7,6},{8,9},{9,8},{10,11... | collective-permute-start | bytes 786440 | tf_op jit(solution)/shard_map/ppermute | solution.py:58
  34.1 10.4 %collective-permute-start.14 = (bf16[4,128,256]{2,1,0:T(8,128)(2,1)S(1)}, bf16[4,128,256]{2,1,0:T(8,128)(2,1)S(1)}, u32[]{:S(2)}, u32[]{:S(2)}) collective-permute-start(bf16[4,128,256]{2,1,0:T(8,128)(2,1)S(1)} %add_convert_fusion.7), channel_id=1, source_target_pairs={{0,2},{1,3},{2,0},{3,1},{4,6},{5,7},{6,4},{7,5},{8,10},{9,11},{10,... | collective-permute-start | bytes 786440 | tf_op jit(solution)/shard_map/ppermute | solution.py:54
  39.6 10.0 %collective-permute-start.20 = (bf16[4,128,256]{2,1,0:T(8,128)(2,1)S(1)}, bf16[4,128,256]{2,1,0:T(8,128)(2,1)S(1)}, u32[]{:S(2)}, u32[]{:S(2)}) collective-permute-start(bf16[4,128,256]{2,1,0:T(8,128)(2,1)S(1)} %add_convert_fusion.4), channel_id=1, source_target_pairs={{0,12},{1,13},{2,14},{3,15},{4,0},{5,1},{6,2},{7,3},{8,4},{9,5},{1... | collective-permute-start | bytes 786440 | tf_op jit(solution)/shard_map/ppermute | solution.py:50
  41.5 11.2 %collective-permute-start.7 = (bf16[4,128,256]{2,1,0:T(8,128)(2,1)S(1)}, bf16[4,128,256]{2,1,0:T(8,128)(2,1)S(1)}, u32[]{:S(2)}, u32[]{:S(2)}) collective-permute-start(bf16[4,128,256]{2,1,0:T(8,128)(2,1)S(1)} %get-tuple-element.57), channel_id=1, source_target_pairs={{0,1},{1,0},{2,3},{3,2},{4,5},{5,4},{6,7},{7,6},{8,9},{9,8},{10,11... | collective-permute-start | bytes 786440 | tf_op jit(solution)/shard_map/ppermute | solution.py:58
  44.5 10.2 %collective-permute-start.9 = (bf16[4,128,256]{2,1,0:T(8,128)(2,1)S(1)}, bf16[4,128,256]{2,1,0:T(8,128)(2,1)S(1)}, u32[]{:S(2)}, u32[]{:S(2)}) collective-permute-start(bf16[4,128,256]{2,1,0:T(8,128)(2,1)S(1)} %add_convert_fusion.9), channel_id=1, source_target_pairs={{0,4},{1,5},{2,6},{3,7},{4,8},{5,9},{6,10},{7,11},{8,12},{9,13},{1... | collective-permute-start | bytes 786440 | tf_op jit(solution)/shard_map/ppermute | solution.py:50
  46.1 12.5 %collective-permute-start.11 = (bf16[4,128,256]{2,1,0:T(8,128)(2,1)S(1)}, bf16[4,128,256]{2,1,0:T(8,128)(2,1)S(1)}, u32[]{:S(2)}, u32[]{:S(2)}) collective-permute-start(bf16[4,128,256]{2,1,0:T(8,128)(2,1)S(1)} %add_convert_fusion.8), channel_id=1, source_target_pairs={{0,12},{1,13},{2,14},{3,15},{4,0},{5,1},{6,2},{7,3},{8,4},{9,5},{1... | collective-permute-start | bytes 786440 | tf_op jit(solution)/shard_map/ppermute | solution.py:50
  47.9 11.8 %collective-permute-start.15 = (bf16[4,128,256]{2,1,0:T(8,128)(2,1)S(1)}, bf16[4,128,256]{2,1,0:T(8,128)(2,1)S(1)}, u32[]{:S(2)}, u32[]{:S(2)}) collective-permute-start(bf16[4,128,256]{2,1,0:T(8,128)(2,1)S(1)} %add_convert_fusion.6), channel_id=1, source_target_pairs={{0,8},{1,9},{2,10},{3,11},{4,12},{5,13},{6,14},{7,15},{8,0},{9,1},... | collective-permute-start | bytes 786440 | tf_op jit(solution)/shard_map/ppermute | solution.py:50
  73.2 15.0 %collective-permute-start.29 = (bf16[4,128,256]{2,1,0:T(8,128)(2,1)S(1)}, bf16[4,128,256]{2,1,0:T(8,128)(2,1)S(1)}, u32[]{:S(2)}, u32[]{:S(2)}) collective-permute-start(bf16[4,128,256]{2,1,0:T(8,128)(2,1)S(1)} %get-tuple-element.76.rest_0_), channel_id=1, source_target_pairs={{0,8},{1,9},{2,10},{3,11},{4,12},{5,13},{6,14},{7,15},{8,0},{9,1},... | collective-permute-start | bytes 786440 | tf_op jit(solution)/shard_map/ppermute | solution.py:50
  75.9 12.3 %collective-permute-start.27 = (bf16[4,128,256]{2,1,0:T(8,128)(2,1)S(1)}, bf16[4,128,256]{2,1,0:T(8,128)(2,1)S(1)}, u32[]{:S(2)}, u32[]{:S(2)}) collective-permute-start(bf16[4,128,256]{2,1,0:T(8,128)(2,1)S(1)} %get-tuple-element.76.rest_0_), channel_id=1, source_target_pairs={{0,12},{1,13},{2,14},{3,15},{4,0},{5,1},{6,2},{7,3},{8,4},{9,5},{1... | collective-permute-start | bytes 786440 | tf_op jit(solution)/shard_map/ppermute | solution.py:50
  75.9 15.2 %collective-permute-start.26 = (bf16[4,128,256]{2,1,0:T(8,128)(2,1)S(1)}, bf16[4,128,256]{2,1,0:T(8,128)(2,1)S(1)}, u32[]{:S(2)}, u32[]{:S(2)}) collective-permute-start(bf16[4,128,256]{2,1,0:T(8,128)(2,1)S(1)} %get-tuple-element.76.rest_0_), channel_id=1, source_target_pairs={{0,2},{1,3},{2,0},{3,1},{4,6},{5,7},{6,4},{7,5},{8,10},{9,11},{10,... | collective-permute-start | bytes 786440 | tf_op jit(solution)/shard_map/ppermute | solution.py:54
  78.9 13.1 %collective-permute-start.25 = (f32[128,256]{1,0:T(8,128)S(1)}, f32[128,256]{1,0:T(8,128)S(1)}, u32[]{:S(2)}, u32[]{:S(2)}) collective-permute-start(f32[128,256]{1,0:T(8,128)S(1)} %add.170), channel_id=1, source_target_pairs={{0,16},{16,0},{32,48},{48,32},{64,80},{80,64},{96,112},{112,96},{1... | collective-permute-start | bytes 393224 | tf_op jit(solution)/shard_map/ppermute | solution.py:223
  81.8 12.6 %collective-permute-start.39 = (bf16[4,128,256]{2,1,0:T(8,128)(2,1)S(1)}, bf16[4,128,256]{2,1,0:T(8,128)(2,1)S(1)}, u32[]{:S(2)}, u32[]{:S(2)}) collective-permute-start(bf16[4,128,256]{2,1,0:T(8,128)(2,1)S(1)} %collective-permute-done.31.rest_6_), channel_id=1, source_target_pairs={{0,1},{1,0},{2,3},{3,2},{4,5},{5,4},{6,7},{7,6},{8,9},{9,8},{10,11... | collective-permute-start | bytes 786440 | tf_op jit(solution)/shard_map/ppermute | solution.py:58
  88.2 10.2 %collective-permute-start.30 = (bf16[4,128,256]{2,1,0:T(8,128)(2,1)S(1)}, bf16[4,128,256]{2,1,0:T(8,128)(2,1)S(1)}, u32[]{:S(2)}, u32[]{:S(2)}) collective-permute-start(bf16[4,128,256]{2,1,0:T(8,128)(2,1)S(1)} %collective-permute-done.29.rest_4_), channel_id=1, source_target_pairs={{0,2},{1,3},{2,0},{3,1},{4,6},{5,7},{6,4},{7,5},{8,10},{9,11},{10,... | collective-permute-start | bytes 786440 | tf_op jit(solution)/shard_map/ppermute | solution.py:54
  110.5 16.4 %collective-permute-start.46 = (bf16[4,128,256]{2,1,0:T(8,128)(2,1)S(1)}, bf16[4,128,256]{2,1,0:T(8,128)(2,1)S(1)}, u32[]{:S(2)}, u32[]{:S(2)}) collective-permute-start(bf16[4,128,256]{2,1,0:T(8,128)(2,1)S(1)} %get-tuple-element.106), channel_id=1, source_target_pairs={{0,32},{16,48},{32,64},{48,80},{64,96},{80,112},{96,0},{112,16},{1... | collective-permute-start | bytes 786440 | tf_op jit(solution)/shard_map/ppermute | solution.py:42
  112.0 15.0 %collective-permute-start.47 = (bf16[4,128,256]{2,1,0:T(8,128)(2,1)S(1)}, bf16[4,128,256]{2,1,0:T(8,128)(2,1)S(1)}, u32[]{:S(2)}, u32[]{:S(2)}) collective-permute-start(bf16[4,128,256]{2,1,0:T(8,128)(2,1)S(1)} %get-tuple-element.107), channel_id=1, source_target_pairs={{0,96},{16,112},{32,0},{48,16},{64,32},{80,48},{96,64},{112,80},{1... | collective-permute-start | bytes 786440 | tf_op jit(solution)/shard_map/ppermute | solution.py:42
  113.8 15.3 %collective-permute-start.42 = (bf16[4,128,256]{2,1,0:T(8,128)(2,1)S(1)}, bf16[4,128,256]{2,1,0:T(8,128)(2,1)S(1)}, u32[]{:S(2)}, u32[]{:S(2)}) collective-permute-start(bf16[4,128,256]{2,1,0:T(8,128)(2,1)S(1)} %get-tuple-element.101), channel_id=1, source_target_pairs={{0,32},{16,48},{32,64},{48,80},{64,96},{80,112},{96,0},{112,16},{1... | collective-permute-start | bytes 786440 | tf_op jit(solution)/shard_map/ppermute | solution.py:42
  115.4 13.7 %collective-permute-start.43 = (bf16[4,128,256]{2,1,0:T(8,128)(2,1)S(1)}, bf16[4,128,256]{2,1,0:T(8,128)(2,1)S(1)}, u32[]{:S(2)}, u32[]{:S(2)}) collective-permute-start(bf16[4,128,256]{2,1,0:T(8,128)(2,1)S(1)} %get-tuple-element.102), channel_id=1, source_target_pairs={{0,96},{16,112},{32,0},{48,16},{64,32},{80,48},{96,64},{112,80},{1... | collective-permute-start | bytes 786440 | tf_op jit(solution)/shard_map/ppermute | solution.py:42
  (33 other events, 230.8 us)

commit v3 on v2

v3 whole, which is shorter than its diff:
```python
import functools
import math

import jax
import jax.numpy as jnp
from jax import lax
from jax.experimental import pallas as pl
from jax.experimental.pallas import tpu as pltpu
from jax.sharding import PartitionSpec as P

BLK = 128
WIDTH = 256
CAP = 128
UNROLL = 16
CHUNKS = 4
BF16 = jnp.bfloat16
F32 = jnp.float32

NZ, NX = 4, 4


def z_perm(step):
    return [(z * 2 + yl, (z + step) % NZ * 2 + yl) for z in range(NZ) for yl in range(2)]


def yl_perm():
    return [(r, r ^ 1) for r in range(2 * NZ)]


def x_perm(step):
    return [(x * 4 + q, (x + step) % NX * 4 + q) for x in range(NX) for q in range(4)]


def yh_perm():
    return [(c, c ^ 2) for c in range(4 * NX)]


def core_perm():
    return [(c, c ^ 1) for c in range(4 * NX)]


def z_send(v, step):
    return lax.ppermute(v, "row", z_perm(step))


def yl_swap(v):
    return lax.ppermute(v, "row", yl_perm())


def x_send(v, step):
    return lax.ppermute(v, "col", x_perm(step))


def yh_swap(v):
    return lax.ppermute(v, "col", yh_perm())


def core_swap(v):
    return lax.ppermute(v, "col", core_perm())


def add(*terms):
    total = terms[0].astype(F32)
    for term in terms[1:]:
        total = total + term.astype(F32)
    return total.astype(BF16)


def tile_copies(tiles_hbm, tiles, sems):
    size = CAP // CHUNKS
    return [
        pltpu.make_async_copy(
            tiles_hbm.at[pl.ds(c * size, size)], tiles.at[pl.ds(c * size, size)], sems.at[c]
        )
        for c in range(CHUNKS)
    ]


def cell_kernel(transposed, n_in, n_out, out_ref, in_ref, cnt_ref, tiles_hbm, *rest):
    pieces = rest[:n_in]
    outs = rest[n_in : n_in + n_out]
    tiles, blocks, acc, tile_sems, piece_sems = rest[n_in + n_out :]
    copies = [
        pltpu.make_async_copy(piece, blocks.at[pl.ds(4 * i, 4)], piece_sems.at[i])
        for i, piece in enumerate(pieces)
    ]
    loads = tile_copies(tiles_hbm, tiles, tile_sems)
    for copy in copies[:1] + loads[:1] + copies[1:] + loads[1:]:
        copy.start()

    def clear(i, carry):
        acc[i] = jnp.zeros(acc.shape[1:], acc.dtype)
        return carry

    lax.fori_loop(0, acc.shape[0] - 1, clear, 0)
    for copy in copies:
        copy.wait()
    dims = (((0,), (0,)), ((), ())) if transposed else (((1,), (0,)), ((), ()))

    def group(i, carry):
        first = i * UNROLL
        products = [
            lax.dot_general(
                tiles[first + u], blocks[in_ref[first + u]], dims, preferred_element_type=F32
            )
            for u in range(UNROLL)
        ]
        for u in range(UNROLL):
            slot = out_ref[first + u]
            acc[slot] += products[u]
        return carry

    groups = (cnt_ref[0] + UNROLL - 1) // UNROLL
    size = CAP // CHUNKS // UNROLL
    for c, load in enumerate(loads):
        load.wait()
        lax.fori_loop(c * size, jnp.clip(groups, c * size, (c + 1) * size), group, 0)
    for o, out in enumerate(outs):
        def store(i, carry, out=out, o=o):
            out[i] = acc[4 * o + i].astype(BF16)
            return carry

        lax.fori_loop(0, 4, store, 0)


def cell_product(name, transposed, out_slot, in_slot, count, tiles, pieces, n_out):
    live = jnp.arange(CAP, dtype=jnp.int32) < count[0]
    out_slot = jnp.where(live, out_slot, 4 * n_out)
    in_slot = jnp.where(live, in_slot, 0)
    any_spec = pl.BlockSpec(memory_space=pl.ANY)
    vmem_spec = pl.BlockSpec(memory_space=pltpu.VMEM)
    return pl.pallas_call(
        functools.partial(cell_kernel, transposed, len(pieces), n_out),
        grid_spec=pltpu.PrefetchScalarGridSpec(
            num_scalar_prefetch=3,
            grid=(),
            in_specs=[any_spec] * (1 + len(pieces)),
            out_specs=[vmem_spec] * n_out,
            scratch_shapes=[
                pltpu.VMEM((CAP, BLK, BLK), BF16),
                pltpu.VMEM((4 * len(pieces), BLK, WIDTH), BF16),
                pltpu.VMEM((4 * n_out + 1, BLK, WIDTH), F32),
                pltpu.SemaphoreType.DMA((CHUNKS,)),
                pltpu.SemaphoreType.DMA((len(pieces),)),
            ],
        ),
        out_shape=[jax.ShapeDtypeStruct((4, BLK, WIDTH), BF16)] * n_out,
        compiler_params=pltpu.CompilerParams(vmem_limit_bytes=16 * 1024 * 1024),
        cost_estimate=pl.CostEstimate(
            flops=2 * CAP * BLK * BLK * WIDTH,
            bytes_accessed=2 * CAP * BLK * BLK + 8 * (len(pieces) + n_out) * BLK * WIDTH,
            transcendentals=0,
        ),
        name=name,
    )(out_slot, in_slot, count, pltpu.with_memory_space_constraint(tiles, pltpu.HBM), *pieces)


def dense_kernel(scale, n_terms, *refs):
    terms, (w_ref, cot_ref, out_ref, grad_ref, rider_ref) = refs[:n_terms], refs[n_terms:]
    total = terms[0][...].astype(F32)
    for term in terms[1:]:
        total = total + term[...].astype(F32)
    w = w_ref[...]
    agg = total.astype(BF16).reshape(cot_ref.shape)
    pre = jnp.dot(agg, w, preferred_element_type=F32)
    sig = jax.nn.sigmoid(pre)
    out_ref[...] = (pre * sig).astype(BF16)
    grad_pre = (cot_ref[...].astype(F32) * sig * (1.0 + pre * (1.0 - sig))).astype(BF16)
    grad_agg = lax.dot_general(
        grad_pre, w, (((1,), (1,)), ((), ())), preferred_element_type=F32
    ).astype(BF16)
    grad_agg = grad_agg.reshape(grad_ref.shape)
    grad_ref[...] = grad_agg
    rider_ref[pl.ds(0, 4)] = grad_agg
    weight_grad = lax.dot_general(
        agg, grad_pre, (((0,), (0,)), ((), ())), preferred_element_type=F32
    )
    rider_ref[pl.ds(4, 2)] = (weight_grad * scale).astype(BF16).reshape(2, BLK, WIDTH)


def dense(scale, terms, weight, cotangent):
    vmem_spec = pl.BlockSpec(memory_space=pltpu.VMEM)
    nodes = cotangent.shape[0]
    return pl.pallas_call(
        functools.partial(dense_kernel, scale, len(terms)),
        in_specs=[vmem_spec] * (len(terms) + 2),
        out_specs=[vmem_spec] * 3,
        out_shape=[
            jax.ShapeDtypeStruct((nodes, WIDTH), BF16),
            jax.ShapeDtypeStruct((nodes // BLK, BLK, WIDTH), BF16),
            jax.ShapeDtypeStruct((nodes // BLK + 2, BLK, WIDTH), BF16),
        ],
        compiler_params=pltpu.CompilerParams(vmem_limit_bytes=24 * 1024 * 1024),
        cost_estimate=pl.CostEstimate(
            flops=6 * nodes * WIDTH * WIDTH,
            bytes_accessed=8 * nodes * WIDTH,
            transcendentals=nodes * WIDTH,
        ),
        name="dense",
    )(*terms, weight, cotangent)


def after(value, *earlier):
    return lax.optimization_barrier((value, *earlier))[0]


def ring_sum(own, send):
    across, up, down = send(own, 2), send(own, 1), send(own, -1)
    return (own.astype(F32) + across.astype(F32)) + (up.astype(F32) + down.astype(F32))


def shards(tile_values, tile_rows, tile_cols, tile_counts, features, weight, cotangent):
    row, col = lax.axis_index("row"), lax.axis_index("col")
    z, yl = row // 2, row % 2
    x, yh, core = col // 4, col // 2 % 2, col % 2
    tiles = tile_values[0, 0]
    t_row, t_col = tile_rows[0, 0], tile_cols[0, 0]
    count = tile_counts[0]

    own, j = t_row // 4, t_row % 4
    dx, dyh, dk = (own // 4 - x) % 4, (own // 2 % 2) ^ yh, (own % 2) ^ core
    row_slot = dk * 32 + dx * 8 + dyh * 4 + j
    own, j = t_col // 4, t_col % 4
    dz, dyl = (own // 2 - z) % 4, (own % 2) ^ yl
    col_slot = dz * 8 + dyl * 4 + j

    own = features.reshape(4, BLK, WIDTH)
    far = yl_swap(own)
    across = z_send(own, 2)
    up, down = z_send(own, -1), z_send(own, 1)
    far_up, far_down = z_send(far, -1), z_send(far, 1)
    far_across = yl_swap(across)
    own = pltpu.with_memory_space_constraint(own, pltpu.HBM)
    pieces = [own, far, up, far_up, across, far_across, down, far_down]

    parts = cell_product("forward_cell", False, row_slot, col_slot, count, tiles, pieces, 16)
    mine = parts[:8]
    other = [None] * 8
    for i in (5, 3, 7):
        other[i] = core_swap(parts[8 + i])
    for i in (2, 6, 4, 1, 0):
        other[i] = core_swap(after(parts[8 + i], other[7]))
    two = yh_swap(add(mine[5], other[5]))
    up, down = x_send(add(mine[3], other[3]), 1), x_send(add(mine[7], other[7]), -1)
    own_up, own_down = x_send(add(mine[2], other[2]), 1), x_send(add(mine[6], other[6]), -1)
    across = x_send(add(mine[4], other[4], two), 2)
    far = yh_swap(add(mine[1], other[1], up, down))
    terms = [mine[0], other[0], own_up, own_down, across, far]
    scale = 1.0 / math.sqrt(features.shape[0] * lax.axis_size("row") * lax.axis_size("col"))
    output, own, own_rider = dense(scale, terms, weight, cotangent)

    far_rider = yh_swap(own_rider)
    far = far_rider[:4]
    across = x_send(own, 2)
    up, down = x_send(own, -1), x_send(own, 1)
    far_up, far_down = x_send(far, -1), x_send(far, 1)
    far_across = yh_swap(across)
    pieces = [own, far, up, far_up, across, far_across, down, far_down]
    far_rider, *ready = lax.optimization_barrier((far_rider, *pieces))
    term = add(own_rider[4:], far_rider[4:])
    term = add(term, yl_swap(term))
    pieces = [*ready, *(core_swap(v) for v in ready)]
    term = add(term, core_swap(term))
    term = ring_sum(term, z_send).astype(BF16)
    back = cell_product("backward_cell", True, col_slot, row_slot, count, tiles, pieces, 8)
    two = yl_swap(back[5])
    up, down = z_send(back[3], 1), z_send(back[7], -1)
    own_up, own_down = z_send(back[2], 1), z_send(back[6], -1)
    across = z_send(add(back[4], two), 2)
    far = yl_swap(add(back[1], up, down))
    grad_features = add(back[0], own_up, own_down, across, far)
    weight_grad = ring_sum(after(term, up, down), x_send).reshape(WIDTH, WIDTH)
    return (output, grad_features.reshape(4 * BLK, WIDTH), weight_grad)


def solution(mesh):
    in_specs = (
        P("row", "col", None, None, None),
        P("row", "col", None),
        P("row", "col", None),
        P("row", "col"),
        P(("col", "row"), None),
        P(),
        P(("row", "col"), None),
    )
    out_specs = (P(("row", "col"), None), P(("col", "row"), None), P())
    return jax.shard_map(shards, mesh=mesh, in_specs=in_specs, out_specs=out_specs, check_vma=False)
```

time: 138 us -> 128 us (0.928)
  local copies, waits for them, and re-layouts: 5.35 us -> 0.03 us
  starting transfers between devices: 64 us -> 59.3 us
  Pallas kernels: 6.57 us -> 9.63 us
  waiting for transfers between devices: 56.1 us -> 54.3 us
    ppermute x6 -> x0, starting transfers between devices: 11.3 us -> none  [pair_sum(): lax.ppermute(v, axis, [(i, i ^ flip) for i in range(lax.axis_size(axis))])]
    ppermute x6 -> x0, waiting for transfers between devices: 9.47 us -> none  [pair_sum(): lax.ppermute(v, axis, [(i, i ^ flip) for i in range(lax.axis_size(axis))])]
    ppermute x10 -> x13, starting transfers between devices: 15.7 us -> 21.7 us  [x_send(): return lax.ppermute(v, 'col', x_perm(step))]
    unnamed x10 -> x4, local copies, waits for them, and re-layouts: 5.34 us -> 0.01 us
    ppermute x10 -> x13, waiting for transfers between devices: 13 us -> 17.1 us  [z_send(): return lax.ppermute(v, 'row', z_perm(step))]
    ppermute x18 -> x17, waiting for transfers between devices: 5.34 us -> 1.33 us  [core_swap(): return lax.ppermute(v, 'col', core_perm())]
    ppermute x10 -> x13, starting transfers between devices: 18.3 us -> 22.3 us  [z_send(): return lax.ppermute(v, 'row', z_perm(step))]
    ppermute x4, starting transfers between devices: 12.7 us -> 8.99 us  [yh_swap(): return lax.ppermute(v, 'col', yh_perm())]
  transfers between devices with their start and end apart: 52 -> 52, of which waited for: 27 -> 22; matrix products, arithmetic and copies ran while one was open for 2% -> 2% of each run, Pallas kernels for 2% -> 3%
where the time goes in v3:
time: 128 us
  starting transfers between devices  59.3 us (46%)
  waiting for transfers between devices  54.3 us (42%)
  Pallas kernels  9.63 us (8%)
  other arithmetic  3.27 us (3%)
  between operations  1.53 us (1%)
    ppermute x13, starting transfers between devices, z_send(): return lax.ppermute(v, 'row', z_perm(step))  22.3 us
    ppermute x13, starting transfers between devices, x_send(): return lax.ppermute(v, 'col', x_perm(step))  21.7 us
    ppermute x13, waiting for transfers between devices, x_send(): return lax.ppermute(v, 'col', x_perm(step))  19.2 us
    ppermute x13, waiting for transfers between devices, z_send(): return lax.ppermute(v, 'row', z_perm(step))  17.1 us
    ppermute x4, waiting for transfers between devices, yh_swap(): return lax.ppermute(v, 'col', yh_perm())  10.1 us
    ppermute x4, starting transfers between devices, yh_swap(): return lax.ppermute(v, 'col', yh_perm())  8.99 us
    pallas_call x2, Pallas kernels, cell_product(): pl.pallas_call(functools.partial(cell_kernel, transposed, len(pieces), n_...  8.52 us
    ppermute x5, waiting for transfers between devices, yl_swap(): return lax.ppermute(v, 'row', yl_perm())  6.64 us
  transfers between devices with their start and end apart: 52, of which 22 were waited for; matrix products, arithmetic and copies ran while one was open for 2% of the time, Pallas kernels for 3%

profile of v3, /device:TPU:0, one launch (start us, length us, event | category | flops | bytes accessed | tf_op | source)
XLA Modules:
  0.0 128.0 jit_solution(15759004812275881355)
XLA Ops:
  2.4 3.9 %collective-permute-start.3 = (bf16[4,128,256]{2,1,0:T(8,128)(2,1)}, bf16[4,128,256]{2,1,0:T(8,128)(2,1)S(1)}, u32[]{:S(2)}, u32[]{:S(2)}) collective-permute-start(bf16[4,128,256]{2,1,0:T(8,128)(2,1)} %bitcast.42), channel_id=1, source_target_pairs={{0,64},{16,80},{32,96},{48,112},{64,0},{80,16},{96,32},{112,48},{1... | collective-permute-start | bytes 786440 | tf_op jit(solution)/shard_map/ppermute | solution.py:43
  7.3 2.2 %collective-permute-start.1 = (bf16[4,128,256]{2,1,0:T(8,128)(2,1)}, bf16[4,128,256]{2,1,0:T(8,128)(2,1)S(1)}, u32[]{:S(2)}, u32[]{:S(2)}) collective-permute-start(bf16[4,128,256]{2,1,0:T(8,128)(2,1)} %bitcast.44), channel_id=1, source_target_pairs={{0,96},{16,112},{32,0},{48,16},{64,32},{80,48},{96,64},{112,80},{1... | collective-permute-start | bytes 786440 | tf_op jit(solution)/shard_map/ppermute | solution.py:43
  11.0 3.2 %collective-permute-start.2 = (bf16[4,128,256]{2,1,0:T(8,128)(2,1)S(1)}, bf16[4,128,256]{2,1,0:T(8,128)(2,1)S(1)}, u32[]{:S(2)}, u32[]{:S(2)}) collective-permute-start(bf16[4,128,256]{2,1,0:T(8,128)(2,1)S(1)} %collective-permute-done.rest_1_), channel_id=1, source_target_pairs={{0,96},{16,112},{32,0},{48,16},{64,32},{80,48},{96,64},{112,80},{1... | collective-permute-start | bytes 786440 | tf_op jit(solution)/shard_map/ppermute | solution.py:43
  14.7 4.3 %collective-permute-done.5.rest_6_ = bf16[4,128,256]{2,1,0:T(8,128)(2,1)S(1)} collective-permute-done((bf16[4,128,256]{2,1,0:T(8,128)(2,1)}, bf16[4,128,256]{2,1,0:T(8,128)(2,1)S(1)}, u32[]{:S(2)}, u32[]{:S(2)}) %collective-permute-start.5) | collective-permute-done | bytes 262176 | tf_op jit(solution)/shard_map/ppermute | solution.py:43
  20.6 3.2 %collective-permute-done.6.rest_7_ = bf16[4,128,256]{2,1,0:T(8,128)(2,1)S(1)} collective-permute-done((bf16[4,128,256]{2,1,0:T(8,128)(2,1)S(1)}, bf16[4,128,256]{2,1,0:T(8,128)(2,1)S(1)}, u32[]{:S(2)}, u32[]{:S(2)}) %collective-permute-start.6) | collective-permute-done | bytes 262176 | tf_op jit(solution)/shard_map/ppermute | solution.py:43
  24.5 4.3 %forward_cell.1 = (bf16[4,128,256]{2,1,0:T(8,128)(2,1)S(1)}, bf16[4,128,256]{2,1,0:T(8,128)(2,1)S(1)}, bf16[4,128,256]{2,1,0:T(8,128)(2,1)S(1)}, bf16[4,128,256]...) custom-call(s32[128]{0:T(128)S(1)} %fusion.19.out_ref, ...), custom_call_target="tpu_custom_call" | custom-call | flops 1073741824 | bytes 10485760 | tf_op jit(solution)/shard_map/forward_cell/pallas_call | solution.py:132
  31.7 2.4 %collective-permute-start.20 = (bf16[4,128,256]{2,1,0:T(8,128)(2,1)S(1)}, bf16[4,128,256]{2,1,0:T(8,128)(2,1)S(1)}, u32[]{:S(2)}, u32[]{:S(2)}) collective-permute-start(bf16[4,128,256]{2,1,0:T(8,128)(2,1)S(1)} %add_convert_fusion.4), channel_id=1, source_target_pairs={{0,12},{1,13},{2,14},{3,15},{4,0},{5,1},{6,2},{7,3},{8,4},{9,5},{1... | collective-permute-start | bytes 786440 | tf_op jit(solution)/shard_map/ppermute | solution.py:51
  34.2 2.6 %collective-permute-start.15 = (bf16[4,128,256]{2,1,0:T(8,128)(2,1)S(1)}, bf16[4,128,256]{2,1,0:T(8,128)(2,1)S(1)}, u32[]{:S(2)}, u32[]{:S(2)}) collective-permute-start(bf16[4,128,256]{2,1,0:T(8,128)(2,1)S(1)} %add_convert_fusion.7), channel_id=1, source_target_pairs={{0,2},{1,3},{2,0},{3,1},{4,6},{5,7},{6,4},{7,5},{8,10},{9,11},{10,... | collective-permute-start | bytes 786440 | tf_op jit(solution)/shard_map/ppermute | solution.py:55
  38.5 5.4 %collective-permute-done.15 = bf16[4,128,256]{2,1,0:T(8,128)(2,1)S(1)} collective-permute-done((bf16[4,128,256]{2,1,0:T(8,128)(2,1)S(1)}, bf16[4,128,256]{2,1,0:T(8,128)(2,1)S(1)}, u32[]{:S(2)}, u32[]{:S(2)}) %collective-permute-start.15) | collective-permute-done | bytes 262176 | tf_op jit(solution)/shard_map/ppermute | solution.py:55
  44.9 2.4 %collective-permute-start.12 = (bf16[4,128,256]{2,1,0:T(8,128)(2,1)S(1)}, bf16[4,128,256]{2,1,0:T(8,128)(2,1)S(1)}, u32[]{:S(2)}, u32[]{:S(2)}) collective-permute-start(bf16[4,128,256]{2,1,0:T(8,128)(2,1)S(1)} %add_convert_fusion.8), channel_id=1, source_target_pairs={{0,12},{1,13},{2,14},{3,15},{4,0},{5,1},{6,2},{7,3},{8,4},{9,5},{1... | collective-permute-start | bytes 786440 | tf_op jit(solution)/shard_map/ppermute | solution.py:51
  49.0 3.2 %collective-permute-start.21 = (bf16[4,128,256]{2,1,0:T(8,128)(2,1)S(1)}, bf16[4,128,256]{2,1,0:T(8,128)(2,1)S(1)}, u32[]{:S(2)}, u32[]{:S(2)}) collective-permute-start(bf16[4,128,256]{2,1,0:T(8,128)(2,1)S(1)} %add_convert_fusion.3), channel_id=1, source_target_pairs={{0,2},{1,3},{2,0},{3,1},{4,6},{5,7},{6,4},{7,5},{8,10},{9,11},{10,... | collective-permute-start | bytes 786440 | tf_op jit(solution)/shard_map/ppermute | solution.py:55
  53.2 4.2 %collective-permute-done.12.refs_3_ = bf16[4,128,256]{2,1,0:T(8,128)(2,1)S(1)} collective-permute-done((bf16[4,128,256]{2,1,0:T(8,128)(2,1)S(1)}, bf16[4,128,256]{2,1,0:T(8,128)(2,1)S(1)}, u32[]{:S(2)}, u32[]{:S(2)}) %collective-permute-start.12) | collective-permute-done | bytes 262176 | tf_op jit(solution)/shard_map/ppermute | solution.py:51
  60.2 2.9 %collective-permute-start.22 = (bf16[6,128,256]{2,1,0:T(8,128)(2,1)S(1)}, bf16[6,128,256]{2,1,0:T(8,128)(2,1)S(1)}, u32[]{:S(2)}, u32[]{:S(2)}) collective-permute-start(bf16[6,128,256]{2,1,0:T(8,128)(2,1)S(1)} %get-tuple-element.67), channel_id=1, source_target_pairs={{0,2},{1,3},{2,0},{3,1},{4,6},{5,7},{6,4},{7,5},{8,10},{9,11},{10,... | collective-permute-start | bytes 1179656 | tf_op jit(solution)/shard_map/ppermute | solution.py:55
  67.1 6.7 %collective-permute-done.25.rest_4_ = bf16[4,128,256]{2,1,0:T(8,128)(2,1)S(1)} collective-permute-done((bf16[4,128,256]{2,1,0:T(8,128)(2,1)S(1)}, bf16[4,128,256]{2,1,0:T(8,128)(2,1)S(1)}, u32[]{:S(2)}, u32[]{:S(2)}) %collective-permute-start.25) | collective-permute-done | bytes 262176 | tf_op jit(solution)/shard_map/ppermute | solution.py:51
  78.2 4.7 %collective-permute-done.26.rest_5_ = bf16[4,128,256]{2,1,0:T(8,128)(2,1)S(1)} collective-permute-done((bf16[4,128,256]{2,1,0:T(8,128)(2,1)S(1)}, bf16[4,128,256]{2,1,0:T(8,128)(2,1)S(1)}, u32[]{:S(2)}, u32[]{:S(2)}) %collective-permute-start.26) | collective-permute-done | bytes 262176 | tf_op jit(solution)/shard_map/ppermute | solution.py:55
  83.6 4.3 %collective-permute-done.44 = bf16[2,128,256]{2,1,0:T(8,128)(2,1)S(1)} collective-permute-done((bf16[2,128,256]{2,1,0:T(8,128)(2,1)S(1)}, bf16[2,128,256]{2,1,0:T(8,128)(2,1)S(1)}, u32[]{:S(2)}, u32[]{:S(2)}) %collective-permute-start.44) | collective-permute-done | bytes 131104 | tf_op jit(solution)/shard_map/ppermute | solution.py:47
  89.8 3.5 %collective-permute-start.48 = (bf16[2,128,256]{2,1,0:T(8,128)(2,1)S(1)}, bf16[2,128,256]{2,1,0:T(8,128)(2,1)S(1)}, u32[]{:S(2)}, u32[]{:S(2)}) collective-permute-start(bf16[2,128,256]{2,1,0:T(8,128)(2,1)S(1)} %add_convert_fusion.11), channel_id=1, source_target_pairs={{0,96},{16,112},{32,0},{48,16},{64,32},{80,48},{96,64},{112,80},{1... | collective-permute-start | bytes 393224 | tf_op jit(solution)/shard_map/ppermute | solution.py:43
  95.1 4.2 %backward_cell.1 = (bf16[4,128,256]{2,1,0:T(8,128)(2,1)S(1)}, bf16[4,128,256]{2,1,0:T(8,128)(2,1)S(1)}, bf16[4,128,256]{2,1,0:T(8,128)(2,1)S(1)}, bf16[4,128,256...) custom-call(s32[128]{0:T(128)S(1)} %get-tuple-element.91.out_ref, ...), custom_call_target="tpu_custom_call" | custom-call | flops 1073741824 | bytes 10485760 | tf_op jit(solution)/shard_map/backward_cell/pallas_call | solution.py:132
  102.8 3.1 %collective-permute-start.38 = (bf16[4,128,256]{2,1,0:T(8,128)(2,1)S(1)}, bf16[4,128,256]{2,1,0:T(8,128)(2,1)S(1)}, u32[]{:S(2)}, u32[]{:S(2)}) collective-permute-start(bf16[4,128,256]{2,1,0:T(8,128)(2,1)S(1)} %get-tuple-element.79), channel_id=1, source_target_pairs={{0,96},{16,112},{32,0},{48,16},{64,32},{80,48},{96,64},{112,80},{1... | collective-permute-start | bytes 786440 | tf_op jit(solution)/shard_map/ppermute | solution.py:43
  105.9 3.9 %collective-permute-done.41 = bf16[4,128,256]{2,1,0:T(8,128)(2,1)S(1)} collective-permute-done((bf16[4,128,256]{2,1,0:T(8,128)(2,1)S(1)}, bf16[4,128,256]{2,1,0:T(8,128)(2,1)S(1)}, u32[]{:S(2)}, u32[]{:S(2)}) %collective-permute-start.41) | collective-permute-done | bytes 262176 | tf_op jit(solution)/shard_map/ppermute | solution.py:43
  110.0 3.2 %collective-permute-start.51 = (bf16[2,128,256]{2,1,0:T(8,128)(2,1)S(1)}, bf16[2,128,256]{2,1,0:T(8,128)(2,1)S(1)}, u32[]{:S(2)}, u32[]{:S(2)}) collective-permute-start(bf16[2,128,256]{2,1,0:T(8,128)(2,1)S(1)} %add_convert_fusion.10), channel_id=1, source_target_pairs={{0,12},{1,13},{2,14},{3,15},{4,0},{5,1},{6,2},{7,3},{8,4},{9,5},{1... | collective-permute-start | bytes 393224 | tf_op jit(solution)/shard_map/ppermute | solution.py:51
  113.3 2.4 %collective-permute-start.49 = (bf16[2,128,256]{2,1,0:T(8,128)(2,1)S(1)}, bf16[2,128,256]{2,1,0:T(8,128)(2,1)S(1)}, u32[]{:S(2)}, u32[]{:S(2)}) collective-permute-start(bf16[2,128,256]{2,1,0:T(8,128)(2,1)S(1)} %add_convert_fusion.10), channel_id=1, source_target_pairs={{0,8},{1,9},{2,10},{3,11},{4,12},{5,13},{6,14},{7,15},{8,0},{9,1},... | collective-permute-start | bytes 393224 | tf_op jit(solution)/shard_map/ppermute | solution.py:51
  117.1 3.7 %collective-permute-done.50 = bf16[2,128,256]{2,1,0:T(8,128)(2,1)S(1)} collective-permute-done((bf16[2,128,256]{2,1,0:T(8,128)(2,1)S(1)}, bf16[2,128,256]{2,1,0:T(8,128)(2,1)S(1)}, u32[]{:S(2)}, u32[]{:S(2)}) %collective-permute-start.50) | collective-permute-done | bytes 131104 | tf_op jit(solution)/shard_map/ppermute | solution.py:51
  121.6 3.4 %collective-permute-done.40 = bf16[4,128,256]{2,1,0:T(8,128)(2,1)S(1)} collective-permute-done((bf16[4,128,256]{2,1,0:T(8,128)(2,1)S(1)}, bf16[4,128,256]{2,1,0:T(8,128)(2,1)S(1)}, u32[]{:S(2)}, u32[]{:S(2)}) %collective-permute-start.40) | collective-permute-done | bytes 262176 | tf_op jit(solution)/shard_map/ppermute | solution.py:43
  (106 shorter events, 39.3 us)
Async XLA Ops:
  0.6 10.2 %collective-permute-start = (bf16[4,128,256]{2,1,0:T(8,128)(2,1)}, bf16[4,128,256]{2,1,0:T(8,128)(2,1)S(1)}, u32[]{:S(2)}, u32[]{:S(2)}) collective-permute-start(bf16[4,128,256]{2,1,0:T(8,128)(2,1)} %bitcast.41), channel_id=1, source_target_pairs={{0,16},{16,0},{32,48},{48,32},{64,80},{80,64},{96,112},{112,96},{1... | collective-permute-start | bytes 786440 | tf_op jit(solution)/shard_map/ppermute | solution.py:47
  2.4 11.8 %collective-permute-start.3 = (bf16[4,128,256]{2,1,0:T(8,128)(2,1)}, bf16[4,128,256]{2,1,0:T(8,128)(2,1)S(1)}, u32[]{:S(2)}, u32[]{:S(2)}) collective-permute-start(bf16[4,128,256]{2,1,0:T(8,128)(2,1)} %bitcast.42), channel_id=1, source_target_pairs={{0,64},{16,80},{32,96},{48,112},{64,0},{80,16},{96,32},{112,48},{1... | collective-permute-start | bytes 786440 | tf_op jit(solution)/shard_map/ppermute | solution.py:43
  6.2 12.7 %collective-permute-start.5 = (bf16[4,128,256]{2,1,0:T(8,128)(2,1)}, bf16[4,128,256]{2,1,0:T(8,128)(2,1)S(1)}, u32[]{:S(2)}, u32[]{:S(2)}) collective-permute-start(bf16[4,128,256]{2,1,0:T(8,128)(2,1)} %bitcast.43), channel_id=1, source_target_pairs={{0,32},{16,48},{32,64},{48,80},{64,96},{80,112},{96,0},{112,16},{1... | collective-permute-start | bytes 786440 | tf_op jit(solution)/shard_map/ppermute | solution.py:43
  7.3 13.1 %collective-permute-start.1 = (bf16[4,128,256]{2,1,0:T(8,128)(2,1)}, bf16[4,128,256]{2,1,0:T(8,128)(2,1)S(1)}, u32[]{:S(2)}, u32[]{:S(2)}) collective-permute-start(bf16[4,128,256]{2,1,0:T(8,128)(2,1)} %bitcast.44), channel_id=1, source_target_pairs={{0,96},{16,112},{32,0},{48,16},{64,32},{80,48},{96,64},{112,80},{1... | collective-permute-start | bytes 786440 | tf_op jit(solution)/shard_map/ppermute | solution.py:43
  10.9 12.9 %collective-permute-start.6 = (bf16[4,128,256]{2,1,0:T(8,128)(2,1)S(1)}, bf16[4,128,256]{2,1,0:T(8,128)(2,1)S(1)}, u32[]{:S(2)}, u32[]{:S(2)}) collective-permute-start(bf16[4,128,256]{2,1,0:T(8,128)(2,1)S(1)} %collective-permute-done.rest_1_), channel_id=1, source_target_pairs={{0,32},{16,48},{32,64},{48,80},{64,96},{80,112},{96,0},{112,16},{1... | collective-permute-start | bytes 786440 | tf_op jit(solution)/shard_map/ppermute | solution.py:43
  11.0 13.5 %collective-permute-start.2 = (bf16[4,128,256]{2,1,0:T(8,128)(2,1)S(1)}, bf16[4,128,256]{2,1,0:T(8,128)(2,1)S(1)}, u32[]{:S(2)}, u32[]{:S(2)}) collective-permute-start(bf16[4,128,256]{2,1,0:T(8,128)(2,1)S(1)} %collective-permute-done.rest_1_), channel_id=1, source_target_pairs={{0,96},{16,112},{32,0},{48,16},{64,32},{80,48},{96,64},{112,80},{1... | collective-permute-start | bytes 786440 | tf_op jit(solution)/shard_map/ppermute | solution.py:43
  31.2 13.6 %collective-permute-start.17 = (bf16[4,128,256]{2,1,0:T(8,128)(2,1)S(1)}, bf16[4,128,256]{2,1,0:T(8,128)(2,1)S(1)}, u32[]{:S(2)}, u32[]{:S(2)}) collective-permute-start(bf16[4,128,256]{2,1,0:T(8,128)(2,1)S(1)} %get-tuple-element.62), channel_id=1, source_target_pairs={{0,1},{1,0},{2,3},{3,2},{4,5},{5,4},{6,7},{7,6},{8,9},{9,8},{10,11... | collective-permute-start | bytes 786440 | tf_op jit(solution)/shard_map/ppermute | solution.py:59
  31.7 15.6 %collective-permute-start.20 = (bf16[4,128,256]{2,1,0:T(8,128)(2,1)S(1)}, bf16[4,128,256]{2,1,0:T(8,128)(2,1)S(1)}, u32[]{:S(2)}, u32[]{:S(2)}) collective-permute-start(bf16[4,128,256]{2,1,0:T(8,128)(2,1)S(1)} %add_convert_fusion.4), channel_id=1, source_target_pairs={{0,12},{1,13},{2,14},{3,15},{4,0},{5,1},{6,2},{7,3},{8,4},{9,5},{1... | collective-permute-start | bytes 786440 | tf_op jit(solution)/shard_map/ppermute | solution.py:51
  34.2 9.7 %collective-permute-start.15 = (bf16[4,128,256]{2,1,0:T(8,128)(2,1)S(1)}, bf16[4,128,256]{2,1,0:T(8,128)(2,1)S(1)}, u32[]{:S(2)}, u32[]{:S(2)}) collective-permute-start(bf16[4,128,256]{2,1,0:T(8,128)(2,1)S(1)} %add_convert_fusion.7), channel_id=1, source_target_pairs={{0,2},{1,3},{2,0},{3,1},{4,6},{5,7},{6,4},{7,5},{8,10},{9,11},{10,... | collective-permute-start | bytes 786440 | tf_op jit(solution)/shard_map/ppermute | solution.py:55
  36.9 11.9 %collective-permute-start.19 = (bf16[4,128,256]{2,1,0:T(8,128)(2,1)S(1)}, bf16[4,128,256]{2,1,0:T(8,128)(2,1)S(1)}, u32[]{:S(2)}, u32[]{:S(2)}) collective-permute-start(bf16[4,128,256]{2,1,0:T(8,128)(2,1)S(1)} %add_convert_fusion.5), channel_id=1, source_target_pairs={{0,4},{1,5},{2,6},{3,7},{4,8},{5,9},{6,10},{7,11},{8,12},{9,13},{1... | collective-permute-start | bytes 786440 | tf_op jit(solution)/shard_map/ppermute | solution.py:51
  38.4 13.8 %collective-permute-start.8 = (bf16[4,128,256]{2,1,0:T(8,128)(2,1)S(1)}, bf16[4,128,256]{2,1,0:T(8,128)(2,1)S(1)}, u32[]{:S(2)}, u32[]{:S(2)}) collective-permute-start(bf16[4,128,256]{2,1,0:T(8,128)(2,1)S(1)} %get-tuple-element.48), channel_id=1, source_target_pairs={{0,1},{1,0},{2,3},{3,2},{4,5},{5,4},{6,7},{7,6},{8,9},{9,8},{10,11... | collective-permute-start | bytes 786440 | tf_op jit(solution)/shard_map/ppermute | solution.py:59
  44.9 12.6 %collective-permute-start.12 = (bf16[4,128,256]{2,1,0:T(8,128)(2,1)S(1)}, bf16[4,128,256]{2,1,0:T(8,128)(2,1)S(1)}, u32[]{:S(2)}, u32[]{:S(2)}) collective-permute-start(bf16[4,128,256]{2,1,0:T(8,128)(2,1)S(1)} %add_convert_fusion.8), channel_id=1, source_target_pairs={{0,12},{1,13},{2,14},{3,15},{4,0},{5,1},{6,2},{7,3},{8,4},{9,5},{1... | collective-permute-start | bytes 786440 | tf_op jit(solution)/shard_map/ppermute | solution.py:51
  47.3 11.8 %collective-permute-start.16 = (bf16[4,128,256]{2,1,0:T(8,128)(2,1)S(1)}, bf16[4,128,256]{2,1,0:T(8,128)(2,1)S(1)}, u32[]{:S(2)}, u32[]{:S(2)}) collective-permute-start(bf16[4,128,256]{2,1,0:T(8,128)(2,1)S(1)} %add_convert_fusion.6), channel_id=1, source_target_pairs={{0,8},{1,9},{2,10},{3,11},{4,12},{5,13},{6,14},{7,15},{8,0},{9,1},... | collective-permute-start | bytes 786440 | tf_op jit(solution)/shard_map/ppermute | solution.py:51
  49.0 10.1 %collective-permute-start.21 = (bf16[4,128,256]{2,1,0:T(8,128)(2,1)S(1)}, bf16[4,128,256]{2,1,0:T(8,128)(2,1)S(1)}, u32[]{:S(2)}, u32[]{:S(2)}) collective-permute-start(bf16[4,128,256]{2,1,0:T(8,128)(2,1)S(1)} %add_convert_fusion.3), channel_id=1, source_target_pairs={{0,2},{1,3},{2,0},{3,1},{4,6},{5,7},{6,4},{7,5},{8,10},{9,11},{10,... | collective-permute-start | bytes 786440 | tf_op jit(solution)/shard_map/ppermute | solution.py:55
  60.2 13.9 %collective-permute-start.22 = (bf16[6,128,256]{2,1,0:T(8,128)(2,1)S(1)}, bf16[6,128,256]{2,1,0:T(8,128)(2,1)S(1)}, u32[]{:S(2)}, u32[]{:S(2)}) collective-permute-start(bf16[6,128,256]{2,1,0:T(8,128)(2,1)S(1)} %get-tuple-element.67), channel_id=1, source_target_pairs={{0,2},{1,3},{2,0},{3,1},{4,6},{5,7},{6,4},{7,5},{8,10},{9,11},{10,... | collective-permute-start | bytes 1179656 | tf_op jit(solution)/shard_map/ppermute | solution.py:55
  63.1 10.7 %collective-permute-start.25 = (bf16[4,128,256]{2,1,0:T(8,128)(2,1)S(1)}, bf16[4,128,256]{2,1,0:T(8,128)(2,1)S(1)}, u32[]{:S(2)}, u32[]{:S(2)}) collective-permute-start(bf16[4,128,256]{2,1,0:T(8,128)(2,1)S(1)} %get-tuple-element.69.rest_0_), channel_id=1, source_target_pairs={{0,8},{1,9},{2,10},{3,11},{4,12},{5,13},{6,14},{7,15},{8,0},{9,1},... | collective-permute-start | bytes 786440 | tf_op jit(solution)/shard_map/ppermute | solution.py:51
  63.8 13.9 %collective-permute-start.27 = (bf16[4,128,256]{2,1,0:T(8,128)(2,1)S(1)}, bf16[4,128,256]{2,1,0:T(8,128)(2,1)S(1)}, u32[]{:S(2)}, u32[]{:S(2)}) collective-permute-start(bf16[4,128,256]{2,1,0:T(8,128)(2,1)S(1)} %get-tuple-element.69.rest_0_), channel_id=1, source_target_pairs={{0,4},{1,5},{2,6},{3,7},{4,8},{5,9},{6,10},{7,11},{8,12},{9,13},{1... | collective-permute-start | bytes 786440 | tf_op jit(solution)/shard_map/ppermute | solution.py:51
  66.0 12.2 %collective-permute-start.23 = (bf16[4,128,256]{2,1,0:T(8,128)(2,1)S(1)}, bf16[4,128,256]{2,1,0:T(8,128)(2,1)S(1)}, u32[]{:S(2)}, u32[]{:S(2)}) collective-permute-start(bf16[4,128,256]{2,1,0:T(8,128)(2,1)S(1)} %get-tuple-element.69.rest_0_), channel_id=1, source_target_pairs={{0,12},{1,13},{2,14},{3,15},{4,0},{5,1},{6,2},{7,3},{8,4},{9,5},{1... | collective-permute-start | bytes 786440 | tf_op jit(solution)/shard_map/ppermute | solution.py:51
  89.8 12.8 %collective-permute-start.48 = (bf16[2,128,256]{2,1,0:T(8,128)(2,1)S(1)}, bf16[2,128,256]{2,1,0:T(8,128)(2,1)S(1)}, u32[]{:S(2)}, u32[]{:S(2)}) collective-permute-start(bf16[2,128,256]{2,1,0:T(8,128)(2,1)S(1)} %add_convert_fusion.11), channel_id=1, source_target_pairs={{0,96},{16,112},{32,0},{48,16},{64,32},{80,48},{96,64},{112,80},{1... | collective-permute-start | bytes 393224 | tf_op jit(solution)/shard_map/ppermute | solution.py:43
  93.3 9.5 %collective-permute-start.47 = (bf16[2,128,256]{2,1,0:T(8,128)(2,1)S(1)}, bf16[2,128,256]{2,1,0:T(8,128)(2,1)S(1)}, u32[]{:S(2)}, u32[]{:S(2)}) collective-permute-start(bf16[2,128,256]{2,1,0:T(8,128)(2,1)S(1)} %add_convert_fusion.11), channel_id=1, source_target_pairs={{0,32},{16,48},{32,64},{48,80},{64,96},{80,112},{96,0},{112,16},{1... | collective-permute-start | bytes 393224 | tf_op jit(solution)/shard_map/ppermute | solution.py:43
  93.3 12.6 %collective-permute-start.46 = (bf16[2,128,256]{2,1,0:T(8,128)(2,1)S(1)}, bf16[2,128,256]{2,1,0:T(8,128)(2,1)S(1)}, u32[]{:S(2)}, u32[]{:S(2)}) collective-permute-start(bf16[2,128,256]{2,1,0:T(8,128)(2,1)S(1)} %add_convert_fusion.11), channel_id=1, source_target_pairs={{0,64},{16,80},{32,96},{48,112},{64,0},{80,16},{96,32},{112,48},{1... | collective-permute-start | bytes 393224 | tf_op jit(solution)/shard_map/ppermute | solution.py:43
  99.3 10.5 %collective-permute-start.41 = (bf16[4,128,256]{2,1,0:T(8,128)(2,1)S(1)}, bf16[4,128,256]{2,1,0:T(8,128)(2,1)S(1)}, u32[]{:S(2)}, u32[]{:S(2)}) collective-permute-start(bf16[4,128,256]{2,1,0:T(8,128)(2,1)S(1)} %get-tuple-element.83), channel_id=1, source_target_pairs={{0,32},{16,48},{32,64},{48,80},{64,96},{80,112},{96,0},{112,16},{1... | collective-permute-start | bytes 786440 | tf_op jit(solution)/shard_map/ppermute | solution.py:43
  102.6 19.0 %collective-permute-start.37 = (bf16[4,128,256]{2,1,0:T(8,128)(2,1)S(1)}, bf16[4,128,256]{2,1,0:T(8,128)(2,1)S(1)}, u32[]{:S(2)}, u32[]{:S(2)}) collective-permute-start(bf16[4,128,256]{2,1,0:T(8,128)(2,1)S(1)} %get-tuple-element.78), channel_id=1, source_target_pairs={{0,32},{16,48},{32,64},{48,80},{64,96},{80,112},{96,0},{112,16},{1... | collective-permute-start | bytes 786440 | tf_op jit(solution)/shard_map/ppermute | solution.py:43
  102.8 18.8 %collective-permute-start.38 = (bf16[4,128,256]{2,1,0:T(8,128)(2,1)S(1)}, bf16[4,128,256]{2,1,0:T(8,128)(2,1)S(1)}, u32[]{:S(2)}, u32[]{:S(2)}) collective-permute-start(bf16[4,128,256]{2,1,0:T(8,128)(2,1)S(1)} %get-tuple-element.79), channel_id=1, source_target_pairs={{0,96},{16,112},{32,0},{48,16},{64,32},{80,48},{96,64},{112,80},{1... | collective-permute-start | bytes 786440 | tf_op jit(solution)/shard_map/ppermute | solution.py:43
  (30 other events, 223.8 us)

commit v4 on v3

--- a/solution.py
+++ b/solution.py
@@ -11,7 +11,7 @@
 BLK = 128
 WIDTH = 256
 CAP = 128
-UNROLL = 16
+UNROLL = 32
 CHUNKS = 4
 BF16 = jnp.bfloat16
 F32 = jnp.float32
@@ -41,6 +41,10 @@
 
 def z_send(v, step):
     return lax.ppermute(v, "row", z_perm(step))
+
+
+def z_pair(v, flip):
+    return lax.ppermute(v, "row", [(r, r ^ (2 * flip)) for r in range(2 * NZ)])
 
 
 def yl_swap(v):
@@ -99,15 +103,11 @@
 
     def group(i, carry):
         first = i * UNROLL
-        products = [
-            lax.dot_general(
+        for u in range(UNROLL):
+            slot = out_ref[first + u]
+            acc[slot] += lax.dot_general(
                 tiles[first + u], blocks[in_ref[first + u]], dims, preferred_element_type=F32
             )
-            for u in range(UNROLL)
-        ]
-        for u in range(UNROLL):
-            slot = out_ref[first + u]
-            acc[slot] += products[u]
         return carry
 
     groups = (cnt_ref[0] + UNROLL - 1) // UNROLL
@@ -145,7 +145,7 @@
             ],
         ),
         out_shape=[jax.ShapeDtypeStruct((4, BLK, WIDTH), BF16)] * n_out,
-        compiler_params=pltpu.CompilerParams(vmem_limit_bytes=16 * 1024 * 1024),
+        compiler_params=pltpu.CompilerParams(vmem_limit_bytes=(19 if len(pieces) == 8 else 16) * 1024 * 1024),
         cost_estimate=pl.CostEstimate(
             flops=2 * CAP * BLK * BLK * WIDTH,
             bytes_accessed=2 * CAP * BLK * BLK + 8 * (len(pieces) + n_out) * BLK * WIDTH,
@@ -243,7 +243,7 @@
     two = yh_swap(add(mine[5], other[5]))
     up, down = x_send(add(mine[3], other[3]), 1), x_send(add(mine[7], other[7]), -1)
     own_up, own_down = x_send(add(mine[2], other[2]), 1), x_send(add(mine[6], other[6]), -1)
-    across = x_send(add(mine[4], other[4], two), 2)
+    across = x_send(after(add(mine[4], other[4], two), own_up, own_down), 2)
     far = yh_swap(add(mine[1], other[1], up, down))
     terms = [mine[0], other[0], own_up, own_down, across, far]
     scale = 1.0 / math.sqrt(features.shape[0] * lax.axis_size("row") * lax.axis_size("col"))
@@ -256,20 +256,23 @@
     far_up, far_down = x_send(far, -1), x_send(far, 1)
     far_across = yh_swap(across)
     pieces = [own, far, up, far_up, across, far_across, down, far_down]
-    far_rider, *ready = lax.optimization_barrier((far_rider, *pieces))
-    term = add(own_rider[4:], far_rider[4:])
-    term = add(term, yl_swap(term))
+    term = add(own_rider[4:], after(far_rider[4:], up, down))
+    near_term = z_pair(term, 1)
+    term, near_term, *ready = lax.optimization_barrier((term, near_term, *pieces))
+    term = add(term, near_term)
     pieces = [*ready, *(core_swap(v) for v in ready)]
     term = add(term, core_swap(term))
-    term = ring_sum(term, z_send).astype(BF16)
+    near_term = z_pair(term, 2)
     back = cell_product("backward_cell", True, col_slot, row_slot, count, tiles, pieces, 8)
     two = yl_swap(back[5])
     up, down = z_send(back[3], 1), z_send(back[7], -1)
     own_up, own_down = z_send(back[2], 1), z_send(back[6], -1)
-    across = z_send(add(back[4], two), 2)
+    across = z_send(after(add(back[4], two), own_up, own_down), 2)
     far = yl_swap(add(back[1], up, down))
     grad_features = add(back[0], own_up, own_down, across, far)
-    weight_grad = ring_sum(after(term, up, down), x_send).reshape(WIDTH, WIDTH)
+    term = add(term, after(near_term, back[0]))
+    term = add(term, yl_swap(term))
+    weight_grad = ring_sum(term, x_send).reshape(WIDTH, WIDTH)
     return (output, grad_features.reshape(4 * BLK, WIDTH), weight_grad)
 
 

time: 128 us -> 121 us (0.945); the launches traced: 128 us -> 120 us
  waiting for transfers between devices: 54.3 us -> 42.2 us
  starting transfers between devices: 59.3 us -> 63.5 us
    ppermute x4, waiting for transfers between devices: 10.1 us -> 1.27 us  [yh_swap(): return lax.ppermute(v, 'col', yh_perm())]
    ppermute x13 -> x10, waiting for transfers between devices: 17.1 us -> 10.3 us  [z_send(): return lax.ppermute(v, 'row', z_perm(step))]
    ppermute x5, waiting for transfers between devices: 6.64 us -> 1.46 us  [yl_swap(): return lax.ppermute(v, 'row', yl_perm())]
    ppermute x13, waiting for transfers between devices: 19.2 us -> 24.3 us  [x_send(): return lax.ppermute(v, 'col', x_perm(step))]
    ppermute x0 -> x2, starting transfers between devices: none -> 4.9 us  [z_pair(): return lax.ppermute(v, 'row', [(r, r ^ 2 * flip) for r in range(2 * NZ)])]
    ppermute x5, starting transfers between devices: 2.32 us -> 5.08 us  [yl_swap(): return lax.ppermute(v, 'row', yl_perm())]
    ppermute x13 -> x10, starting transfers between devices: 22.3 us -> 19.6 us  [z_send(): return lax.ppermute(v, 'row', z_perm(step))]
    ppermute x0 -> x2, waiting for transfers between devices: none -> 2.6 us  [z_pair(): return lax.ppermute(v, 'row', [(r, r ^ 2 * flip) for r in range(2 * NZ)])]
  transfers between devices with their start and end apart: 52 -> 51, of which waited for: 22 -> 20; matrix products, arithmetic and copies ran while one was open for 2% -> 2% of each run, Pallas kernels for 3% -> 3%
where the time goes in v4:
time: 121 us; the launch traced here: 120 us
  starting transfers between devices  63.5 us (52%)
  waiting for transfers between devices  42.2 us (35%)
  Pallas kernels  8.91 us (7%)
  other arithmetic  3.28 us (3%)
  between operations  1.58 us (1%)
    ppermute x13, waiting for transfers between devices, x_send(): return lax.ppermute(v, 'col', x_perm(step))  24.3 us
    ppermute x10, starting transfers between devices, z_send(): return lax.ppermute(v, 'row', z_perm(step))  19.6 us
    ppermute x13, starting transfers between devices, x_send(): return lax.ppermute(v, 'col', x_perm(step))  19.5 us
    ppermute x4, starting transfers between devices, yh_swap(): return lax.ppermute(v, 'col', yh_perm())  10.4 us
    ppermute x10, waiting for transfers between devices, z_send(): return lax.ppermute(v, 'row', z_perm(step))  10.3 us
    pallas_call x2, Pallas kernels, cell_product(): pl.pallas_call(functools.partial(cell_kernel, transposed, len(pieces), n_...  7.81 us
    ppermute x5, starting transfers between devices, yl_swap(): return lax.ppermute(v, 'row', yl_perm())  5.08 us
    ppermute x2, starting transfers between devices, z_pair(): return lax.ppermute(v, 'row', [(r, r ^ 2 * flip) for r in range(2 * NZ)])  4.9 us
  transfers between devices with their start and end apart: 51, of which 20 were waited for; matrix products, arithmetic and copies ran while one was open for 2% of the time, Pallas kernels for 3%

profile of v4, /device:TPU:0, one launch (start us, length us, event | category | flops | bytes accessed | tf_op | source)
XLA Modules:
  0.0 119.5 jit_solution(15455899870304947728)
XLA Ops:
  2.4 3.9 %collective-permute-start.3 = (bf16[4,128,256]{2,1,0:T(8,128)(2,1)}, bf16[4,128,256]{2,1,0:T(8,128)(2,1)S(1)}, u32[]{:S(2)}, u32[]{:S(2)}) collective-permute-start(bf16[4,128,256]{2,1,0:T(8,128)(2,1)} %bitcast.42), channel_id=1, source_target_pairs={{0,64},{16,80},{32,96},{48,112},{64,0},{80,16},{96,32},{112,48},{1... | collective-permute-start | bytes 786440 | tf_op jit(solution)/shard_map/ppermute | solution.py:43
  7.3 2.2 %collective-permute-start.1 = (bf16[4,128,256]{2,1,0:T(8,128)(2,1)}, bf16[4,128,256]{2,1,0:T(8,128)(2,1)S(1)}, u32[]{:S(2)}, u32[]{:S(2)}) collective-permute-start(bf16[4,128,256]{2,1,0:T(8,128)(2,1)} %bitcast.44), channel_id=1, source_target_pairs={{0,96},{16,112},{32,0},{48,16},{64,32},{80,48},{96,64},{112,80},{1... | collective-permute-start | bytes 786440 | tf_op jit(solution)/shard_map/ppermute | solution.py:43
  11.0 3.2 %collective-permute-start.2 = (bf16[4,128,256]{2,1,0:T(8,128)(2,1)S(1)}, bf16[4,128,256]{2,1,0:T(8,128)(2,1)S(1)}, u32[]{:S(2)}, u32[]{:S(2)}) collective-permute-start(bf16[4,128,256]{2,1,0:T(8,128)(2,1)S(1)} %collective-permute-done.rest_1_), channel_id=1, source_target_pairs={{0,96},{16,112},{32,0},{48,16},{64,32},{80,48},{96,64},{112,80},{1... | collective-permute-start | bytes 786440 | tf_op jit(solution)/shard_map/ppermute | solution.py:43
  14.7 4.3 %collective-permute-done.5.rest_6_ = bf16[4,128,256]{2,1,0:T(8,128)(2,1)S(1)} collective-permute-done((bf16[4,128,256]{2,1,0:T(8,128)(2,1)}, bf16[4,128,256]{2,1,0:T(8,128)(2,1)S(1)}, u32[]{:S(2)}, u32[]{:S(2)}) %collective-permute-start.5) | collective-permute-done | bytes 262176 | tf_op jit(solution)/shard_map/ppermute | solution.py:43
  20.6 3.2 %collective-permute-done.6.rest_7_ = bf16[4,128,256]{2,1,0:T(8,128)(2,1)S(1)} collective-permute-done((bf16[4,128,256]{2,1,0:T(8,128)(2,1)S(1)}, bf16[4,128,256]{2,1,0:T(8,128)(2,1)S(1)}, u32[]{:S(2)}, u32[]{:S(2)}) %collective-permute-start.6) | collective-permute-done | bytes 262176 | tf_op jit(solution)/shard_map/ppermute | solution.py:43
  24.5 4.0 %forward_cell.1 = (bf16[4,128,256]{2,1,0:T(8,128)(2,1)S(1)}, bf16[4,128,256]{2,1,0:T(8,128)(2,1)S(1)}, bf16[4,128,256]{2,1,0:T(8,128)(2,1)S(1)}, bf16[4,128,256]...) custom-call(s32[128]{0:T(128)S(1)} %fusion.19.out_ref, ...), custom_call_target="tpu_custom_call" | custom-call | flops 1073741824 | bytes 10485760 | tf_op jit(solution)/shard_map/forward_cell/pallas_call | solution.py:132
  31.4 3.2 %collective-permute-start.20 = (bf16[4,128,256]{2,1,0:T(8,128)(2,1)S(1)}, bf16[4,128,256]{2,1,0:T(8,128)(2,1)S(1)}, u32[]{:S(2)}, u32[]{:S(2)}) collective-permute-start(bf16[4,128,256]{2,1,0:T(8,128)(2,1)S(1)} %add_convert_fusion.4), channel_id=1, source_target_pairs={{0,12},{1,13},{2,14},{3,15},{4,0},{5,1},{6,2},{7,3},{8,4},{9,5},{1... | collective-permute-start | bytes 786440 | tf_op jit(solution)/shard_map/ppermute | solution.py:55
  34.8 3.3 %collective-permute-start.15 = (bf16[4,128,256]{2,1,0:T(8,128)(2,1)S(1)}, bf16[4,128,256]{2,1,0:T(8,128)(2,1)S(1)}, u32[]{:S(2)}, u32[]{:S(2)}) collective-permute-start(bf16[4,128,256]{2,1,0:T(8,128)(2,1)S(1)} %add_convert_fusion.7), channel_id=1, source_target_pairs={{0,2},{1,3},{2,0},{3,1},{4,6},{5,7},{6,4},{7,5},{8,10},{9,11},{10,... | collective-permute-start | bytes 786440 | tf_op jit(solution)/shard_map/ppermute | solution.py:59
  38.3 2.4 %collective-permute-done.20 = bf16[4,128,256]{2,1,0:T(8,128)(2,1)S(1)} collective-permute-done((bf16[4,128,256]{2,1,0:T(8,128)(2,1)S(1)}, bf16[4,128,256]{2,1,0:T(8,128)(2,1)S(1)}, u32[]{:S(2)}, u32[]{:S(2)}) %collective-permute-start.20) | collective-permute-done | bytes 262176 | tf_op jit(solution)/shard_map/ppermute | solution.py:55
  41.3 2.9 %collective-permute-done.19 = bf16[4,128,256]{2,1,0:T(8,128)(2,1)S(1)} collective-permute-done((bf16[4,128,256]{2,1,0:T(8,128)(2,1)S(1)}, bf16[4,128,256]{2,1,0:T(8,128)(2,1)S(1)}, u32[]{:S(2)}, u32[]{:S(2)}) %collective-permute-start.19) | collective-permute-done | bytes 262176 | tf_op jit(solution)/shard_map/ppermute | solution.py:55
  44.5 3.1 %collective-permute-start.21 = (bf16[4,128,256]{2,1,0:T(8,128)(2,1)S(1)}, bf16[4,128,256]{2,1,0:T(8,128)(2,1)S(1)}, u32[]{:S(2)}, u32[]{:S(2)}) collective-permute-start(bf16[4,128,256]{2,1,0:T(8,128)(2,1)S(1)} %add_convert_fusion.3), channel_id=1, source_target_pairs={{0,2},{1,3},{2,0},{3,1},{4,6},{5,7},{6,4},{7,5},{8,10},{9,11},{10,... | collective-permute-start | bytes 786440 | tf_op jit(solution)/shard_map/ppermute | solution.py:59
  47.7 2.7 %collective-permute-done.10.refs_2_ = bf16[4,128,256]{2,1,0:T(8,128)(2,1)S(1)} collective-permute-done((bf16[4,128,256]{2,1,0:T(8,128)(2,1)S(1)}, bf16[4,128,256]{2,1,0:T(8,128)(2,1)S(1)}, u32[]{:S(2)}, u32[]{:S(2)}) %collective-permute-start.10) | collective-permute-done | bytes 262176 | tf_op jit(solution)/shard_map/ppermute | solution.py:55
  53.6 6.1 %collective-permute-done.16.refs_4_ = bf16[4,128,256]{2,1,0:T(8,128)(2,1)S(1)} collective-permute-done((bf16[4,128,256]{2,1,0:T(8,128)(2,1)S(1)}, bf16[4,128,256]{2,1,0:T(8,128)(2,1)S(1)}, u32[]{:S(2)}, u32[]{:S(2)}) %collective-permute-start.16) | collective-permute-done | bytes 262176 | tf_op jit(solution)/shard_map/ppermute | solution.py:55
  67.6 4.4 %collective-permute-done.27.rest_4_ = bf16[4,128,256]{2,1,0:T(8,128)(2,1)S(1)} collective-permute-done((bf16[4,128,256]{2,1,0:T(8,128)(2,1)S(1)}, bf16[4,128,256]{2,1,0:T(8,128)(2,1)S(1)}, u32[]{:S(2)}, u32[]{:S(2)}) %collective-permute-start.27) | collective-permute-done | bytes 262176 | tf_op jit(solution)/shard_map/ppermute | solution.py:55
  72.0 2.0 %collective-permute-start.28 = (bf16[4,128,256]{2,1,0:T(8,128)(2,1)S(1)}, bf16[4,128,256]{2,1,0:T(8,128)(2,1)S(1)}, u32[]{:S(2)}, u32[]{:S(2)}) collective-permute-start(bf16[4,128,256]{2,1,0:T(8,128)(2,1)S(1)} %collective-permute-done.27.rest_4_), channel_id=1, source_target_pairs={{0,2},{1,3},{2,0},{3,1},{4,6},{5,7},{6,4},{7,5},{8,10},{9,11},{10,... | collective-permute-start | bytes 786440 | tf_op jit(solution)/shard_map/ppermute | solution.py:59
  74.7 2.7 %collective-permute-start.26 = (bf16[4,128,256]{2,1,0:T(8,128)(2,1)S(1)}, bf16[4,128,256]{2,1,0:T(8,128)(2,1)S(1)}, u32[]{:S(2)}, u32[]{:S(2)}) collective-permute-start(bf16[4,128,256]{2,1,0:T(8,128)(2,1)S(1)} %slice.13.rest_1_), channel_id=1, source_target_pairs={{0,12},{1,13},{2,14},{3,15},{4,0},{5,1},{6,2},{7,3},{8,4},{9,5},{1... | collective-permute-start | bytes 786440 | tf_op jit(solution)/shard_map/ppermute | solution.py:55
  79.9 2.6 %collective-permute-done.25 = bf16[2,128,256]{2,1,0:T(8,128)(2,1)S(1)} collective-permute-done((bf16[2,128,256]{2,1,0:T(8,128)(2,1)S(1)}, bf16[2,128,256]{2,1,0:T(8,128)(2,1)S(1)}, u32[]{:S(2)}, u32[]{:S(2)}) %collective-permute-start.25) | collective-permute-done | bytes 131104 | tf_op jit(solution)/shard_map/ppermute | solution.py:47
  86.1 3.4 %collective-permute-start.46 = (bf16[2,128,256]{2,1,0:T(8,128)(2,1)S(1)}, bf16[2,128,256]{2,1,0:T(8,128)(2,1)S(1)}, u32[]{:S(2)}, u32[]{:S(2)}) collective-permute-start(bf16[2,128,256]{2,1,0:T(8,128)(2,1)S(1)} %add_convert_fusion.12), channel_id=1, source_target_pairs={{0,64},{16,80},{32,96},{48,112},{64,0},{80,16},{96,32},{112,48},{1... | collective-permute-start | bytes 393224 | tf_op jit(solution)/shard_map/ppermute | solution.py:47
  89.5 3.8 %backward_cell.1 = (bf16[4,128,256]{2,1,0:T(8,128)(2,1)S(1)}, bf16[4,128,256]{2,1,0:T(8,128)(2,1)S(1)}, bf16[4,128,256]{2,1,0:T(8,128)(2,1)S(1)}, bf16[4,128,256...) custom-call(s32[128]{0:T(128)S(1)} %get-tuple-element.99.out_ref, ...), custom_call_target="tpu_custom_call" | custom-call | flops 1073741824 | bytes 10485760 | tf_op jit(solution)/shard_map/backward_cell/pallas_call | solution.py:132
  96.9 2.3 %collective-permute-start.39 = (bf16[4,128,256]{2,1,0:T(8,128)(2,1)S(1)}, bf16[4,128,256]{2,1,0:T(8,128)(2,1)S(1)}, u32[]{:S(2)}, u32[]{:S(2)}) collective-permute-start(bf16[4,128,256]{2,1,0:T(8,128)(2,1)S(1)} %get-tuple-element.85), channel_id=1, source_target_pairs={{0,96},{16,112},{32,0},{48,16},{64,32},{80,48},{96,64},{112,80},{1... | collective-permute-start | bytes 786440 | tf_op jit(solution)/shard_map/ppermute | solution.py:43
  99.8 3.8 %collective-permute-start.43 = (bf16[4,128,256]{2,1,0:T(8,128)(2,1)S(1)}, bf16[4,128,256]{2,1,0:T(8,128)(2,1)S(1)}, u32[]{:S(2)}, u32[]{:S(2)}) collective-permute-start(bf16[4,128,256]{2,1,0:T(8,128)(2,1)S(1)} %get-tuple-element.91), channel_id=1, source_target_pairs={{0,96},{16,112},{32,0},{48,16},{64,32},{80,48},{96,64},{112,80},{1... | collective-permute-start | bytes 786440 | tf_op jit(solution)/shard_map/ppermute | solution.py:43
  104.3 3.1 %collective-permute-start.50 = (bf16[2,128,256]{2,1,0:T(8,128)(2,1)S(1)}, bf16[2,128,256]{2,1,0:T(8,128)(2,1)S(1)}, u32[]{:S(2)}, u32[]{:S(2)}) collective-permute-start(bf16[2,128,256]{2,1,0:T(8,128)(2,1)S(1)} %add_convert_fusion.10), channel_id=1, source_target_pairs={{0,12},{1,13},{2,14},{3,15},{4,0},{5,1},{6,2},{7,3},{8,4},{9,5},{1... | collective-permute-start | bytes 393224 | tf_op jit(solution)/shard_map/ppermute | solution.py:55
  107.7 2.4 %collective-permute-start.48 = (bf16[2,128,256]{2,1,0:T(8,128)(2,1)S(1)}, bf16[2,128,256]{2,1,0:T(8,128)(2,1)S(1)}, u32[]{:S(2)}, u32[]{:S(2)}) collective-permute-start(bf16[2,128,256]{2,1,0:T(8,128)(2,1)S(1)} %add_convert_fusion.10), channel_id=1, source_target_pairs={{0,8},{1,9},{2,10},{3,11},{4,12},{5,13},{6,14},{7,15},{8,0},{9,1},... | collective-permute-start | bytes 393224 | tf_op jit(solution)/shard_map/ppermute | solution.py:55
  112.5 4.6 %collective-permute-done.49 = bf16[2,128,256]{2,1,0:T(8,128)(2,1)S(1)} collective-permute-done((bf16[2,128,256]{2,1,0:T(8,128)(2,1)S(1)}, bf16[2,128,256]{2,1,0:T(8,128)(2,1)S(1)}, u32[]{:S(2)}, u32[]{:S(2)}) %collective-permute-start.49) | collective-permute-done | bytes 131104 | tf_op jit(solution)/shard_map/ppermute | solution.py:55
  (106 shorter events, 38.3 us)
Async XLA Ops:
  0.6 10.2 %collective-permute-start = (bf16[4,128,256]{2,1,0:T(8,128)(2,1)}, bf16[4,128,256]{2,1,0:T(8,128)(2,1)S(1)}, u32[]{:S(2)}, u32[]{:S(2)}) collective-permute-start(bf16[4,128,256]{2,1,0:T(8,128)(2,1)} %bitcast.41), channel_id=1, source_target_pairs={{0,16},{16,0},{32,48},{48,32},{64,80},{80,64},{96,112},{112,96},{1... | collective-permute-start | bytes 786440 | tf_op jit(solution)/shard_map/ppermute | solution.py:51
  2.4 11.8 %collective-permute-start.3 = (bf16[4,128,256]{2,1,0:T(8,128)(2,1)}, bf16[4,128,256]{2,1,0:T(8,128)(2,1)S(1)}, u32[]{:S(2)}, u32[]{:S(2)}) collective-permute-start(bf16[4,128,256]{2,1,0:T(8,128)(2,1)} %bitcast.42), channel_id=1, source_target_pairs={{0,64},{16,80},{32,96},{48,112},{64,0},{80,16},{96,32},{112,48},{1... | collective-permute-start | bytes 786440 | tf_op jit(solution)/shard_map/ppermute | solution.py:43
  6.2 12.7 %collective-permute-start.5 = (bf16[4,128,256]{2,1,0:T(8,128)(2,1)}, bf16[4,128,256]{2,1,0:T(8,128)(2,1)S(1)}, u32[]{:S(2)}, u32[]{:S(2)}) collective-permute-start(bf16[4,128,256]{2,1,0:T(8,128)(2,1)} %bitcast.43), channel_id=1, source_target_pairs={{0,32},{16,48},{32,64},{48,80},{64,96},{80,112},{96,0},{112,16},{1... | collective-permute-start | bytes 786440 | tf_op jit(solution)/shard_map/ppermute | solution.py:43
  7.3 13.1 %collective-permute-start.1 = (bf16[4,128,256]{2,1,0:T(8,128)(2,1)}, bf16[4,128,256]{2,1,0:T(8,128)(2,1)S(1)}, u32[]{:S(2)}, u32[]{:S(2)}) collective-permute-start(bf16[4,128,256]{2,1,0:T(8,128)(2,1)} %bitcast.44), channel_id=1, source_target_pairs={{0,96},{16,112},{32,0},{48,16},{64,32},{80,48},{96,64},{112,80},{1... | collective-permute-start | bytes 786440 | tf_op jit(solution)/shard_map/ppermute | solution.py:43
  10.9 12.9 %collective-permute-start.6 = (bf16[4,128,256]{2,1,0:T(8,128)(2,1)S(1)}, bf16[4,128,256]{2,1,0:T(8,128)(2,1)S(1)}, u32[]{:S(2)}, u32[]{:S(2)}) collective-permute-start(bf16[4,128,256]{2,1,0:T(8,128)(2,1)S(1)} %collective-permute-done.rest_1_), channel_id=1, source_target_pairs={{0,32},{16,48},{32,64},{48,80},{64,96},{80,112},{96,0},{112,16},{1... | collective-permute-start | bytes 786440 | tf_op jit(solution)/shard_map/ppermute | solution.py:43
  11.0 13.5 %collective-permute-start.2 = (bf16[4,128,256]{2,1,0:T(8,128)(2,1)S(1)}, bf16[4,128,256]{2,1,0:T(8,128)(2,1)S(1)}, u32[]{:S(2)}, u32[]{:S(2)}) collective-permute-start(bf16[4,128,256]{2,1,0:T(8,128)(2,1)S(1)} %collective-permute-done.rest_1_), channel_id=1, source_target_pairs={{0,96},{16,112},{32,0},{48,16},{64,32},{80,48},{96,64},{112,80},{1... | collective-permute-start | bytes 786440 | tf_op jit(solution)/shard_map/ppermute | solution.py:43
  30.8 13.7 %collective-permute-start.13 = (bf16[4,128,256]{2,1,0:T(8,128)(2,1)S(1)}, bf16[4,128,256]{2,1,0:T(8,128)(2,1)S(1)}, u32[]{:S(2)}, u32[]{:S(2)}) collective-permute-start(bf16[4,128,256]{2,1,0:T(8,128)(2,1)S(1)} %get-tuple-element.61), channel_id=1, source_target_pairs={{0,1},{1,0},{2,3},{3,2},{4,5},{5,4},{6,7},{7,6},{8,9},{9,8},{10,11... | collective-permute-start | bytes 786440 | tf_op jit(solution)/shard_map/ppermute | solution.py:63
  31.4 9.2 %collective-permute-start.20 = (bf16[4,128,256]{2,1,0:T(8,128)(2,1)S(1)}, bf16[4,128,256]{2,1,0:T(8,128)(2,1)S(1)}, u32[]{:S(2)}, u32[]{:S(2)}) collective-permute-start(bf16[4,128,256]{2,1,0:T(8,128)(2,1)S(1)} %add_convert_fusion.4), channel_id=1, source_target_pairs={{0,12},{1,13},{2,14},{3,15},{4,0},{5,1},{6,2},{7,3},{8,4},{9,5},{1... | collective-permute-start | bytes 786440 | tf_op jit(solution)/shard_map/ppermute | solution.py:55
  34.6 9.6 %collective-permute-start.19 = (bf16[4,128,256]{2,1,0:T(8,128)(2,1)S(1)}, bf16[4,128,256]{2,1,0:T(8,128)(2,1)S(1)}, u32[]{:S(2)}, u32[]{:S(2)}) collective-permute-start(bf16[4,128,256]{2,1,0:T(8,128)(2,1)S(1)} %add_convert_fusion.5), channel_id=1, source_target_pairs={{0,4},{1,5},{2,6},{3,7},{4,8},{5,9},{6,10},{7,11},{8,12},{9,13},{1... | collective-permute-start | bytes 786440 | tf_op jit(solution)/shard_map/ppermute | solution.py:55
  34.8 12.8 %collective-permute-start.15 = (bf16[4,128,256]{2,1,0:T(8,128)(2,1)S(1)}, bf16[4,128,256]{2,1,0:T(8,128)(2,1)S(1)}, u32[]{:S(2)}, u32[]{:S(2)}) collective-permute-start(bf16[4,128,256]{2,1,0:T(8,128)(2,1)S(1)} %add_convert_fusion.7), channel_id=1, source_target_pairs={{0,2},{1,3},{2,0},{3,1},{4,6},{5,7},{6,4},{7,5},{8,10},{9,11},{10,... | collective-permute-start | bytes 786440 | tf_op jit(solution)/shard_map/ppermute | solution.py:59
  38.2 15.1 %collective-permute-start.8 = (bf16[4,128,256]{2,1,0:T(8,128)(2,1)S(1)}, bf16[4,128,256]{2,1,0:T(8,128)(2,1)S(1)}, u32[]{:S(2)}, u32[]{:S(2)}) collective-permute-start(bf16[4,128,256]{2,1,0:T(8,128)(2,1)S(1)} %get-tuple-element.52), channel_id=1, source_target_pairs={{0,1},{1,0},{2,3},{3,2},{4,5},{5,4},{6,7},{7,6},{8,9},{9,8},{10,11... | collective-permute-start | bytes 786440 | tf_op jit(solution)/shard_map/ppermute | solution.py:63
  40.7 9.7 %collective-permute-start.10 = (bf16[4,128,256]{2,1,0:T(8,128)(2,1)S(1)}, bf16[4,128,256]{2,1,0:T(8,128)(2,1)S(1)}, u32[]{:S(2)}, u32[]{:S(2)}) collective-permute-start(bf16[4,128,256]{2,1,0:T(8,128)(2,1)S(1)} %add_convert_fusion.9), channel_id=1, source_target_pairs={{0,4},{1,5},{2,6},{3,7},{4,8},{5,9},{6,10},{7,11},{8,12},{9,13},{1... | collective-permute-start | bytes 786440 | tf_op jit(solution)/shard_map/ppermute | solution.py:55
  44.5 9.1 %collective-permute-start.21 = (bf16[4,128,256]{2,1,0:T(8,128)(2,1)S(1)}, bf16[4,128,256]{2,1,0:T(8,128)(2,1)S(1)}, u32[]{:S(2)}, u32[]{:S(2)}) collective-permute-start(bf16[4,128,256]{2,1,0:T(8,128)(2,1)S(1)} %add_convert_fusion.3), channel_id=1, source_target_pairs={{0,2},{1,3},{2,0},{3,1},{4,6},{5,7},{6,4},{7,5},{8,10},{9,11},{10,... | collective-permute-start | bytes 786440 | tf_op jit(solution)/shard_map/ppermute | solution.py:59
  60.8 13.2 %collective-permute-start.22 = (bf16[6,128,256]{2,1,0:T(8,128)(2,1)S(1)}, bf16[6,128,256]{2,1,0:T(8,128)(2,1)S(1)}, u32[]{:S(2)}, u32[]{:S(2)}) collective-permute-start(bf16[6,128,256]{2,1,0:T(8,128)(2,1)S(1)} %get-tuple-element.72), channel_id=1, source_target_pairs={{0,2},{1,3},{2,0},{3,1},{4,6},{5,7},{6,4},{7,5},{8,10},{9,11},{10,... | collective-permute-start | bytes 1179656 | tf_op jit(solution)/shard_map/ppermute | solution.py:59
  62.7 9.3 %collective-permute-start.27 = (bf16[4,128,256]{2,1,0:T(8,128)(2,1)S(1)}, bf16[4,128,256]{2,1,0:T(8,128)(2,1)S(1)}, u32[]{:S(2)}, u32[]{:S(2)}) collective-permute-start(bf16[4,128,256]{2,1,0:T(8,128)(2,1)S(1)} %get-tuple-element.75.rest_0_), channel_id=1, source_target_pairs={{0,8},{1,9},{2,10},{3,11},{4,12},{5,13},{6,14},{7,15},{8,0},{9,1},... | collective-permute-start | bytes 786440 | tf_op jit(solution)/shard_map/ppermute | solution.py:55
  64.4 13.0 %collective-permute-start.24 = (bf16[4,128,256]{2,1,0:T(8,128)(2,1)S(1)}, bf16[4,128,256]{2,1,0:T(8,128)(2,1)S(1)}, u32[]{:S(2)}, u32[]{:S(2)}) collective-permute-start(bf16[4,128,256]{2,1,0:T(8,128)(2,1)S(1)} %get-tuple-element.75.rest_0_), channel_id=1, source_target_pairs={{0,4},{1,5},{2,6},{3,7},{4,8},{5,9},{6,10},{7,11},{8,12},{9,13},{1... | collective-permute-start | bytes 786440 | tf_op jit(solution)/shard_map/ppermute | solution.py:55
  65.7 11.7 %collective-permute-start.23 = (bf16[4,128,256]{2,1,0:T(8,128)(2,1)S(1)}, bf16[4,128,256]{2,1,0:T(8,128)(2,1)S(1)}, u32[]{:S(2)}, u32[]{:S(2)}) collective-permute-start(bf16[4,128,256]{2,1,0:T(8,128)(2,1)S(1)} %get-tuple-element.75.rest_0_), channel_id=1, source_target_pairs={{0,12},{1,13},{2,14},{3,15},{4,0},{5,1},{6,2},{7,3},{8,4},{9,5},{1... | collective-permute-start | bytes 786440 | tf_op jit(solution)/shard_map/ppermute | solution.py:55
  93.6 10.7 %collective-permute-start.40 = (bf16[4,128,256]{2,1,0:T(8,128)(2,1)S(1)}, bf16[4,128,256]{2,1,0:T(8,128)(2,1)S(1)}, u32[]{:S(2)}, u32[]{:S(2)}) collective-permute-start(bf16[4,128,256]{2,1,0:T(8,128)(2,1)S(1)} %get-tuple-element.87), channel_id=1, source_target_pairs={{0,16},{16,0},{32,48},{48,32},{64,80},{80,64},{96,112},{112,96},{1... | collective-permute-start | bytes 786440 | tf_op jit(solution)/shard_map/ppermute | solution.py:51
  95.5 12.1 %collective-permute-start.38 = (bf16[4,128,256]{2,1,0:T(8,128)(2,1)S(1)}, bf16[4,128,256]{2,1,0:T(8,128)(2,1)S(1)}, u32[]{:S(2)}, u32[]{:S(2)}) collective-permute-start(bf16[4,128,256]{2,1,0:T(8,128)(2,1)S(1)} %get-tuple-element.84), channel_id=1, source_target_pairs={{0,32},{16,48},{32,64},{48,80},{64,96},{80,112},{96,0},{112,16},{1... | collective-permute-start | bytes 786440 | tf_op jit(solution)/shard_map/ppermute | solution.py:43
  96.9 10.7 %collective-permute-start.39 = (bf16[4,128,256]{2,1,0:T(8,128)(2,1)S(1)}, bf16[4,128,256]{2,1,0:T(8,128)(2,1)S(1)}, u32[]{:S(2)}, u32[]{:S(2)}) collective-permute-start(bf16[4,128,256]{2,1,0:T(8,128)(2,1)S(1)} %get-tuple-element.85), channel_id=1, source_target_pairs={{0,96},{16,112},{32,0},{48,16},{64,32},{80,48},{96,64},{112,80},{1... | collective-permute-start | bytes 786440 | tf_op jit(solution)/shard_map/ppermute | solution.py:43
  99.3 10.9 %collective-permute-start.42 = (bf16[4,128,256]{2,1,0:T(8,128)(2,1)S(1)}, bf16[4,128,256]{2,1,0:T(8,128)(2,1)S(1)}, u32[]{:S(2)}, u32[]{:S(2)}) collective-permute-start(bf16[4,128,256]{2,1,0:T(8,128)(2,1)S(1)} %get-tuple-element.90), channel_id=1, source_target_pairs={{0,32},{16,48},{32,64},{48,80},{64,96},{80,112},{96,0},{112,16},{1... | collective-permute-start | bytes 786440 | tf_op jit(solution)/shard_map/ppermute | solution.py:43
  99.8 11.8 %collective-permute-start.43 = (bf16[4,128,256]{2,1,0:T(8,128)(2,1)S(1)}, bf16[4,128,256]{2,1,0:T(8,128)(2,1)S(1)}, u32[]{:S(2)}, u32[]{:S(2)}) collective-permute-start(bf16[4,128,256]{2,1,0:T(8,128)(2,1)S(1)} %get-tuple-element.91), channel_id=1, source_target_pairs={{0,96},{16,112},{32,0},{48,16},{64,32},{80,48},{96,64},{112,80},{1... | collective-permute-start | bytes 786440 | tf_op jit(solution)/shard_map/ppermute | solution.py:43
  107.6 9.6 %collective-permute-start.49 = (bf16[2,128,256]{2,1,0:T(8,128)(2,1)S(1)}, bf16[2,128,256]{2,1,0:T(8,128)(2,1)S(1)}, u32[]{:S(2)}, u32[]{:S(2)}) collective-permute-start(bf16[2,128,256]{2,1,0:T(8,128)(2,1)S(1)} %add_convert_fusion.10), channel_id=1, source_target_pairs={{0,4},{1,5},{2,6},{3,7},{4,8},{5,9},{6,10},{7,11},{8,12},{9,13},{1... | collective-permute-start | bytes 393224 | tf_op jit(solution)/shard_map/ppermute | solution.py:55
  107.7 9.5 %collective-permute-start.48 = (bf16[2,128,256]{2,1,0:T(8,128)(2,1)S(1)}, bf16[2,128,256]{2,1,0:T(8,128)(2,1)S(1)}, u32[]{:S(2)}, u32[]{:S(2)}) collective-permute-start(bf16[2,128,256]{2,1,0:T(8,128)(2,1)S(1)} %add_convert_fusion.10), channel_id=1, source_target_pairs={{0,8},{1,9},{2,10},{3,11},{4,12},{5,13},{6,14},{7,15},{8,0},{9,1},... | collective-permute-start | bytes 393224 | tf_op jit(solution)/shard_map/ppermute | solution.py:55
  (29 other events, 202.1 us)

commit v5 on v4

--- a/solution.py
+++ b/solution.py
@@ -243,7 +243,7 @@
     two = yh_swap(add(mine[5], other[5]))
     up, down = x_send(add(mine[3], other[3]), 1), x_send(add(mine[7], other[7]), -1)
     own_up, own_down = x_send(add(mine[2], other[2]), 1), x_send(add(mine[6], other[6]), -1)
-    across = x_send(after(add(mine[4], other[4], two), own_up, own_down), 2)
+    across = x_send(add(mine[4], other[4], two), 2)
     far = yh_swap(add(mine[1], other[1], up, down))
     terms = [mine[0], other[0], own_up, own_down, across, far]
     scale = 1.0 / math.sqrt(features.shape[0] * lax.axis_size("row") * lax.axis_size("col"))
@@ -259,6 +259,7 @@
     term = add(own_rider[4:], after(far_rider[4:], up, down))
     near_term = z_pair(term, 1)
     term, near_term, *ready = lax.optimization_barrier((term, near_term, *pieces))
+    ready = pieces
     term = add(term, near_term)
     pieces = [*ready, *(core_swap(v) for v in ready)]
     term = add(term, core_swap(term))

time: 121 us -> 120 us (level)
  starting transfers between devices: 63.5 us -> 58.1 us
  waiting for transfers between devices: 42.2 us -> 47.4 us
    ppermute x4, waiting for transfers between devices: 1.27 us -> 8.88 us  [yh_swap(): return lax.ppermute(v, 'col', yh_perm())]
    ppermute x13, waiting for transfers between devices: 24.3 us -> 17.7 us  [x_send(): return lax.ppermute(v, 'col', x_perm(step))]
    ppermute x10, waiting for transfers between devices: 10.3 us -> 15.2 us  [z_send(): return lax.ppermute(v, 'row', z_perm(step))]
    ppermute x13, starting transfers between devices: 19.5 us -> 17.5 us  [x_send(): return lax.ppermute(v, 'col', x_perm(step))]
    ppermute x4, starting transfers between devices: 10.4 us -> 8.92 us  [yh_swap(): return lax.ppermute(v, 'col', yh_perm())]
  transfers between devices with their start and end apart: 51 -> 51, of which waited for: 20 -> 21; matrix products, arithmetic and copies ran while one was open for 2% -> 2% of each run, Pallas kernels for 3% -> 3%
where the time goes in v5:
time: 120 us; the launch traced here: 119 us
  starting transfers between devices  58.1 us (48%)
  waiting for transfers between devices  47.4 us (40%)
  Pallas kernels  8.92 us (7%)
  other arithmetic  3.28 us (3%)
  between operations  1.55 us (1%)
    ppermute x10, starting transfers between devices, z_send(): return lax.ppermute(v, 'row', z_perm(step))  18.8 us
    ppermute x13, waiting for transfers between devices, x_send(): return lax.ppermute(v, 'col', x_perm(step))  17.7 us
    ppermute x13, starting transfers between devices, x_send(): return lax.ppermute(v, 'col', x_perm(step))  17.5 us
    ppermute x10, waiting for transfers between devices, z_send(): return lax.ppermute(v, 'row', z_perm(step))  15.2 us
    ppermute x4, starting transfers between devices, yh_swap(): return lax.ppermute(v, 'col', yh_perm())  8.92 us
    ppermute x4, waiting for transfers between devices, yh_swap(): return lax.ppermute(v, 'col', yh_perm())  8.88 us
    pallas_call x2, Pallas kernels, cell_product(): pl.pallas_call(functools.partial(cell_kernel, transposed, len(pieces), n_...  7.82 us
    ppermute x5, starting transfers between devices, yl_swap(): return lax.ppermute(v, 'row', yl_perm())  4.77 us
  transfers between devices with their start and end apart: 51, of which 21 were waited for; matrix products, arithmetic and copies ran while one was open for 2% of the time, Pallas kernels for 3%

profile of v5, /device:TPU:0, one launch (start us, length us, event | category | flops | bytes accessed | tf_op | source)
XLA Modules:
  0.0 119.3 jit_solution(8458771321946310457)
XLA Ops:
  2.4 3.9 %collective-permute-start.3 = (bf16[4,128,256]{2,1,0:T(8,128)(2,1)}, bf16[4,128,256]{2,1,0:T(8,128)(2,1)S(1)}, u32[]{:S(2)}, u32[]{:S(2)}) collective-permute-start(bf16[4,128,256]{2,1,0:T(8,128)(2,1)} %bitcast.42), channel_id=1, source_target_pairs={{0,64},{16,80},{32,96},{48,112},{64,0},{80,16},{96,32},{112,48},{1... | collective-permute-start | bytes 786440 | tf_op jit(solution)/shard_map/ppermute | solution.py:43
  7.3 2.2 %collective-permute-start.1 = (bf16[4,128,256]{2,1,0:T(8,128)(2,1)}, bf16[4,128,256]{2,1,0:T(8,128)(2,1)S(1)}, u32[]{:S(2)}, u32[]{:S(2)}) collective-permute-start(bf16[4,128,256]{2,1,0:T(8,128)(2,1)} %bitcast.44), channel_id=1, source_target_pairs={{0,96},{16,112},{32,0},{48,16},{64,32},{80,48},{96,64},{112,80},{1... | collective-permute-start | bytes 786440 | tf_op jit(solution)/shard_map/ppermute | solution.py:43
  11.0 3.2 %collective-permute-start.2 = (bf16[4,128,256]{2,1,0:T(8,128)(2,1)S(1)}, bf16[4,128,256]{2,1,0:T(8,128)(2,1)S(1)}, u32[]{:S(2)}, u32[]{:S(2)}) collective-permute-start(bf16[4,128,256]{2,1,0:T(8,128)(2,1)S(1)} %collective-permute-done.rest_1_), channel_id=1, source_target_pairs={{0,96},{16,112},{32,0},{48,16},{64,32},{80,48},{96,64},{112,80},{1... | collective-permute-start | bytes 786440 | tf_op jit(solution)/shard_map/ppermute | solution.py:43
  14.7 4.3 %collective-permute-done.5.rest_6_ = bf16[4,128,256]{2,1,0:T(8,128)(2,1)S(1)} collective-permute-done((bf16[4,128,256]{2,1,0:T(8,128)(2,1)}, bf16[4,128,256]{2,1,0:T(8,128)(2,1)S(1)}, u32[]{:S(2)}, u32[]{:S(2)}) %collective-permute-start.5) | collective-permute-done | bytes 262176 | tf_op jit(solution)/shard_map/ppermute | solution.py:43
  20.6 3.2 %collective-permute-done.6.rest_7_ = bf16[4,128,256]{2,1,0:T(8,128)(2,1)S(1)} collective-permute-done((bf16[4,128,256]{2,1,0:T(8,128)(2,1)S(1)}, bf16[4,128,256]{2,1,0:T(8,128)(2,1)S(1)}, u32[]{:S(2)}, u32[]{:S(2)}) %collective-permute-start.6) | collective-permute-done | bytes 262176 | tf_op jit(solution)/shard_map/ppermute | solution.py:43
  24.5 4.0 %forward_cell.1 = (bf16[4,128,256]{2,1,0:T(8,128)(2,1)S(1)}, bf16[4,128,256]{2,1,0:T(8,128)(2,1)S(1)}, bf16[4,128,256]{2,1,0:T(8,128)(2,1)S(1)}, bf16[4,128,256]...) custom-call(s32[128]{0:T(128)S(1)} %fusion.19.out_ref, ...), custom_call_target="tpu_custom_call" | custom-call | flops 1073741824 | bytes 10485760 | tf_op jit(solution)/shard_map/forward_cell/pallas_call | solution.py:132
  31.7 2.5 %collective-permute-start.20 = (bf16[4,128,256]{2,1,0:T(8,128)(2,1)S(1)}, bf16[4,128,256]{2,1,0:T(8,128)(2,1)S(1)}, u32[]{:S(2)}, u32[]{:S(2)}) collective-permute-start(bf16[4,128,256]{2,1,0:T(8,128)(2,1)S(1)} %add_convert_fusion.4), channel_id=1, source_target_pairs={{0,12},{1,13},{2,14},{3,15},{4,0},{5,1},{6,2},{7,3},{8,4},{9,5},{1... | collective-permute-start | bytes 786440 | tf_op jit(solution)/shard_map/ppermute | solution.py:55
  34.3 3.0 %collective-permute-start.15 = (bf16[4,128,256]{2,1,0:T(8,128)(2,1)S(1)}, bf16[4,128,256]{2,1,0:T(8,128)(2,1)S(1)}, u32[]{:S(2)}, u32[]{:S(2)}) collective-permute-start(bf16[4,128,256]{2,1,0:T(8,128)(2,1)S(1)} %add_convert_fusion.7), channel_id=1, source_target_pairs={{0,2},{1,3},{2,0},{3,1},{4,6},{5,7},{6,4},{7,5},{8,10},{9,11},{10,... | collective-permute-start | bytes 786440 | tf_op jit(solution)/shard_map/ppermute | solution.py:59
  37.6 6.3 %collective-permute-done.15 = bf16[4,128,256]{2,1,0:T(8,128)(2,1)S(1)} collective-permute-done((bf16[4,128,256]{2,1,0:T(8,128)(2,1)S(1)}, bf16[4,128,256]{2,1,0:T(8,128)(2,1)S(1)}, u32[]{:S(2)}, u32[]{:S(2)}) %collective-permute-start.15) | collective-permute-done | bytes 262176 | tf_op jit(solution)/shard_map/ppermute | solution.py:59
  44.1 3.3 %collective-permute-start.12 = (bf16[4,128,256]{2,1,0:T(8,128)(2,1)S(1)}, bf16[4,128,256]{2,1,0:T(8,128)(2,1)S(1)}, u32[]{:S(2)}, u32[]{:S(2)}) collective-permute-start(bf16[4,128,256]{2,1,0:T(8,128)(2,1)S(1)} %add_convert_fusion.8), channel_id=1, source_target_pairs={{0,12},{1,13},{2,14},{3,15},{4,0},{5,1},{6,2},{7,3},{8,4},{9,5},{1... | collective-permute-start | bytes 786440 | tf_op jit(solution)/shard_map/ppermute | solution.py:55
  47.6 3.0 %collective-permute-start.21 = (bf16[4,128,256]{2,1,0:T(8,128)(2,1)S(1)}, bf16[4,128,256]{2,1,0:T(8,128)(2,1)S(1)}, u32[]{:S(2)}, u32[]{:S(2)}) collective-permute-start(bf16[4,128,256]{2,1,0:T(8,128)(2,1)S(1)} %add_convert_fusion.3), channel_id=1, source_target_pairs={{0,2},{1,3},{2,0},{3,1},{4,6},{5,7},{6,4},{7,5},{8,10},{9,11},{10,... | collective-permute-start | bytes 786440 | tf_op jit(solution)/shard_map/ppermute | solution.py:59
  50.5 7.5 %collective-permute-done.10.refs_2_ = bf16[4,128,256]{2,1,0:T(8,128)(2,1)S(1)} collective-permute-done((bf16[4,128,256]{2,1,0:T(8,128)(2,1)S(1)}, bf16[4,128,256]{2,1,0:T(8,128)(2,1)S(1)}, u32[]{:S(2)}, u32[]{:S(2)}) %collective-permute-start.10) | collective-permute-done | bytes 262176 | tf_op jit(solution)/shard_map/ppermute | solution.py:55
  59.1 2.9 %collective-permute-start.22 = (bf16[6,128,256]{2,1,0:T(8,128)(2,1)S(1)}, bf16[6,128,256]{2,1,0:T(8,128)(2,1)S(1)}, u32[]{:S(2)}, u32[]{:S(2)}) collective-permute-start(bf16[6,128,256]{2,1,0:T(8,128)(2,1)S(1)} %get-tuple-element.63), channel_id=1, source_target_pairs={{0,2},{1,3},{2,0},{3,1},{4,6},{5,7},{6,4},{7,5},{8,10},{9,11},{10,... | collective-permute-start | bytes 1179656 | tf_op jit(solution)/shard_map/ppermute | solution.py:59
  63.0 3.0 %collective-permute-start.27 = (bf16[4,128,256]{2,1,0:T(8,128)(2,1)S(1)}, bf16[4,128,256]{2,1,0:T(8,128)(2,1)S(1)}, u32[]{:S(2)}, u32[]{:S(2)}) collective-permute-start(bf16[4,128,256]{2,1,0:T(8,128)(2,1)S(1)} %get-tuple-element.62.rest_0_), channel_id=1, source_target_pairs={{0,4},{1,5},{2,6},{3,7},{4,8},{5,9},{6,10},{7,11},{8,12},{9,13},{1... | collective-permute-start | bytes 786440 | tf_op jit(solution)/shard_map/ppermute | solution.py:55
  66.3 6.5 %collective-permute-done.25.rest_4_ = bf16[4,128,256]{2,1,0:T(8,128)(2,1)S(1)} collective-permute-done((bf16[4,128,256]{2,1,0:T(8,128)(2,1)S(1)}, bf16[4,128,256]{2,1,0:T(8,128)(2,1)S(1)}, u32[]{:S(2)}, u32[]{:S(2)}) %collective-permute-start.25) | collective-permute-done | bytes 262176 | tf_op jit(solution)/shard_map/ppermute | solution.py:55
  74.2 2.0 %collective-permute-start.24 = (bf16[4,128,256]{2,1,0:T(8,128)(2,1)S(1)}, bf16[4,128,256]{2,1,0:T(8,128)(2,1)S(1)}, u32[]{:S(2)}, u32[]{:S(2)}) collective-permute-start(bf16[4,128,256]{2,1,0:T(8,128)(2,1)S(1)} %slice.12.rest_1_), channel_id=1, source_target_pairs={{0,12},{1,13},{2,14},{3,15},{4,0},{5,1},{6,2},{7,3},{8,4},{9,5},{1... | collective-permute-start | bytes 786440 | tf_op jit(solution)/shard_map/ppermute | solution.py:55
  78.1 2.5 %collective-permute-done.26.rest_5_ = bf16[4,128,256]{2,1,0:T(8,128)(2,1)S(1)} collective-permute-done((bf16[4,128,256]{2,1,0:T(8,128)(2,1)S(1)}, bf16[4,128,256]{2,1,0:T(8,128)(2,1)S(1)}, u32[]{:S(2)}, u32[]{:S(2)}) %collective-permute-start.26) | collective-permute-done | bytes 262176 | tf_op jit(solution)/shard_map/ppermute | solution.py:59
  84.3 2.9 %collective-permute-start.46 = (bf16[2,128,256]{2,1,0:T(8,128)(2,1)S(1)}, bf16[2,128,256]{2,1,0:T(8,128)(2,1)S(1)}, u32[]{:S(2)}, u32[]{:S(2)}) collective-permute-start(bf16[2,128,256]{2,1,0:T(8,128)(2,1)S(1)} %add_convert_fusion.12), channel_id=1, source_target_pairs={{0,64},{16,80},{32,96},{48,112},{64,0},{80,16},{96,32},{112,48},{1... | collective-permute-start | bytes 393224 | tf_op jit(solution)/shard_map/ppermute | solution.py:47
  87.2 3.8 %backward_cell.1 = (bf16[4,128,256]{2,1,0:T(8,128)(2,1)S(1)}, bf16[4,128,256]{2,1,0:T(8,128)(2,1)S(1)}, bf16[4,128,256]{2,1,0:T(8,128)(2,1)S(1)}, bf16[4,128,256...) custom-call(s32[128]{0:T(128)S(1)} %get-tuple-element.81.out_ref, ...), custom_call_target="tpu_custom_call" | custom-call | flops 1073741824 | bytes 10485760 | tf_op jit(solution)/shard_map/backward_cell/pallas_call | solution.py:132
  93.5 2.2 %collective-permute-start.37 = (bf16[4,128,256]{2,1,0:T(8,128)(2,1)S(1)}, bf16[4,128,256]{2,1,0:T(8,128)(2,1)S(1)}, u32[]{:S(2)}, u32[]{:S(2)}) collective-permute-start(bf16[4,128,256]{2,1,0:T(8,128)(2,1)S(1)} %get-tuple-element.65), channel_id=1, source_target_pairs={{0,32},{16,48},{32,64},{48,80},{64,96},{80,112},{96,0},{112,16},{1... | collective-permute-start | bytes 786440 | tf_op jit(solution)/shard_map/ppermute | solution.py:43
  97.8 3.2 %collective-permute-start.42 = (bf16[4,128,256]{2,1,0:T(8,128)(2,1)S(1)}, bf16[4,128,256]{2,1,0:T(8,128)(2,1)S(1)}, u32[]{:S(2)}, u32[]{:S(2)}) collective-permute-start(bf16[4,128,256]{2,1,0:T(8,128)(2,1)S(1)} %get-tuple-element.72), channel_id=1, source_target_pairs={{0,96},{16,112},{32,0},{48,16},{64,32},{80,48},{96,64},{112,80},{1... | collective-permute-start | bytes 786440 | tf_op jit(solution)/shard_map/ppermute | solution.py:43
  101.1 2.4 %collective-permute-done.39 = bf16[4,128,256]{2,1,0:T(8,128)(2,1)S(1)} collective-permute-done((bf16[4,128,256]{2,1,0:T(8,128)(2,1)S(1)}, bf16[4,128,256]{2,1,0:T(8,128)(2,1)S(1)}, u32[]{:S(2)}, u32[]{:S(2)}) %collective-permute-start.39) | collective-permute-done | bytes 262176 | tf_op jit(solution)/shard_map/ppermute | solution.py:51
  105.6 2.0 %collective-permute-start.48 = (bf16[2,128,256]{2,1,0:T(8,128)(2,1)S(1)}, bf16[2,128,256]{2,1,0:T(8,128)(2,1)S(1)}, u32[]{:S(2)}, u32[]{:S(2)}) collective-permute-start(bf16[2,128,256]{2,1,0:T(8,128)(2,1)S(1)} %add_convert_fusion.10), channel_id=1, source_target_pairs={{0,8},{1,9},{2,10},{3,11},{4,12},{5,13},{6,14},{7,15},{8,0},{9,1},... | collective-permute-start | bytes 393224 | tf_op jit(solution)/shard_map/ppermute | solution.py:55
  114.2 4.2 %collective-permute-done.40 = bf16[4,128,256]{2,1,0:T(8,128)(2,1)S(1)} collective-permute-done((bf16[4,128,256]{2,1,0:T(8,128)(2,1)S(1)}, bf16[4,128,256]{2,1,0:T(8,128)(2,1)S(1)}, u32[]{:S(2)}, u32[]{:S(2)}) %collective-permute-start.40) | collective-permute-done | bytes 262176 | tf_op jit(solution)/shard_map/ppermute | solution.py:43
  (106 shorter events, 33.8 us)
Async XLA Ops:
  0.6 10.2 %collective-permute-start = (bf16[4,128,256]{2,1,0:T(8,128)(2,1)}, bf16[4,128,256]{2,1,0:T(8,128)(2,1)S(1)}, u32[]{:S(2)}, u32[]{:S(2)}) collective-permute-start(bf16[4,128,256]{2,1,0:T(8,128)(2,1)} %bitcast.41), channel_id=1, source_target_pairs={{0,16},{16,0},{32,48},{48,32},{64,80},{80,64},{96,112},{112,96},{1... | collective-permute-start | bytes 786440 | tf_op jit(solution)/shard_map/ppermute | solution.py:51
  2.4 11.8 %collective-permute-start.3 = (bf16[4,128,256]{2,1,0:T(8,128)(2,1)}, bf16[4,128,256]{2,1,0:T(8,128)(2,1)S(1)}, u32[]{:S(2)}, u32[]{:S(2)}) collective-permute-start(bf16[4,128,256]{2,1,0:T(8,128)(2,1)} %bitcast.42), channel_id=1, source_target_pairs={{0,64},{16,80},{32,96},{48,112},{64,0},{80,16},{96,32},{112,48},{1... | collective-permute-start | bytes 786440 | tf_op jit(solution)/shard_map/ppermute | solution.py:43
  6.2 12.7 %collective-permute-start.5 = (bf16[4,128,256]{2,1,0:T(8,128)(2,1)}, bf16[4,128,256]{2,1,0:T(8,128)(2,1)S(1)}, u32[]{:S(2)}, u32[]{:S(2)}) collective-permute-start(bf16[4,128,256]{2,1,0:T(8,128)(2,1)} %bitcast.43), channel_id=1, source_target_pairs={{0,32},{16,48},{32,64},{48,80},{64,96},{80,112},{96,0},{112,16},{1... | collective-permute-start | bytes 786440 | tf_op jit(solution)/shard_map/ppermute | solution.py:43
  7.3 13.1 %collective-permute-start.1 = (bf16[4,128,256]{2,1,0:T(8,128)(2,1)}, bf16[4,128,256]{2,1,0:T(8,128)(2,1)S(1)}, u32[]{:S(2)}, u32[]{:S(2)}) collective-permute-start(bf16[4,128,256]{2,1,0:T(8,128)(2,1)} %bitcast.44), channel_id=1, source_target_pairs={{0,96},{16,112},{32,0},{48,16},{64,32},{80,48},{96,64},{112,80},{1... | collective-permute-start | bytes 786440 | tf_op jit(solution)/shard_map/ppermute | solution.py:43
  10.9 12.9 %collective-permute-start.6 = (bf16[4,128,256]{2,1,0:T(8,128)(2,1)S(1)}, bf16[4,128,256]{2,1,0:T(8,128)(2,1)S(1)}, u32[]{:S(2)}, u32[]{:S(2)}) collective-permute-start(bf16[4,128,256]{2,1,0:T(8,128)(2,1)S(1)} %collective-permute-done.rest_1_), channel_id=1, source_target_pairs={{0,32},{16,48},{32,64},{48,80},{64,96},{80,112},{96,0},{112,16},{1... | collective-permute-start | bytes 786440 | tf_op jit(solution)/shard_map/ppermute | solution.py:43
  11.0 13.5 %collective-permute-start.2 = (bf16[4,128,256]{2,1,0:T(8,128)(2,1)S(1)}, bf16[4,128,256]{2,1,0:T(8,128)(2,1)S(1)}, u32[]{:S(2)}, u32[]{:S(2)}) collective-permute-start(bf16[4,128,256]{2,1,0:T(8,128)(2,1)S(1)} %collective-permute-done.rest_1_), channel_id=1, source_target_pairs={{0,96},{16,112},{32,0},{48,16},{64,32},{80,48},{96,64},{112,80},{1... | collective-permute-start | bytes 786440 | tf_op jit(solution)/shard_map/ppermute | solution.py:43
  31.4 12.7 %collective-permute-start.17 = (bf16[4,128,256]{2,1,0:T(8,128)(2,1)S(1)}, bf16[4,128,256]{2,1,0:T(8,128)(2,1)S(1)}, u32[]{:S(2)}, u32[]{:S(2)}) collective-permute-start(bf16[4,128,256]{2,1,0:T(8,128)(2,1)S(1)} %get-tuple-element.57), channel_id=1, source_target_pairs={{0,1},{1,0},{2,3},{3,2},{4,5},{5,4},{6,7},{7,6},{8,9},{9,8},{10,11... | collective-permute-start | bytes 786440 | tf_op jit(solution)/shard_map/ppermute | solution.py:63
  31.7 15.7 %collective-permute-start.20 = (bf16[4,128,256]{2,1,0:T(8,128)(2,1)S(1)}, bf16[4,128,256]{2,1,0:T(8,128)(2,1)S(1)}, u32[]{:S(2)}, u32[]{:S(2)}) collective-permute-start(bf16[4,128,256]{2,1,0:T(8,128)(2,1)S(1)} %add_convert_fusion.4), channel_id=1, source_target_pairs={{0,12},{1,13},{2,14},{3,15},{4,0},{5,1},{6,2},{7,3},{8,4},{9,5},{1... | collective-permute-start | bytes 786440 | tf_op jit(solution)/shard_map/ppermute | solution.py:55
  34.3 9.7 %collective-permute-start.15 = (bf16[4,128,256]{2,1,0:T(8,128)(2,1)S(1)}, bf16[4,128,256]{2,1,0:T(8,128)(2,1)S(1)}, u32[]{:S(2)}, u32[]{:S(2)}) collective-permute-start(bf16[4,128,256]{2,1,0:T(8,128)(2,1)S(1)} %add_convert_fusion.7), channel_id=1, source_target_pairs={{0,2},{1,3},{2,0},{3,1},{4,6},{5,7},{6,4},{7,5},{8,10},{9,11},{10,... | collective-permute-start | bytes 786440 | tf_op jit(solution)/shard_map/ppermute | solution.py:59
  37.4 10.0 %collective-permute-start.19 = (bf16[4,128,256]{2,1,0:T(8,128)(2,1)S(1)}, bf16[4,128,256]{2,1,0:T(8,128)(2,1)S(1)}, u32[]{:S(2)}, u32[]{:S(2)}) collective-permute-start(bf16[4,128,256]{2,1,0:T(8,128)(2,1)S(1)} %add_convert_fusion.5), channel_id=1, source_target_pairs={{0,4},{1,5},{2,6},{3,7},{4,8},{5,9},{6,10},{7,11},{8,12},{9,13},{1... | collective-permute-start | bytes 786440 | tf_op jit(solution)/shard_map/ppermute | solution.py:55
  37.5 13.0 %collective-permute-start.8 = (bf16[4,128,256]{2,1,0:T(8,128)(2,1)S(1)}, bf16[4,128,256]{2,1,0:T(8,128)(2,1)S(1)}, u32[]{:S(2)}, u32[]{:S(2)}) collective-permute-start(bf16[4,128,256]{2,1,0:T(8,128)(2,1)S(1)} %get-tuple-element.43), channel_id=1, source_target_pairs={{0,1},{1,0},{2,3},{3,2},{4,5},{5,4},{6,7},{7,6},{8,9},{9,8},{10,11... | collective-permute-start | bytes 786440 | tf_op jit(solution)/shard_map/ppermute | solution.py:63
  44.0 14.0 %collective-permute-start.10 = (bf16[4,128,256]{2,1,0:T(8,128)(2,1)S(1)}, bf16[4,128,256]{2,1,0:T(8,128)(2,1)S(1)}, u32[]{:S(2)}, u32[]{:S(2)}) collective-permute-start(bf16[4,128,256]{2,1,0:T(8,128)(2,1)S(1)} %add_convert_fusion.9), channel_id=1, source_target_pairs={{0,4},{1,5},{2,6},{3,7},{4,8},{5,9},{6,10},{7,11},{8,12},{9,13},{1... | collective-permute-start | bytes 786440 | tf_op jit(solution)/shard_map/ppermute | solution.py:55
  44.1 13.9 %collective-permute-start.12 = (bf16[4,128,256]{2,1,0:T(8,128)(2,1)S(1)}, bf16[4,128,256]{2,1,0:T(8,128)(2,1)S(1)}, u32[]{:S(2)}, u32[]{:S(2)}) collective-permute-start(bf16[4,128,256]{2,1,0:T(8,128)(2,1)S(1)} %add_convert_fusion.8), channel_id=1, source_target_pairs={{0,12},{1,13},{2,14},{3,15},{4,0},{5,1},{6,2},{7,3},{8,4},{9,5},{1... | collective-permute-start | bytes 786440 | tf_op jit(solution)/shard_map/ppermute | solution.py:55
  47.4 10.6 %collective-permute-start.16 = (bf16[4,128,256]{2,1,0:T(8,128)(2,1)S(1)}, bf16[4,128,256]{2,1,0:T(8,128)(2,1)S(1)}, u32[]{:S(2)}, u32[]{:S(2)}) collective-permute-start(bf16[4,128,256]{2,1,0:T(8,128)(2,1)S(1)} %add_convert_fusion.6), channel_id=1, source_target_pairs={{0,8},{1,9},{2,10},{3,11},{4,12},{5,13},{6,14},{7,15},{8,0},{9,1},... | collective-permute-start | bytes 786440 | tf_op jit(solution)/shard_map/ppermute | solution.py:55
  47.6 10.5 %collective-permute-start.21 = (bf16[4,128,256]{2,1,0:T(8,128)(2,1)S(1)}, bf16[4,128,256]{2,1,0:T(8,128)(2,1)S(1)}, u32[]{:S(2)}, u32[]{:S(2)}) collective-permute-start(bf16[4,128,256]{2,1,0:T(8,128)(2,1)S(1)} %add_convert_fusion.3), channel_id=1, source_target_pairs={{0,2},{1,3},{2,0},{3,1},{4,6},{5,7},{6,4},{7,5},{8,10},{9,11},{10,... | collective-permute-start | bytes 786440 | tf_op jit(solution)/shard_map/ppermute | solution.py:59
  59.1 13.7 %collective-permute-start.22 = (bf16[6,128,256]{2,1,0:T(8,128)(2,1)S(1)}, bf16[6,128,256]{2,1,0:T(8,128)(2,1)S(1)}, u32[]{:S(2)}, u32[]{:S(2)}) collective-permute-start(bf16[6,128,256]{2,1,0:T(8,128)(2,1)S(1)} %get-tuple-element.63), channel_id=1, source_target_pairs={{0,2},{1,3},{2,0},{3,1},{4,6},{5,7},{6,4},{7,5},{8,10},{9,11},{10,... | collective-permute-start | bytes 1179656 | tf_op jit(solution)/shard_map/ppermute | solution.py:59
  62.0 10.8 %collective-permute-start.25 = (bf16[4,128,256]{2,1,0:T(8,128)(2,1)S(1)}, bf16[4,128,256]{2,1,0:T(8,128)(2,1)S(1)}, u32[]{:S(2)}, u32[]{:S(2)}) collective-permute-start(bf16[4,128,256]{2,1,0:T(8,128)(2,1)S(1)} %get-tuple-element.62.rest_0_), channel_id=1, source_target_pairs={{0,8},{1,9},{2,10},{3,11},{4,12},{5,13},{6,14},{7,15},{8,0},{9,1},... | collective-permute-start | bytes 786440 | tf_op jit(solution)/shard_map/ppermute | solution.py:55
  63.0 13.2 %collective-permute-start.27 = (bf16[4,128,256]{2,1,0:T(8,128)(2,1)S(1)}, bf16[4,128,256]{2,1,0:T(8,128)(2,1)S(1)}, u32[]{:S(2)}, u32[]{:S(2)}) collective-permute-start(bf16[4,128,256]{2,1,0:T(8,128)(2,1)S(1)} %get-tuple-element.62.rest_0_), channel_id=1, source_target_pairs={{0,4},{1,5},{2,6},{3,7},{4,8},{5,9},{6,10},{7,11},{8,12},{9,13},{1... | collective-permute-start | bytes 786440 | tf_op jit(solution)/shard_map/ppermute | solution.py:55
  66.0 11.0 %collective-permute-start.23 = (bf16[4,128,256]{2,1,0:T(8,128)(2,1)S(1)}, bf16[4,128,256]{2,1,0:T(8,128)(2,1)S(1)}, u32[]{:S(2)}, u32[]{:S(2)}) collective-permute-start(bf16[4,128,256]{2,1,0:T(8,128)(2,1)S(1)} %get-tuple-element.62.rest_0_), channel_id=1, source_target_pairs={{0,12},{1,13},{2,14},{3,15},{4,0},{5,1},{6,2},{7,3},{8,4},{9,5},{1... | collective-permute-start | bytes 786440 | tf_op jit(solution)/shard_map/ppermute | solution.py:55
  91.9 11.6 %collective-permute-start.39 = (bf16[4,128,256]{2,1,0:T(8,128)(2,1)S(1)}, bf16[4,128,256]{2,1,0:T(8,128)(2,1)S(1)}, u32[]{:S(2)}, u32[]{:S(2)}) collective-permute-start(bf16[4,128,256]{2,1,0:T(8,128)(2,1)S(1)} %get-tuple-element.68), channel_id=1, source_target_pairs={{0,16},{16,0},{32,48},{48,32},{64,80},{80,64},{96,112},{112,96},{1... | collective-permute-start | bytes 786440 | tf_op jit(solution)/shard_map/ppermute | solution.py:51
  93.5 10.8 %collective-permute-start.37 = (bf16[4,128,256]{2,1,0:T(8,128)(2,1)S(1)}, bf16[4,128,256]{2,1,0:T(8,128)(2,1)S(1)}, u32[]{:S(2)}, u32[]{:S(2)}) collective-permute-start(bf16[4,128,256]{2,1,0:T(8,128)(2,1)S(1)} %get-tuple-element.65), channel_id=1, source_target_pairs={{0,32},{16,48},{32,64},{48,80},{64,96},{80,112},{96,0},{112,16},{1... | collective-permute-start | bytes 786440 | tf_op jit(solution)/shard_map/ppermute | solution.py:43
  95.7 9.9 %collective-permute-start.38 = (bf16[4,128,256]{2,1,0:T(8,128)(2,1)S(1)}, bf16[4,128,256]{2,1,0:T(8,128)(2,1)S(1)}, u32[]{:S(2)}, u32[]{:S(2)}) collective-permute-start(bf16[4,128,256]{2,1,0:T(8,128)(2,1)S(1)} %get-tuple-element.66), channel_id=1, source_target_pairs={{0,96},{16,112},{32,0},{48,16},{64,32},{80,48},{96,64},{112,80},{1... | collective-permute-start | bytes 786440 | tf_op jit(solution)/shard_map/ppermute | solution.py:43
  96.8 12.2 %collective-permute-start.41 = (bf16[4,128,256]{2,1,0:T(8,128)(2,1)S(1)}, bf16[4,128,256]{2,1,0:T(8,128)(2,1)S(1)}, u32[]{:S(2)}, u32[]{:S(2)}) collective-permute-start(bf16[4,128,256]{2,1,0:T(8,128)(2,1)S(1)} %get-tuple-element.71), channel_id=1, source_target_pairs={{0,32},{16,48},{32,64},{48,80},{64,96},{80,112},{96,0},{112,16},{1... | collective-permute-start | bytes 786440 | tf_op jit(solution)/shard_map/ppermute | solution.py:43
  97.8 12.1 %collective-permute-start.42 = (bf16[4,128,256]{2,1,0:T(8,128)(2,1)S(1)}, bf16[4,128,256]{2,1,0:T(8,128)(2,1)S(1)}, u32[]{:S(2)}, u32[]{:S(2)}) collective-permute-start(bf16[4,128,256]{2,1,0:T(8,128)(2,1)S(1)} %get-tuple-element.72), channel_id=1, source_target_pairs={{0,96},{16,112},{32,0},{48,16},{64,32},{80,48},{96,64},{112,80},{1... | collective-permute-start | bytes 786440 | tf_op jit(solution)/shard_map/ppermute | solution.py:43
  (29 other events, 199.4 us)

commit v6 on v5

--- a/solution.py
+++ b/solution.py
@@ -115,17 +115,20 @@
     for c, load in enumerate(loads):
         load.wait()
         lax.fori_loop(c * size, jnp.clip(groups, c * size, (c + 1) * size), group, 0)
-    for o, out in enumerate(outs):
-        def store(i, carry, out=out, o=o):
-            out[i] = acc[4 * o + i].astype(BF16)
+    first = 0
+    for out in outs:
+        def store(i, carry, out=out, first=first):
+            out[i] = acc[first + i].astype(BF16)
             return carry
 
-        lax.fori_loop(0, 4, store, 0)
-
-
-def cell_product(name, transposed, out_slot, in_slot, count, tiles, pieces, n_out):
+        lax.fori_loop(0, out.shape[0], store, 0)
+        first += out.shape[0]
+
+
+def cell_product(name, transposed, out_slot, in_slot, count, tiles, pieces, sizes):
+    n_out, out_blocks = len(sizes), sum(sizes)
     live = jnp.arange(CAP, dtype=jnp.int32) < count[0]
-    out_slot = jnp.where(live, out_slot, 4 * n_out)
+    out_slot = jnp.where(live, out_slot, out_blocks)
     in_slot = jnp.where(live, in_slot, 0)
     any_spec = pl.BlockSpec(memory_space=pl.ANY)
     vmem_spec = pl.BlockSpec(memory_space=pltpu.VMEM)
@@ -139,16 +142,16 @@
             scratch_shapes=[
                 pltpu.VMEM((CAP, BLK, BLK), BF16),
                 pltpu.VMEM((4 * len(pieces), BLK, WIDTH), BF16),
-                pltpu.VMEM((4 * n_out + 1, BLK, WIDTH), F32),
+                pltpu.VMEM((out_blocks + 1, BLK, WIDTH), F32),
                 pltpu.SemaphoreType.DMA((CHUNKS,)),
                 pltpu.SemaphoreType.DMA((len(pieces),)),
             ],
         ),
-        out_shape=[jax.ShapeDtypeStruct((4, BLK, WIDTH), BF16)] * n_out,
+        out_shape=[jax.ShapeDtypeStruct((size, BLK, WIDTH), BF16) for size in sizes],
         compiler_params=pltpu.CompilerParams(vmem_limit_bytes=(19 if len(pieces) == 8 else 16) * 1024 * 1024),
         cost_estimate=pl.CostEstimate(
             flops=2 * CAP * BLK * BLK * WIDTH,
-            bytes_accessed=2 * CAP * BLK * BLK + 8 * (len(pieces) + n_out) * BLK * WIDTH,
+            bytes_accessed=2 * CAP * BLK * BLK + 2 * (4 * len(pieces) + out_blocks) * BLK * WIDTH,
             transcendentals=0,
         ),
         name=name,
@@ -220,6 +223,9 @@
     own, j = t_row // 4, t_row % 4
     dx, dyh, dk = (own // 4 - x) % 4, (own // 2 % 2) ^ yh, (own % 2) ^ core
     row_slot = dk * 32 + dx * 8 + dyh * 4 + j
+    piece = dx * 2 + dyh
+    rank = sum(jnp.where(piece == i, n, 0) for i, n in enumerate((7, 6, 3, 1, 5, 0, 4, 2)))
+    row_out = jnp.where(dk == 0, row_slot, 32 + rank * 4 + j)
     own, j = t_col // 4, t_col % 4
     dz, dyl = (own // 2 - z) % 4, (own % 2) ^ yl
     col_slot = dz * 8 + dyl * 4 + j
@@ -233,13 +239,20 @@
     own = pltpu.with_memory_space_constraint(own, pltpu.HBM)
     pieces = [own, far, up, far_up, across, far_across, down, far_down]
 
-    parts = cell_product("forward_cell", False, row_slot, col_slot, count, tiles, pieces, 16)
+    parts = cell_product(
+        "forward_cell",
+        False,
+        row_out,
+        col_slot,
+        count,
+        tiles,
+        pieces,
+        [4] * 8 + [4, 8, 8, 4, 4, 4],
+    )
     mine = parts[:8]
-    other = [None] * 8
-    for i in (5, 3, 7):
-        other[i] = core_swap(parts[8 + i])
-    for i in (2, 6, 4, 1, 0):
-        other[i] = core_swap(after(parts[8 + i], other[7]))
+    first, near = core_swap(parts[8]), core_swap(parts[9])
+    own_near, *rest = [core_swap(after(v, near)) for v in parts[10:]]
+    other = [rest[2], rest[1], own_near[:4], near[:4], rest[0], first, own_near[4:], near[4:]]
     two = yh_swap(add(mine[5], other[5]))
     up, down = x_send(add(mine[3], other[3]), 1), x_send(add(mine[7], other[7]), -1)
     own_up, own_down = x_send(add(mine[2], other[2]), 1), x_send(add(mine[6], other[6]), -1)
@@ -264,7 +277,7 @@
     pieces = [*ready, *(core_swap(v) for v in ready)]
     term = add(term, core_swap(term))
     near_term = z_pair(term, 2)
-    back = cell_product("backward_cell", True, col_slot, row_slot, count, tiles, pieces, 8)
+    back = cell_product("backward_cell", True, col_slot, row_slot, count, tiles, pieces, [4] * 8)
     two = yl_swap(back[5])
     up, down = z_send(back[3], 1), z_send(back[7], -1)
     own_up, own_down = z_send(back[2], 1), z_send(back[6], -1)

time: 120 us -> 130 us (1.083)
  starting transfers between devices: 58.1 us -> 64.1 us
  waiting for transfers between devices: 47.4 us -> 50.8 us
  other arithmetic: 3.28 us -> 4.63 us
    ppermute x13, waiting for transfers between devices: 17.7 us -> 25.4 us  [x_send(): return lax.ppermute(v, 'col', x_perm(step))]
    ppermute x13, starting transfers between devices: 17.5 us -> 24.8 us  [x_send(): return lax.ppermute(v, 'col', x_perm(step))]
    ppermute x10, waiting for transfers between devices: 15.2 us -> 12.7 us  [z_send(): return lax.ppermute(v, 'row', z_perm(step))]
    ppermute x4, waiting for transfers between devices: 8.88 us -> 6.7 us  [yh_swap(): return lax.ppermute(v, 'col', yh_perm())]
    ppermute x5, waiting for transfers between devices: 2.65 us -> 1.25 us  [yl_swap(): return lax.ppermute(v, 'row', yl_perm())]
    select_n x1 -> x2, other arithmetic: 0.01 us -> 1.36 us  [cell_product(): out_slot = jnp.where(live, out_slot, out_blocks)]
    ppermute x17 -> x15, starting transfers between devices: 4.11 us -> 2.84 us  [core_swap(): return lax.ppermute(v, 'col', core_perm())]
  transfers between devices with their start and end apart: 51 -> 49, of which waited for: 21 -> 24; matrix products, arithmetic and copies ran while one was open for 2% -> 3% of each run, Pallas kernels for 3% -> 3%
where the time goes in v6:
time: 130 us; the launch traced here: 129 us
  starting transfers between devices  64.1 us (49%)
  waiting for transfers between devices  50.8 us (39%)
  Pallas kernels  7.93 us (6%)
  other arithmetic  4.63 us (4%)
  between operations  1.51 us (1%)
    ppermute x13, waiting for transfers between devices, x_send(): return lax.ppermute(v, 'col', x_perm(step))  25.4 us
    ppermute x13, starting transfers between devices, x_send(): return lax.ppermute(v, 'col', x_perm(step))  24.8 us
    ppermute x10, starting transfers between devices, z_send(): return lax.ppermute(v, 'row', z_perm(step))  19.2 us
    ppermute x10, waiting for transfers between devices, z_send(): return lax.ppermute(v, 'row', z_perm(step))  12.7 us
    ppermute x4, starting transfers between devices, yh_swap(): return lax.ppermute(v, 'col', yh_perm())  7.95 us
    pallas_call x2, Pallas kernels, cell_product(): pl.pallas_call(functools.partial(cell_kernel, transposed, len(pieces), n_...  6.83 us
    ppermute x4, waiting for transfers between devices, yh_swap(): return lax.ppermute(v, 'col', yh_perm())  6.7 us
    ppermute x5, starting transfers between devices, yl_swap(): return lax.ppermute(v, 'row', yl_perm())  5.57 us
  transfers between devices with their start and end apart: 49, of which 24 were waited for; matrix products, arithmetic and copies ran while one was open for 3% of the time, Pallas kernels for 3%

profile of v6, /device:TPU:0, one launch (start us, length us, event | category | flops | bytes accessed | tf_op | source)
XLA Modules:
  0.0 129.1 jit_solution(5488697023619228378)
XLA Ops:
  2.4 3.9 %collective-permute-start.3 = (bf16[4,128,256]{2,1,0:T(8,128)(2,1)}, bf16[4,128,256]{2,1,0:T(8,128)(2,1)S(1)}, u32[]{:S(2)}, u32[]{:S(2)}) collective-permute-start(bf16[4,128,256]{2,1,0:T(8,128)(2,1)} %bitcast.45), channel_id=1, source_target_pairs={{0,64},{16,80},{32,96},{48,112},{64,0},{80,16},{96,32},{112,48},{1... | collective-permute-start | bytes 786440 | tf_op jit(solution)/shard_map/ppermute | solution.py:43
  11.0 3.2 %collective-permute-start.2 = (bf16[4,128,256]{2,1,0:T(8,128)(2,1)S(1)}, bf16[4,128,256]{2,1,0:T(8,128)(2,1)S(1)}, u32[]{:S(2)}, u32[]{:S(2)}) collective-permute-start(bf16[4,128,256]{2,1,0:T(8,128)(2,1)S(1)} %collective-permute-done.rest_1_), channel_id=1, source_target_pairs={{0,96},{16,112},{32,0},{48,16},{64,32},{80,48},{96,64},{112,80},{1... | collective-permute-start | bytes 786440 | tf_op jit(solution)/shard_map/ppermute | solution.py:43
  16.0 2.9 %collective-permute-done.5.rest_6_ = bf16[4,128,256]{2,1,0:T(8,128)(2,1)S(1)} collective-permute-done((bf16[4,128,256]{2,1,0:T(8,128)(2,1)}, bf16[4,128,256]{2,1,0:T(8,128)(2,1)S(1)}, u32[]{:S(2)}, u32[]{:S(2)}) %collective-permute-start.5) | collective-permute-done | bytes 262176 | tf_op jit(solution)/shard_map/ppermute | solution.py:43
  20.5 3.2 %collective-permute-done.6.rest_7_ = bf16[4,128,256]{2,1,0:T(8,128)(2,1)S(1)} collective-permute-done((bf16[4,128,256]{2,1,0:T(8,128)(2,1)S(1)}, bf16[4,128,256]{2,1,0:T(8,128)(2,1)S(1)}, u32[]{:S(2)}, u32[]{:S(2)}) %collective-permute-start.6) | collective-permute-done | bytes 262176 | tf_op jit(solution)/shard_map/ppermute | solution.py:43
  24.5 3.5 %forward_cell.1 = (bf16[4,128,256]{2,1,0:T(8,128)(2,1)S(1)}, bf16[4,128,256]{2,1,0:T(8,128)(2,1)S(1)}, bf16[4,128,256]{2,1,0:T(8,128)(2,1)S(1)}, bf16[4,128,256]...) custom-call(s32[128]{0:T(128)S(1)} %get-tuple-element.81.out_ref, ...), custom_call_target="tpu_custom_call" | custom-call | flops 1073741824 | bytes 10485760 | tf_op jit(solution)/shard_map/forward_cell/pallas_call | solution.py:135
  30.5 3.0 %collective-permute-start.14 = (bf16[4,128,256]{2,1,0:T(8,128)(2,1)S(1)}, bf16[4,128,256]{2,1,0:T(8,128)(2,1)S(1)}, u32[]{:S(2)}, u32[]{:S(2)}) collective-permute-start(bf16[4,128,256]{2,1,0:T(8,128)(2,1)S(1)} %add_convert_fusion.7), channel_id=1, source_target_pairs={{0,2},{1,3},{2,0},{3,1},{4,6},{5,7},{6,4},{7,5},{8,10},{9,11},{10,... | collective-permute-start | bytes 786440 | tf_op jit(solution)/shard_map/ppermute | solution.py:59
  34.1 3.5 %collective-permute-start.17 = (bf16[4,128,256]{2,1,0:T(8,128)(2,1)S(1)}, bf16[4,128,256]{2,1,0:T(8,128)(2,1)S(1)}, u32[]{:S(2)}, u32[]{:S(2)}) collective-permute-start(bf16[4,128,256]{2,1,0:T(8,128)(2,1)S(1)} %get-tuple-element.77), channel_id=1, source_target_pairs={{0,4},{1,5},{2,6},{3,7},{4,8},{5,9},{6,10},{7,11},{8,12},{9,13},{1... | collective-permute-start | bytes 786440 | tf_op jit(solution)/shard_map/ppermute | solution.py:55
  37.6 2.8 %collective-permute-done.14 = bf16[4,128,256]{2,1,0:T(8,128)(2,1)S(1)} collective-permute-done((bf16[4,128,256]{2,1,0:T(8,128)(2,1)S(1)}, bf16[4,128,256]{2,1,0:T(8,128)(2,1)S(1)}, u32[]{:S(2)}, u32[]{:S(2)}) %collective-permute-start.14) | collective-permute-done | bytes 262176 | tf_op jit(solution)/shard_map/ppermute | solution.py:59
  40.4 4.3 %collective-permute-start.18 = (bf16[4,128,256]{2,1,0:T(8,128)(2,1)S(1)}, bf16[4,128,256]{2,1,0:T(8,128)(2,1)S(1)}, u32[]{:S(2)}, u32[]{:S(2)}) collective-permute-start(bf16[4,128,256]{2,1,0:T(8,128)(2,1)S(1)} %get-tuple-element.78), channel_id=1, source_target_pairs={{0,12},{1,13},{2,14},{3,15},{4,0},{5,1},{6,2},{7,3},{8,4},{9,5},{1... | collective-permute-start | bytes 786440 | tf_op jit(solution)/shard_map/ppermute | solution.py:55
  45.8 9.9 %collective-permute-done.18 = bf16[4,128,256]{2,1,0:T(8,128)(2,1)S(1)} collective-permute-done((bf16[4,128,256]{2,1,0:T(8,128)(2,1)S(1)}, bf16[4,128,256]{2,1,0:T(8,128)(2,1)S(1)}, u32[]{:S(2)}, u32[]{:S(2)}) %collective-permute-start.18) | collective-permute-done | bytes 262176 | tf_op jit(solution)/shard_map/ppermute | solution.py:55
  55.9 2.9 %collective-permute-start.19 = (bf16[4,128,256]{2,1,0:T(8,128)(2,1)S(1)}, bf16[4,128,256]{2,1,0:T(8,128)(2,1)S(1)}, u32[]{:S(2)}, u32[]{:S(2)}) collective-permute-start(bf16[4,128,256]{2,1,0:T(8,128)(2,1)S(1)} %add_convert_fusion.3), channel_id=1, source_target_pairs={{0,2},{1,3},{2,0},{3,1},{4,6},{5,7},{6,4},{7,5},{8,10},{9,11},{10,... | collective-permute-start | bytes 786440 | tf_op jit(solution)/shard_map/ppermute | solution.py:59
  58.9 3.8 %collective-permute-start.11 = (bf16[4,128,256]{2,1,0:T(8,128)(2,1)S(1)}, bf16[4,128,256]{2,1,0:T(8,128)(2,1)S(1)}, u32[]{:S(2)}, u32[]{:S(2)}) collective-permute-start(bf16[4,128,256]{2,1,0:T(8,128)(2,1)S(1)} %get-tuple-element.79), channel_id=1, source_target_pairs={{0,12},{1,13},{2,14},{3,15},{4,0},{5,1},{6,2},{7,3},{8,4},{9,5},{1... | collective-permute-start | bytes 786440 | tf_op jit(solution)/shard_map/ppermute | solution.py:55
  63.8 2.9 %collective-permute-done.11.refs_3_ = bf16[4,128,256]{2,1,0:T(8,128)(2,1)S(1)} collective-permute-done((bf16[4,128,256]{2,1,0:T(8,128)(2,1)S(1)}, bf16[4,128,256]{2,1,0:T(8,128)(2,1)S(1)}, u32[]{:S(2)}, u32[]{:S(2)}) %collective-permute-start.11) | collective-permute-done | bytes 262176 | tf_op jit(solution)/shard_map/ppermute | solution.py:55
  66.7 3.7 %collective-permute-done.10.refs_2_ = bf16[4,128,256]{2,1,0:T(8,128)(2,1)S(1)} collective-permute-done((bf16[4,128,256]{2,1,0:T(8,128)(2,1)S(1)}, bf16[4,128,256]{2,1,0:T(8,128)(2,1)S(1)}, u32[]{:S(2)}, u32[]{:S(2)}) %collective-permute-start.10) | collective-permute-done | bytes 262176 | tf_op jit(solution)/shard_map/ppermute | solution.py:55
  73.1 2.2 %collective-permute-start.21 = (bf16[4,128,256]{2,1,0:T(8,128)(2,1)S(1)}, bf16[4,128,256]{2,1,0:T(8,128)(2,1)S(1)}, u32[]{:S(2)}, u32[]{:S(2)}) collective-permute-start(bf16[4,128,256]{2,1,0:T(8,128)(2,1)S(1)} %get-tuple-element.56.rest_0_), channel_id=1, source_target_pairs={{0,12},{1,13},{2,14},{3,15},{4,0},{5,1},{6,2},{7,3},{8,4},{9,5},{1... | collective-permute-start | bytes 786440 | tf_op jit(solution)/shard_map/ppermute | solution.py:55
  75.3 7.5 %collective-permute-done.23.rest_4_ = bf16[4,128,256]{2,1,0:T(8,128)(2,1)S(1)} collective-permute-done((bf16[4,128,256]{2,1,0:T(8,128)(2,1)S(1)}, bf16[4,128,256]{2,1,0:T(8,128)(2,1)S(1)}, u32[]{:S(2)}, u32[]{:S(2)}) %collective-permute-start.23) | collective-permute-done | bytes 262176 | tf_op jit(solution)/shard_map/ppermute | solution.py:55
  84.4 3.2 %collective-permute-start.22 = (bf16[4,128,256]{2,1,0:T(8,128)(2,1)S(1)}, bf16[4,128,256]{2,1,0:T(8,128)(2,1)S(1)}, u32[]{:S(2)}, u32[]{:S(2)}) collective-permute-start(bf16[4,128,256]{2,1,0:T(8,128)(2,1)S(1)} %slice.32.rest_1_), channel_id=1, source_target_pairs={{0,12},{1,13},{2,14},{3,15},{4,0},{5,1},{6,2},{7,3},{8,4},{9,5},{1... | collective-permute-start | bytes 786440 | tf_op jit(solution)/shard_map/ppermute | solution.py:55
  87.8 2.8 %collective-permute-done.24.rest_5_ = bf16[4,128,256]{2,1,0:T(8,128)(2,1)S(1)} collective-permute-done((bf16[4,128,256]{2,1,0:T(8,128)(2,1)S(1)}, bf16[4,128,256]{2,1,0:T(8,128)(2,1)S(1)}, u32[]{:S(2)}, u32[]{:S(2)}) %collective-permute-start.24) | collective-permute-done | bytes 262176 | tf_op jit(solution)/shard_map/ppermute | solution.py:59
  94.9 3.7 %collective-permute-start.44 = (bf16[2,128,256]{2,1,0:T(8,128)(2,1)S(1)}, bf16[2,128,256]{2,1,0:T(8,128)(2,1)S(1)}, u32[]{:S(2)}, u32[]{:S(2)}) collective-permute-start(bf16[2,128,256]{2,1,0:T(8,128)(2,1)S(1)} %add_convert_fusion.12), channel_id=1, source_target_pairs={{0,64},{16,80},{32,96},{48,112},{64,0},{80,16},{96,32},{112,48},{1... | collective-permute-start | bytes 393224 | tf_op jit(solution)/shard_map/ppermute | solution.py:47
  98.6 3.3 %backward_cell.1 = (bf16[4,128,256]{2,1,0:T(8,128)(2,1)S(1)}, bf16[4,128,256]{2,1,0:T(8,128)(2,1)S(1)}, bf16[4,128,256]{2,1,0:T(8,128)(2,1)S(1)}, bf16[4,128,256...) custom-call(s32[128]{0:T(128)S(1)} %get-tuple-element.75.out_ref, ...), custom_call_target="tpu_custom_call" | custom-call | flops 1073741824 | bytes 10485760 | tf_op jit(solution)/shard_map/backward_cell/pallas_call | solution.py:135
  106.0 2.4 %collective-permute-start.36 = (bf16[4,128,256]{2,1,0:T(8,128)(2,1)S(1)}, bf16[4,128,256]{2,1,0:T(8,128)(2,1)S(1)}, u32[]{:S(2)}, u32[]{:S(2)}) collective-permute-start(bf16[4,128,256]{2,1,0:T(8,128)(2,1)S(1)} %get-tuple-element.60), channel_id=1, source_target_pairs={{0,96},{16,112},{32,0},{48,16},{64,32},{80,48},{96,64},{112,80},{1... | collective-permute-start | bytes 786440 | tf_op jit(solution)/shard_map/ppermute | solution.py:43
  108.9 3.8 %collective-permute-start.40 = (bf16[4,128,256]{2,1,0:T(8,128)(2,1)S(1)}, bf16[4,128,256]{2,1,0:T(8,128)(2,1)S(1)}, u32[]{:S(2)}, u32[]{:S(2)}) collective-permute-start(bf16[4,128,256]{2,1,0:T(8,128)(2,1)S(1)} %get-tuple-element.66), channel_id=1, source_target_pairs={{0,96},{16,112},{32,0},{48,16},{64,32},{80,48},{96,64},{112,80},{1... | collective-permute-start | bytes 786440 | tf_op jit(solution)/shard_map/ppermute | solution.py:43
  115.6 3.7 %collective-permute-start.46 = (bf16[2,128,256]{2,1,0:T(8,128)(2,1)S(1)}, bf16[2,128,256]{2,1,0:T(8,128)(2,1)S(1)}, u32[]{:S(2)}, u32[]{:S(2)}) collective-permute-start(bf16[2,128,256]{2,1,0:T(8,128)(2,1)S(1)} %add_convert_fusion.10), channel_id=1, source_target_pairs={{0,8},{1,9},{2,10},{3,11},{4,12},{5,13},{6,14},{7,15},{8,0},{9,1},... | collective-permute-start | bytes 393224 | tf_op jit(solution)/shard_map/ppermute | solution.py:55
  124.4 3.8 %collective-permute-done.38 = bf16[4,128,256]{2,1,0:T(8,128)(2,1)S(1)} collective-permute-done((bf16[4,128,256]{2,1,0:T(8,128)(2,1)S(1)}, bf16[4,128,256]{2,1,0:T(8,128)(2,1)S(1)}, u32[]{:S(2)}, u32[]{:S(2)}) %collective-permute-start.38) | collective-permute-done | bytes 262176 | tf_op jit(solution)/shard_map/ppermute | solution.py:43
  (100 shorter events, 37.6 us)
Async XLA Ops:
  0.6 10.2 %collective-permute-start = (bf16[4,128,256]{2,1,0:T(8,128)(2,1)}, bf16[4,128,256]{2,1,0:T(8,128)(2,1)S(1)}, u32[]{:S(2)}, u32[]{:S(2)}) collective-permute-start(bf16[4,128,256]{2,1,0:T(8,128)(2,1)} %bitcast.44), channel_id=1, source_target_pairs={{0,16},{16,0},{32,48},{48,32},{64,80},{80,64},{96,112},{112,96},{1... | collective-permute-start | bytes 786440 | tf_op jit(solution)/shard_map/ppermute | solution.py:51
  2.4 11.8 %collective-permute-start.3 = (bf16[4,128,256]{2,1,0:T(8,128)(2,1)}, bf16[4,128,256]{2,1,0:T(8,128)(2,1)S(1)}, u32[]{:S(2)}, u32[]{:S(2)}) collective-permute-start(bf16[4,128,256]{2,1,0:T(8,128)(2,1)} %bitcast.45), channel_id=1, source_target_pairs={{0,64},{16,80},{32,96},{48,112},{64,0},{80,16},{96,32},{112,48},{1... | collective-permute-start | bytes 786440 | tf_op jit(solution)/shard_map/ppermute | solution.py:43
  6.2 12.7 %collective-permute-start.5 = (bf16[4,128,256]{2,1,0:T(8,128)(2,1)}, bf16[4,128,256]{2,1,0:T(8,128)(2,1)S(1)}, u32[]{:S(2)}, u32[]{:S(2)}) collective-permute-start(bf16[4,128,256]{2,1,0:T(8,128)(2,1)} %bitcast.46), channel_id=1, source_target_pairs={{0,32},{16,48},{32,64},{48,80},{64,96},{80,112},{96,0},{112,16},{1... | collective-permute-start | bytes 786440 | tf_op jit(solution)/shard_map/ppermute | solution.py:43
  7.3 13.1 %collective-permute-start.1 = (bf16[4,128,256]{2,1,0:T(8,128)(2,1)}, bf16[4,128,256]{2,1,0:T(8,128)(2,1)S(1)}, u32[]{:S(2)}, u32[]{:S(2)}) collective-permute-start(bf16[4,128,256]{2,1,0:T(8,128)(2,1)} %bitcast.47), channel_id=1, source_target_pairs={{0,96},{16,112},{32,0},{48,16},{64,32},{80,48},{96,64},{112,80},{1... | collective-permute-start | bytes 786440 | tf_op jit(solution)/shard_map/ppermute | solution.py:43
  10.8 12.9 %collective-permute-start.6 = (bf16[4,128,256]{2,1,0:T(8,128)(2,1)S(1)}, bf16[4,128,256]{2,1,0:T(8,128)(2,1)S(1)}, u32[]{:S(2)}, u32[]{:S(2)}) collective-permute-start(bf16[4,128,256]{2,1,0:T(8,128)(2,1)S(1)} %collective-permute-done.rest_1_), channel_id=1, source_target_pairs={{0,32},{16,48},{32,64},{48,80},{64,96},{80,112},{96,0},{112,16},{1... | collective-permute-start | bytes 786440 | tf_op jit(solution)/shard_map/ppermute | solution.py:43
  11.0 13.5 %collective-permute-start.2 = (bf16[4,128,256]{2,1,0:T(8,128)(2,1)S(1)}, bf16[4,128,256]{2,1,0:T(8,128)(2,1)S(1)}, u32[]{:S(2)}, u32[]{:S(2)}) collective-permute-start(bf16[4,128,256]{2,1,0:T(8,128)(2,1)S(1)} %collective-permute-done.rest_1_), channel_id=1, source_target_pairs={{0,96},{16,112},{32,0},{48,16},{64,32},{80,48},{96,64},{112,80},{1... | collective-permute-start | bytes 786440 | tf_op jit(solution)/shard_map/ppermute | solution.py:43
  30.5 9.9 %collective-permute-start.14 = (bf16[4,128,256]{2,1,0:T(8,128)(2,1)S(1)}, bf16[4,128,256]{2,1,0:T(8,128)(2,1)S(1)}, u32[]{:S(2)}, u32[]{:S(2)}) collective-permute-start(bf16[4,128,256]{2,1,0:T(8,128)(2,1)S(1)} %add_convert_fusion.7), channel_id=1, source_target_pairs={{0,2},{1,3},{2,0},{3,1},{4,6},{5,7},{6,4},{7,5},{8,10},{9,11},{10,... | collective-permute-start | bytes 786440 | tf_op jit(solution)/shard_map/ppermute | solution.py:59
  33.5 11.3 %collective-permute-start.12 = (bf16[4,128,256]{2,1,0:T(8,128)(2,1)S(1)}, bf16[4,128,256]{2,1,0:T(8,128)(2,1)S(1)}, u32[]{:S(2)}, u32[]{:S(2)}) collective-permute-start(bf16[4,128,256]{2,1,0:T(8,128)(2,1)S(1)} %get-tuple-element.47), channel_id=1, source_target_pairs={{0,1},{1,0},{2,3},{3,2},{4,5},{5,4},{6,7},{7,6},{8,9},{9,8},{10,11... | collective-permute-start | bytes 786440 | tf_op jit(solution)/shard_map/ppermute | solution.py:63
  33.5 11.4 %collective-permute-start.16 = (bf16[4,128,256]{2,1,0:T(8,128)(2,1)S(1)}, bf16[4,128,256]{2,1,0:T(8,128)(2,1)S(1)}, u32[]{:S(2)}, u32[]{:S(2)}) collective-permute-start(bf16[4,128,256]{2,1,0:T(8,128)(2,1)S(1)} %get-tuple-element.52), channel_id=1, source_target_pairs={{0,1},{1,0},{2,3},{3,2},{4,5},{5,4},{6,7},{7,6},{8,9},{9,8},{10,11... | collective-permute-start | bytes 786440 | tf_op jit(solution)/shard_map/ppermute | solution.py:63
  34.0 24.8 %collective-permute-start.9 = (bf16[8,128,256]{2,1,0:T(8,128)(2,1)S(1)}, bf16[8,128,256]{2,1,0:T(8,128)(2,1)S(1)}, u32[]{:S(2)}, u32[]{:S(2)}) collective-permute-start(bf16[8,128,256]{2,1,0:T(8,128)(2,1)S(1)} %get-tuple-element.43), channel_id=1, source_target_pairs={{0,1},{1,0},{2,3},{3,2},{4,5},{5,4},{6,7},{7,6},{8,9},{9,8},{10,11... | collective-permute-start | bytes 1572872 | tf_op jit(solution)/shard_map/ppermute | solution.py:63
  34.1 11.7 %collective-permute-start.17 = (bf16[4,128,256]{2,1,0:T(8,128)(2,1)S(1)}, bf16[4,128,256]{2,1,0:T(8,128)(2,1)S(1)}, u32[]{:S(2)}, u32[]{:S(2)}) collective-permute-start(bf16[4,128,256]{2,1,0:T(8,128)(2,1)S(1)} %get-tuple-element.77), channel_id=1, source_target_pairs={{0,4},{1,5},{2,6},{3,7},{4,8},{5,9},{6,10},{7,11},{8,12},{9,13},{1... | collective-permute-start | bytes 786440 | tf_op jit(solution)/shard_map/ppermute | solution.py:55
  40.4 15.3 %collective-permute-start.18 = (bf16[4,128,256]{2,1,0:T(8,128)(2,1)S(1)}, bf16[4,128,256]{2,1,0:T(8,128)(2,1)S(1)}, u32[]{:S(2)}, u32[]{:S(2)}) collective-permute-start(bf16[4,128,256]{2,1,0:T(8,128)(2,1)S(1)} %get-tuple-element.78), channel_id=1, source_target_pairs={{0,12},{1,13},{2,14},{3,15},{4,0},{5,1},{6,2},{7,3},{8,4},{9,5},{1... | collective-permute-start | bytes 786440 | tf_op jit(solution)/shard_map/ppermute | solution.py:55
  44.7 18.0 %collective-permute-start.8 = (bf16[4,128,256]{2,1,0:T(8,128)(2,1)S(1)}, bf16[4,128,256]{2,1,0:T(8,128)(2,1)S(1)}, u32[]{:S(2)}, u32[]{:S(2)}) collective-permute-start(bf16[4,128,256]{2,1,0:T(8,128)(2,1)S(1)} %get-tuple-element.40), channel_id=1, source_target_pairs={{0,1},{1,0},{2,3},{3,2},{4,5},{5,4},{6,7},{7,6},{8,9},{9,8},{10,11... | collective-permute-start | bytes 786440 | tf_op jit(solution)/shard_map/ppermute | solution.py:63
  44.9 17.9 %collective-permute-start.15 = (bf16[4,128,256]{2,1,0:T(8,128)(2,1)S(1)}, bf16[4,128,256]{2,1,0:T(8,128)(2,1)S(1)}, u32[]{:S(2)}, u32[]{:S(2)}) collective-permute-start(bf16[4,128,256]{2,1,0:T(8,128)(2,1)S(1)} %add_convert_fusion.6), channel_id=1, source_target_pairs={{0,8},{1,9},{2,10},{3,11},{4,12},{5,13},{6,14},{7,15},{8,0},{9,1},... | collective-permute-start | bytes 786440 | tf_op jit(solution)/shard_map/ppermute | solution.py:55
  71.5 12.8 %collective-permute-start.20 = (bf16[6,128,256]{2,1,0:T(8,128)(2,1)S(1)}, bf16[6,128,256]{2,1,0:T(8,128)(2,1)S(1)}, u32[]{:S(2)}, u32[]{:S(2)}) collective-permute-start(bf16[6,128,256]{2,1,0:T(8,128)(2,1)S(1)} %get-tuple-element.57), channel_id=1, source_target_pairs={{0,2},{1,3},{2,0},{3,1},{4,6},{5,7},{6,4},{7,5},{8,10},{9,11},{10,... | collective-permute-start | bytes 1179656 | tf_op jit(solution)/shard_map/ppermute | solution.py:59
  72.1 10.7 %collective-permute-start.23 = (bf16[4,128,256]{2,1,0:T(8,128)(2,1)S(1)}, bf16[4,128,256]{2,1,0:T(8,128)(2,1)S(1)}, u32[]{:S(2)}, u32[]{:S(2)}) collective-permute-start(bf16[4,128,256]{2,1,0:T(8,128)(2,1)S(1)} %get-tuple-element.56.rest_0_), channel_id=1, source_target_pairs={{0,8},{1,9},{2,10},{3,11},{4,12},{5,13},{6,14},{7,15},{8,0},{9,1},... | collective-permute-start | bytes 786440 | tf_op jit(solution)/shard_map/ppermute | solution.py:55
  72.1 15.5 %collective-permute-start.25 = (bf16[4,128,256]{2,1,0:T(8,128)(2,1)S(1)}, bf16[4,128,256]{2,1,0:T(8,128)(2,1)S(1)}, u32[]{:S(2)}, u32[]{:S(2)}) collective-permute-start(bf16[4,128,256]{2,1,0:T(8,128)(2,1)S(1)} %get-tuple-element.56.rest_0_), channel_id=1, source_target_pairs={{0,4},{1,5},{2,6},{3,7},{4,8},{5,9},{6,10},{7,11},{8,12},{9,13},{1... | collective-permute-start | bytes 786440 | tf_op jit(solution)/shard_map/ppermute | solution.py:55
  73.1 14.5 %collective-permute-start.21 = (bf16[4,128,256]{2,1,0:T(8,128)(2,1)S(1)}, bf16[4,128,256]{2,1,0:T(8,128)(2,1)S(1)}, u32[]{:S(2)}, u32[]{:S(2)}) collective-permute-start(bf16[4,128,256]{2,1,0:T(8,128)(2,1)S(1)} %get-tuple-element.56.rest_0_), channel_id=1, source_target_pairs={{0,12},{1,13},{2,14},{3,15},{4,0},{5,1},{6,2},{7,3},{8,4},{9,5},{1... | collective-permute-start | bytes 786440 | tf_op jit(solution)/shard_map/ppermute | solution.py:55
  103.9 9.4 %collective-permute-start.37 = (bf16[4,128,256]{2,1,0:T(8,128)(2,1)S(1)}, bf16[4,128,256]{2,1,0:T(8,128)(2,1)S(1)}, u32[]{:S(2)}, u32[]{:S(2)}) collective-permute-start(bf16[4,128,256]{2,1,0:T(8,128)(2,1)S(1)} %get-tuple-element.62), channel_id=1, source_target_pairs={{0,16},{16,0},{32,48},{48,32},{64,80},{80,64},{96,112},{112,96},{1... | collective-permute-start | bytes 786440 | tf_op jit(solution)/shard_map/ppermute | solution.py:51
  104.6 11.0 %collective-permute-start.35 = (bf16[4,128,256]{2,1,0:T(8,128)(2,1)S(1)}, bf16[4,128,256]{2,1,0:T(8,128)(2,1)S(1)}, u32[]{:S(2)}, u32[]{:S(2)}) collective-permute-start(bf16[4,128,256]{2,1,0:T(8,128)(2,1)S(1)} %get-tuple-element.59), channel_id=1, source_target_pairs={{0,32},{16,48},{32,64},{48,80},{64,96},{80,112},{96,0},{112,16},{1... | collective-permute-start | bytes 786440 | tf_op jit(solution)/shard_map/ppermute | solution.py:43
  106.0 9.6 %collective-permute-start.36 = (bf16[4,128,256]{2,1,0:T(8,128)(2,1)S(1)}, bf16[4,128,256]{2,1,0:T(8,128)(2,1)S(1)}, u32[]{:S(2)}, u32[]{:S(2)}) collective-permute-start(bf16[4,128,256]{2,1,0:T(8,128)(2,1)S(1)} %get-tuple-element.60), channel_id=1, source_target_pairs={{0,96},{16,112},{32,0},{48,16},{64,32},{80,48},{96,64},{112,80},{1... | collective-permute-start | bytes 786440 | tf_op jit(solution)/shard_map/ppermute | solution.py:43
  108.4 11.4 %collective-permute-start.39 = (bf16[4,128,256]{2,1,0:T(8,128)(2,1)S(1)}, bf16[4,128,256]{2,1,0:T(8,128)(2,1)S(1)}, u32[]{:S(2)}, u32[]{:S(2)}) collective-permute-start(bf16[4,128,256]{2,1,0:T(8,128)(2,1)S(1)} %get-tuple-element.65), channel_id=1, source_target_pairs={{0,32},{16,48},{32,64},{48,80},{64,96},{80,112},{96,0},{112,16},{1... | collective-permute-start | bytes 786440 | tf_op jit(solution)/shard_map/ppermute | solution.py:43
  108.9 12.0 %collective-permute-start.40 = (bf16[4,128,256]{2,1,0:T(8,128)(2,1)S(1)}, bf16[4,128,256]{2,1,0:T(8,128)(2,1)S(1)}, u32[]{:S(2)}, u32[]{:S(2)}) collective-permute-start(bf16[4,128,256]{2,1,0:T(8,128)(2,1)S(1)} %get-tuple-element.66), channel_id=1, source_target_pairs={{0,96},{16,112},{32,0},{48,16},{64,32},{80,48},{96,64},{112,80},{1... | collective-permute-start | bytes 786440 | tf_op jit(solution)/shard_map/ppermute | solution.py:43
  113.2 9.1 %collective-permute-start.48 = (bf16[2,128,256]{2,1,0:T(8,128)(2,1)S(1)}, bf16[2,128,256]{2,1,0:T(8,128)(2,1)S(1)}, u32[]{:S(2)}, u32[]{:S(2)}) collective-permute-start(bf16[2,128,256]{2,1,0:T(8,128)(2,1)S(1)} %add_convert_fusion.10), channel_id=1, source_target_pairs={{0,12},{1,13},{2,14},{3,15},{4,0},{5,1},{6,2},{7,3},{8,4},{9,5},{1... | collective-permute-start | bytes 393224 | tf_op jit(solution)/shard_map/ppermute | solution.py:55
  (27 other events, 228.0 us)
